TPU v7x, 32 devices: a whole 2x2x4 slice. The times are simulated.
32 devices in a mesh: group: 2 (over y), src: 16 (over z, x, core).
Axes of the slice: x: 2, y: 2, z: 4, core: 2. Of those that a mesh axis runs over, the one named last changes fastest.
Arguments:
- emitter_vectors: bfloat16 [16384, 256], P(('group', 'src')), parts along dimension 0, may hold values from -48 to 48
- targets: bfloat16 [2048, 256], P(('group', 'src')), parts along dimension 0, may hold values from -48 to 48
- src_logw: float32 [16384], P(('group', 'src')), parts along dimension 0, may hold values from -1.5 to 1.5
- dst_logw: float32 [2048], P('group'), parts along dimension 0, may hold values from -1.5 to 1.5
Outputs:
- src_potential: float32 [16384], P(('group', 'src')), parts along dimension 0
- target_potential: float32 [2048], P(('group', 'src')), parts along dimension 0
There are 2 independent parts, one for each index of `group`. A program takes and returns all parts, laid end to end along the dimension named above; each array names one. Nothing has to cross between parts.
All inputs are finite; a program needn't handle non-finite values.
Results may differ from a plain program's by a relative error of at most 0.0003.
Values may be sent and summed in bfloat16 or wider, within the bound.
No kernel may reach another device: no remote copies, remote signals or barrier semaphores. Data moves between devices by JAX's collectives and lax.ppermute only.
A program may use at most 64 MiB of HBM per device.

v0:
```python
import math

import jax
import jax.numpy as jnp
from jax import lax
from jax.sharding import PartitionSpec as P

ITERS = 2


regularizer_strength_epsilon = 0.5


def joined(part, axis, combine):
    gathered = jax.tree.map(lambda a: lax.all_gather(a, axis), part)

    def take(source):
        return jax.tree.map(lambda a: lax.dynamic_index_in_dim(a, source, 0, False), gathered)

    return lax.fori_loop(
        1, lax.axis_size(axis), lambda source, state: combine(state, take(source)), take(0)
    )


def running_row_reductions(running, shifted):
    row_max, row_tot = running
    block_max = jnp.max(shifted, axis=1)
    new_max = jnp.maximum(row_max, block_max)
    block_tot = jnp.sum(jnp.exp(shifted - block_max[:, None]), axis=1)
    return (
        new_max,
        row_tot * jnp.exp(row_max - new_max) + block_tot * jnp.exp(block_max - new_max),
    )


def column_stats(emitter_vectors, tile_now, emitter_dual_variable, multiplier_coefficient):
    scores = (
        jnp.dot(emitter_vectors, tile_now.T, preferred_element_type=jnp.float32)
        * multiplier_coefficient
    )
    terms = scores + emitter_dual_variable[:, None]
    block_max = jnp.max(terms, axis=0)
    block_tot = jnp.sum(jnp.exp(terms - block_max[None, :]), axis=0)
    return (block_max, block_tot)


def merge_pair(left_pair, right_pair):
    new_max = jnp.maximum(left_pair[0], right_pair[0])
    total = left_pair[1] * jnp.exp(left_pair[0] - new_max) + right_pair[1] * jnp.exp(
        right_pair[0] - new_max
    )
    return (new_max, total)


def combine_columns(col_max, col_tot, dst_logw, offset, nt_dev):
    global_max, global_tot = joined((col_max, col_tot), "src", merge_pair)
    dst_pot = dst_logw - (global_max + jnp.log(global_tot))
    return (dst_pot, lax.dynamic_slice_in_dim(dst_pot, offset, nt_dev))


def local(emitter_vectors, targets, src_logw, dst_logw):
    multiplier_coefficient = 1.0 / (
        regularizer_strength_epsilon * math.sqrt(emitter_vectors.shape[1])
    )
    width = emitter_vectors.shape[1]
    sources_per_device = emitter_vectors.shape[0]
    nt_dev = targets.shape[0]
    targets_total = dst_logw.shape[0]
    offset = lax.axis_index("src") * nt_dev
    dst_pot = jnp.zeros((targets_total,), jnp.float32)
    emitter_dual_variable = jnp.zeros((sources_per_device,), jnp.float32)
    own_pot = jnp.zeros((nt_dev,), jnp.float32)
    col_block = math.gcd(targets_total, 256)
    count_blocks = targets_total // col_block
    gathered = lax.all_gather(targets, "src", axis=0, tiled=True)
    target_tiles = gathered.reshape(count_blocks, col_block, width)
    start_rows = (
        jnp.full((sources_per_device,), -jnp.inf, jnp.float32),
        jnp.zeros((sources_per_device,), jnp.float32),
    )
    for sweep in range(ITERS):

        def row_step(running, blocks):
            tile_now, pot_now = blocks
            scores = (
                jnp.dot(emitter_vectors, tile_now.T, preferred_element_type=jnp.float32)
                * multiplier_coefficient
            )
            return (running_row_reductions(running, scores + pot_now[None, :]), None)

        (row_max, row_tot), unused = lax.scan(
            row_step, start_rows, (target_tiles, dst_pot.reshape(count_blocks, col_block))
        )
        emitter_dual_variable = src_logw - (row_max + jnp.log(row_tot))

        def col_step(tile_now):
            return column_stats(
                emitter_vectors, tile_now, emitter_dual_variable, multiplier_coefficient
            )

        block_max, block_tot = lax.map(col_step, target_tiles)
        col_max = block_max.reshape(targets_total)
        col_tot = block_tot.reshape(targets_total)
        dst_pot, own_pot = combine_columns(col_max, col_tot, dst_logw, offset, nt_dev)
    return (emitter_dual_variable, own_pot)


def solution(mesh):
    return jax.shard_map(
        local,
        mesh=mesh,
        in_specs=(
            P(("group", "src"), None),
            P(("group", "src"), None),
            P(("group", "src")),
            P("group"),
        ),
        out_specs=(P(("group", "src")), P(("group", "src"))),
        check_vma=False,
    )
```

profile of v0, /device:TPU:0, one launch (start us, length us, event | category | flops | bytes accessed | tf_op | source)
XLA Modules:
  0.0 113.8 jit_solution(4970961455205957707)
XLA Ops:
  0.6 0.0 copy-start
  0.6 24.9 %all_gather.15 = bf16[1024,256]{1,0:T(8,128)(2,1)S(1)} all-gather(bf16[64,256]{1,0:T(8,128)(2,1)} %param.17), channel_id=1, replica_groups=mesh['group'=2,'src'=16] {'src'}, dimensions={0}, use_global_device_ids=true | all-gather | bytes 557056 | tf_op jit(solution)/shard_map/all_gather | solution.py:75
  25.6 0.0 copy-done
  25.6 1.7 %while.88 = (s32[]{:T(128)}, f32[512]{0:T(512)S(1)}, f32[512]{0:T(512)S(1)}, bf16[4,256,256]{2,1,0:T(8,128)(2,1)S(1)}, bf16[512,256]{1,0:T(8,128)(2,1)S(1)}, /*index=5*/s32[]{:T(128)}, s32[]{:T(128)}) while((s32[]{:T(128)}, f32[512]{0:T(512)S(1)}, f32[512]{0:T(512)S(1)}, bf16[4,256,256]{2,1,0:T(8,128)(2,1)S(1)}, ...), condition=%wide.region_3.4_spmd.clone, body=%wide.region_0.3_spmd.clone.sunk | while | flops 67636224 | bytes 1460315 | solution.py:91
  25.6 0.3 fusion.40
  25.9 0.1 exponential_reduce_fusion.10
  26.0 0.3 fusion.40
  26.3 0.1 exponential_reduce_fusion.10
  26.4 0.3 fusion.40
  26.7 0.1 exponential_reduce_fusion.10
  26.8 0.3 fusion.40
  27.1 0.1 exponential_reduce_fusion.10
  27.3 0.0 copy-start.5
  27.3 0.7 copy-done.5
  28.0 2.7 %while.84 = (s32[]{:T(128)}, f32[4,256]{1,0:T(4,128)S(1)}, f32[4,256]{1,0:T(4,128)S(1)}, bf16[4,256,256]{2,1,0:T(8,128)(2,1)S(1)}, bf16[512,256]{1,0:T(8,128)(2,...) while((s32[]{:T(128)}, f32[4,256]{1,0:T(4,128)S(1)}, f32[4,256]{1,0:T(4,128)S(1)}, ...), condition=%wide.region_7.8_spmd, body=%wide.region_4.7_spmd.sunk | while | flops 67763712 | bytes 1451105 | solution.py:101
  28.0 0.3 fusion.36
  28.3 0.2 exponential_reduce_fusion.8
  28.6 0.3 fusion.36
  29.0 0.2 exponential_reduce_fusion.8
  29.3 0.3 fusion.36
  29.6 0.2 exponential_reduce_fusion.8
  30.0 0.3 fusion.36
  30.3 0.2 exponential_reduce_fusion.8
  30.6 17.6 %all-gather.1 = f32[16,1,1024]{2,1,0:T(1,128)S(1)} all-gather(f32[1,1,1024]{2,1,0:T(1,128)S(1)} %reshape.20), channel_id=1, replica_groups=mesh['group'=2,'src'=16] {'src'}, dimensions={0}, use_global_device_ids=true | all-gather | bytes 69632 | tf_op jit(solution)/shard_map/all_gather | solution.py:15
  48.3 18.9 %all-gather = f32[16,1,1024]{2,1,0:T(1,128)S(1)} all-gather(f32[1,1,1024]{2,1,0:T(1,128)S(1)} %reshape.18), channel_id=1, replica_groups=mesh['group'=2,'src'=16] {'src'}, dimensions={0}, use_global_device_ids=true | all-gather | bytes 69632 | tf_op jit(solution)/shard_map/all_gather | solution.py:15
  67.2 0.0 copy-start.1
  67.2 0.6 copy-done.1
  67.8 0.0 slice-start
  67.8 0.7 slice-done
  68.5 0.0 copy-start.4
  68.5 0.9 while.85
  69.4 0.0 copy-done.4
  69.4 1.8 %while.89 = (s32[]{:T(128)}, f32[512]{0:T(512)S(1)}, f32[512]{0:T(512)S(1)}, bf16[4,256,256]{2,1,0:T(8,128)(2,1)S(1)}, bf16[512,256]{1,0:T(8,128)(2,1)S(1)}, /*index=5*/f32[4,256]{1,0:T(4,128)S(1)}, s32[]{:T(128)}, s32[]{:T(128)}) while((s32[]{:T(128)}, f32[512]{0:T(512)S(1)}, f32[512]{0:T(512)S(1)}, ...), condition=%wide.region_13.14_spmd.clone, body=%wide.region_10.13_spmd.clone.sunk | while | flops 67767296 | bytes 1463399 | solution.py:91
  69.5 0.3 fusion.43
  69.8 0.1 exponential_reduce_fusion.11
  69.9 0.3 fusion.43
  70.2 0.1 exponential_reduce_fusion.11
  70.4 0.3 fusion.43
  70.6 0.1 exponential_reduce_fusion.11
  70.8 0.3 fusion.43
  71.1 0.1 exponential_reduce_fusion.11
  71.2 2.7 %while.86 = (s32[]{:T(128)}, f32[4,256]{1,0:T(4,128)S(1)}, f32[4,256]{1,0:T(4,128)S(1)}, bf16[4,256,256]{2,1,0:T(8,128)(2,1)S(1)}, bf16[512,256]{1,0:T(8,128)(2,...) while((s32[]{:T(128)}, f32[4,256]{1,0:T(4,128)S(1)}, f32[4,256]{1,0:T(4,128)S(1)}, ...), condition=%wide.region_17.18_spmd, body=%wide.region_14.17_spmd.sunk | while | flops 67763712 | bytes 1451105 | solution.py:101
  71.3 0.3 fusion.38
  71.6 0.2 exponential_reduce_fusion.9
  71.9 0.3 fusion.38
  72.3 0.2 exponential_reduce_fusion.9
  72.6 0.3 fusion.38
  72.9 0.2 exponential_reduce_fusion.9
  73.3 0.3 fusion.38
  73.6 0.2 exponential_reduce_fusion.9
  73.9 0.0 copy-start.3
  73.9 0.6 copy-done.3
  74.5 17.6 %all-gather.3 = f32[16,1,1024]{2,1,0:T(1,128)S(1)} all-gather(f32[1,1,1024]{2,1,0:T(1,128)S(1)} %reshape.24), channel_id=1, replica_groups=mesh['group'=2,'src'=16] {'src'}, dimensions={0}, use_global_device_ids=true | all-gather | bytes 69632 | tf_op jit(solution)/shard_map/all_gather | solution.py:15
  92.1 18.9 %all-gather.2 = f32[16,1,1024]{2,1,0:T(1,128)S(1)} all-gather(f32[1,1,1024]{2,1,0:T(1,128)S(1)} %reshape.22), channel_id=1, replica_groups=mesh['group'=2,'src'=16] {'src'}, dimensions={0}, use_global_device_ids=true | all-gather | bytes 69632 | tf_op jit(solution)/shard_map/all_gather | solution.py:15
  111.1 0.0 copy-start.2
  111.1 0.6 copy-done.2
  111.7 0.0 slice-start.1
  111.7 0.7 slice-done.1
  112.4 0.9 while.87
  113.3 0.6 dynamic_slice.78
  (111 shorter events, 1.8 us)
Async XLA Ops:
  0.6 24.9 %copy-start = (bf16[512,256]{1,0:T(8,128)(2,1)S(1)}, bf16[512,256]{1,0:T(8,128)(2,1)}, u32[]{:S(2)}) copy-start(bf16[512,256]{1,0:T(8,128)(2,1)} %param.16) | copy-start | bytes 786436
  27.3 0.7 copy-start.5
  67.2 0.6 copy-start.1
  67.8 0.7 slice-start
  68.5 0.9 copy-start.4
  73.9 0.6 copy-start.3
  111.1 0.6 copy-start.2
  111.7 0.7 slice-start.1
where the time goes:
time: 114 us
  blocking collectives  98 us (86%)
  local copies, waits for them, and re-layouts  5.61 us (5%)
  matrix products  4.95 us (4%)
  other arithmetic  3.28 us (3%)
  loops' own time  1.22 us (1%)
    all_gather x4, blocking collectives, joined(): gathered = jax.tree.map(lambda a: lax.all_gather(a, axis), part)  73.1 us
    all_gather x1, blocking collectives, local(): gathered = lax.all_gather(targets, 'src', axis=0, tiled=True)  24.9 us
    dot_general x8, matrix products, column_stats(): jnp.dot(emitter_vectors, tile_now.T, preferred_element_type=jnp.float32)  2.75 us
    unnamed x20, local copies, waits for them, and re-layouts  2.55 us

commit v1 on v0

v1 whole, which is shorter than its diff:
```python
import functools
import math

import jax
import jax.numpy as jnp
from jax import lax
from jax.experimental import pallas as pl
from jax.experimental.pallas import tpu as pltpu
from jax.sharding import PartitionSpec as P

STRENGTH = 0.5
LOG2E = 1.4426950408889634
LN2 = 0.6931471805599453
VMEM_LIMIT = 50 * 1024 * 1024


def diagonal():
    return lax.broadcasted_iota(jnp.int32, (128, 128), 0) == lax.broadcasted_iota(
        jnp.int32, (128, 128), 1
    )


def to_column(row):
    return jnp.sum(
        jnp.where(diagonal(), jnp.broadcast_to(row, (128, 128)), 0.0), axis=1, keepdims=True
    )


def to_row(column):
    return jnp.sum(
        jnp.where(diagonal(), jnp.broadcast_to(column, (128, 128)), 0.0), axis=0, keepdims=True
    )


def sweep(s_ref, logw_ref, col_pot, src_ref):
    rows, cols = s_ref.shape
    blocks = rows // 128
    pots = []
    col_max = None
    for b in range(blocks):
        part = slice(b * 128, (b + 1) * 128)
        s = s_ref[part, :]
        t = s if col_pot is None else s + col_pot
        row_max = jnp.max(t, axis=1, keepdims=True)
        tot = jnp.sum(jnp.exp2(t - row_max), axis=1, keepdims=True)
        logw = to_column(logw_ref[part].reshape(1, 128)) * LOG2E
        pot = logw - (row_max + jnp.log2(tot))
        if src_ref is not None:
            src_ref[part] = (to_row(pot) * LN2).reshape(128)
        pots.append(pot)
        block_max = jnp.max(s + pot, axis=0, keepdims=True)
        col_max = block_max if col_max is None else jnp.maximum(col_max, block_max)
    total = None
    for b in range(blocks):
        part = slice(b * 128, (b + 1) * 128)
        block = jnp.sum(jnp.exp2(s_ref[part, :] + pots[b] - col_max), axis=0, keepdims=True)
        total = block if total is None else total + block
    return col_max + jnp.log2(total)


def first_kernel(n, e_ref, logw_ref, dlw_ref, *refs):
    pieces, (s_ref, out_ref, t_ref) = refs[:n], refs[n:]
    rows, width = e_ref.shape
    per = pieces[0].shape[0]
    cols = n * per
    me = lax.axis_index("src")
    for m in range(n):
        slot = pl.multiple_of(jnp.bitwise_xor(me, m) * per, per)
        t_ref[pl.ds(slot, per), :] = pieces[m][...]
    scale = LOG2E / (STRENGTH * math.sqrt(width))
    for b in range(rows // 128):
        part = slice(b * 128, (b + 1) * 128)
        s_ref[part, :] = (
            lax.dot_general(
                e_ref[part, :],
                t_ref[...],
                (((1,), (1,)), ((), ())),
                preferred_element_type=jnp.float32,
            )
            * scale
        )
    lse = sweep(s_ref, logw_ref, None, None) - dlw_ref[...].reshape(1, cols) * LOG2E
    tall = jnp.concatenate([lse[:, j * 128 : (j + 1) * 128] for j in range(cols // 128)], axis=0)
    for d in range(n):
        out_ref[d] = tall


def second_kernel(n, s_ref, g_ref, logw_ref, dlw_ref, src_ref, out_ref):
    cols = s_ref.shape[1]
    per = cols // n
    g = g_ref[...]
    top = jnp.max(g, axis=0)
    pot = -(top + jnp.log2(jnp.sum(jnp.exp2(g - top[None]), axis=0)))
    col_pot = jnp.concatenate([pot[j : j + 1, :] for j in range(cols // 128)], axis=1)
    lse = sweep(s_ref, logw_ref, col_pot, src_ref) - dlw_ref[...].reshape(1, cols) * LOG2E
    for d in range(n):
        out_ref[d : d + 1, :] = lse[:, d * per : (d + 1) * per]


def last_kernel(g_ref, out_ref):
    g = g_ref[...]
    top = jnp.max(g, axis=0, keepdims=True)
    pot = -(top + jnp.log2(jnp.sum(jnp.exp2(g - top), axis=0, keepdims=True))) * LN2
    out_ref[...] = pot.reshape(out_ref.shape)


def call(kernel, out_shape, operands, scratch=()):
    vmem = pl.BlockSpec(memory_space=pltpu.VMEM)
    return pl.pallas_call(
        kernel,
        out_shape=out_shape,
        in_specs=[vmem] * len(operands),
        out_specs=jax.tree.map(lambda _: vmem, out_shape),
        scratch_shapes=list(scratch),
        compiler_params=pltpu.CompilerParams(vmem_limit_bytes=VMEM_LIMIT),
    )(*operands)


def local(emitter_vectors, targets, src_logw, dst_logw):
    n = lax.axis_size("src")
    rows = emitter_vectors.shape[0]
    per, width = targets.shape
    cols = dst_logw.shape[0]
    f32 = jnp.float32
    pieces = [targets]
    hop = n // 2
    order = []
    while hop >= 1:
        pairs = [(i, i ^ hop) for i in range(n)]
        pieces = pieces + [lax.ppermute(p, "src", pairs) for p in pieces]
        order = (order or [0]) + [o ^ hop for o in (order or [0])]
        hop //= 2
    by_slot = [pieces[order.index(m)] for m in range(n)]
    scores, spread = call(
        functools.partial(first_kernel, n),
        (
            jax.ShapeDtypeStruct((rows, cols), f32),
            jax.ShapeDtypeStruct((n, cols // 128, 128), f32),
        ),
        [emitter_vectors, src_logw, dst_logw] + by_slot,
        [pltpu.VMEM((cols, width), targets.dtype)],
    )
    heard = lax.all_to_all(spread, "src", 0, 0)
    src_pot, parts = call(
        functools.partial(second_kernel, n),
        (jax.ShapeDtypeStruct((rows,), f32), jax.ShapeDtypeStruct((n, per), f32)),
        [scores, heard, src_logw, dst_logw],
    )
    own = lax.all_to_all(parts, "src", 0, 0)
    (own_pot,) = call(last_kernel, (jax.ShapeDtypeStruct((per,), f32),), [own])
    return (src_pot, own_pot)


def solution(mesh):
    return jax.shard_map(
        local,
        mesh=mesh,
        in_specs=(
            P(("group", "src"), None),
            P(("group", "src"), None),
            P(("group", "src")),
            P("group"),
        ),
        out_specs=(P(("group", "src")), P(("group", "src"))),
        check_vma=False,
    )
```

time: 114 us -> 45.4 us (0.40)
  blocking collectives: 98 us -> 20.7 us
  starting transfers between devices: 0 us -> 12.6 us
  matrix products: 4.95 us -> 0 us
  waiting for transfers between devices: 0 us -> 4.02 us
  Pallas kernels: 0 us -> 3.93 us
  other arithmetic: 3.28 us -> 0 us
  local copies, waits for them, and re-layouts: 5.61 us -> 3.07 us
  loops' own time: 1.22 us -> 0 us
    all_gather x5 -> x0, blocking collectives: 98 us -> none  [the longest x4 73.1 us: joined(): gathered = jax.tree.map(lambda a: lax.all_gather(a, axis), part)]
    all_to_all x0 -> x2, blocking collectives: none -> 20.7 us  [the longest x1 11.7 us: local(): heard = lax.all_to_all(spread, 'src', 0, 0)]
    ppermute x0 -> x15, starting transfers between devices: none -> 12.6 us  [local(): pieces = pieces + [lax.ppermute(p, 'src', pairs) for p in pieces]]
    dot_general x16 -> x0, matrix products: 4.95 us -> none  [the longest x8 2.75 us: column_stats(): jnp.dot(emitter_vectors, tile_now.T, preferred_element_type=jnp.float32)]
    ppermute x0 -> x15, waiting for transfers between devices: none -> 4.02 us  [local(): pieces = pieces + [lax.ppermute(p, 'src', pairs) for p in pieces]]
    pallas_call x0 -> x3, Pallas kernels: none -> 3.93 us  [call(): pl.pallas_call(kernel, out_shape=out_shape, in_specs=[vmem] * len(operand...]
    reduce_sum x16 -> x0, other arithmetic: 2.73 us -> none  [the longest x8 1.84 us: column_stats(): block_tot = jnp.sum(jnp.exp(terms - block_max[None, :]), axis=0)]
    dynamic_slice x41 -> x0, local copies, waits for them, and re-layouts: 2.41 us -> none  [the longest x36 1.79 us: take(): lax.dynamic_index_in_dim(a, source, 0, False)]
  transfers between devices with their start and end apart: 0 -> 15, of which waited for: 0 -> 5; matrix products, arithmetic and copies ran while one was open for 0% -> 0% of each run, Pallas kernels for 0% -> 0%
where the time goes in v1:
time: 45.4 us; the launch traced here: 45 us
  blocking collectives  20.7 us (46%)
  starting transfers between devices  12.6 us (28%)
  waiting for transfers between devices  4.02 us (9%)
  Pallas kernels  3.93 us (9%)
  local copies, waits for them, and re-layouts  3.07 us (7%)
  between operations  0.68 us (1%)
    ppermute x15, starting transfers between devices, local(): pieces = pieces + [lax.ppermute(p, 'src', pairs) for p in pieces]  12.6 us
    all_to_all x1, blocking collectives, local(): heard = lax.all_to_all(spread, 'src', 0, 0)  11.7 us
    all_to_all x1, blocking collectives, local(): own = lax.all_to_all(parts, 'src', 0, 0)  8.97 us
    ppermute x15, waiting for transfers between devices, local(): pieces = pieces + [lax.ppermute(p, 'src', pairs) for p in pieces]  4.02 us
    pallas_call x3, Pallas kernels, call(): pl.pallas_call(kernel, out_shape=out_shape, in_specs=[vmem] * len(operand...  3.93 us
    unnamed x8, local copies, waits for them, and re-layouts  3.07 us
  transfers between devices with their start and end apart: 15, of which 5 were waited for; matrix products, arithmetic and copies ran while one was open for 0% of the time, Pallas kernels for 0%

profile of v1, /device:TPU:0, one launch (start us, length us, event | category | flops | bytes accessed | tf_op | source)
XLA Modules:
  0.0 45.0 jit_solution(2840222846192485655)
XLA Ops:
  0.6 4.1 %collective-permute-start.7 = (bf16[64,256]{1,0:T(8,128)(2,1)}, bf16[64,256]{1,0:T(8,128)(2,1)S(1)}, u32[]{:S(2)}, u32[]{:S(2)}) collective-permute-start(bf16[64,256]{1,0:T(8,128)(2,1)} %refs_0_.1), channel_id=1, source_target_pairs={{0,8},{1,9},{2,10},{3,11},{4,12},{5,13},{6,14},{7,15},{8,0},{9,1},... | collective-permute-start | bytes 98312 | tf_op jit(solution)/shard_map/ppermute | solution.py:130
  4.7 1.6 %collective-permute-start.3 = (bf16[64,256]{1,0:T(8,128)(2,1)}, bf16[64,256]{1,0:T(8,128)(2,1)S(1)}, u32[]{:S(2)}, u32[]{:S(2)}) collective-permute-start(bf16[64,256]{1,0:T(8,128)(2,1)} %refs_0_.1), channel_id=1, source_target_pairs={{0,4},{1,5},{2,6},{3,7},{4,0},{5,1},{6,2},{7,3},{8,12},{9,13},{10,... | collective-permute-start | bytes 98312 | tf_op jit(solution)/shard_map/ppermute | solution.py:130
  6.3 1.5 %collective-permute-start.1 = (bf16[64,256]{1,0:T(8,128)(2,1)}, bf16[64,256]{1,0:T(8,128)(2,1)S(1)}, u32[]{:S(2)}, u32[]{:S(2)}) collective-permute-start(bf16[64,256]{1,0:T(8,128)(2,1)} %refs_0_.1), channel_id=1, source_target_pairs={{0,2},{1,3},{2,0},{3,1},{4,6},{5,7},{6,4},{7,5},{8,10},{9,11},{10,... | collective-permute-start | bytes 98312 | tf_op jit(solution)/shard_map/ppermute | solution.py:130
  7.8 0.0 collective-permute-start
  7.8 0.0 collective-permute-done.7.refs_8_
  7.8 0.9 %collective-permute-start.11 = (bf16[64,256]{1,0:T(8,128)(2,1)S(1)}, bf16[64,256]{1,0:T(8,128)(2,1)S(1)}, u32[]{:S(2)}, u32[]{:S(2)}) collective-permute-start(bf16[64,256]{1,0:T(8,128)(2,1)S(1)} %collective-permute-done.7.refs_8_), channel_id=1, source_target_pairs={{0,4},{1,5},{2,6},{3,7},{4,0},{5,1},{6,2},{7,3},{8,12},{9,13},{10,... | collective-permute-start | bytes 98312 | tf_op jit(solution)/shard_map/ppermute | solution.py:130
  8.7 0.1 collective-permute-done.3.refs_4_
  8.9 1.5 %collective-permute-start.5 = (bf16[64,256]{1,0:T(8,128)(2,1)S(1)}, bf16[64,256]{1,0:T(8,128)(2,1)S(1)}, u32[]{:S(2)}, u32[]{:S(2)}) collective-permute-start(bf16[64,256]{1,0:T(8,128)(2,1)S(1)} %collective-permute-done.3.refs_4_), channel_id=1, source_target_pairs={{0,2},{1,3},{2,0},{3,1},{4,6},{5,7},{6,4},{7,5},{8,10},{9,11},{10,... | collective-permute-start | bytes 98312 | tf_op jit(solution)/shard_map/ppermute | solution.py:130
  10.3 0.0 collective-permute-start.4
  10.4 0.1 collective-permute-done.1.refs_2_
  10.4 0.4 collective-permute-start.2
  10.9 0.0 collective-permute-done.refs_1_
  10.9 1.3 %collective-permute-start.9 = (bf16[64,256]{1,0:T(8,128)(2,1)S(1)}, bf16[64,256]{1,0:T(8,128)(2,1)S(1)}, u32[]{:S(2)}, u32[]{:S(2)}) collective-permute-start(bf16[64,256]{1,0:T(8,128)(2,1)S(1)} %collective-permute-done.7.refs_8_), channel_id=1, source_target_pairs={{0,2},{1,3},{2,0},{3,1},{4,6},{5,7},{6,4},{7,5},{8,10},{9,11},{10,... | collective-permute-start | bytes 98312 | tf_op jit(solution)/shard_map/ppermute | solution.py:130
  12.2 0.0 collective-permute-done.11.refs_12_
  12.2 0.7 %collective-permute-start.13 = (bf16[64,256]{1,0:T(8,128)(2,1)S(1)}, bf16[64,256]{1,0:T(8,128)(2,1)S(1)}, u32[]{:S(2)}, u32[]{:S(2)}) collective-permute-start(bf16[64,256]{1,0:T(8,128)(2,1)S(1)} %collective-permute-done.11.refs_12_), channel_id=1, source_target_pairs={{0,2},{1,3},{2,0},{3,1},{4,6},{5,7},{6,4},{7,5},{8,10},{9,11},{10,... | collective-permute-start | bytes 98312 | tf_op jit(solution)/shard_map/ppermute | solution.py:130
  12.9 0.0 collective-permute-done.5.refs_6_
  12.9 0.0 collective-permute-start.8
  12.9 0.0 collective-permute-done.4.refs_5_
  12.9 0.5 %collective-permute-start.12 = (bf16[64,256]{1,0:T(8,128)(2,1)S(1)}, bf16[64,256]{1,0:T(8,128)(2,1)S(1)}, u32[]{:S(2)}, u32[]{:S(2)}) collective-permute-start(bf16[64,256]{1,0:T(8,128)(2,1)S(1)} %collective-permute-done.11.refs_12_), channel_id=1, source_target_pairs={{0,1},{1,0},{2,3},{3,2},{4,5},{5,4},{6,7},{7,6},{8,9},{9,8},{10,11... | collective-permute-start | bytes 98312 | tf_op jit(solution)/shard_map/ppermute | solution.py:130
  13.4 0.0 collective-permute-done.2.refs_3_
  13.4 0.1 collective-permute-start.6
  13.5 1.3 %collective-permute-done.9.refs_10_ = bf16[64,256]{1,0:T(8,128)(2,1)S(1)} collective-permute-done((bf16[64,256]{1,0:T(8,128)(2,1)S(1)}, bf16[64,256]{1,0:T(8,128)(2,1)S(1)}, u32[]{:S(2)}, u32[]{:S(2)}) %collective-permute-start.9) | collective-permute-done | bytes 32800 | tf_op jit(solution)/shard_map/ppermute | solution.py:130
  14.8 0.0 collective-permute-start.10
  14.8 1.3 %collective-permute-done.13.refs_14_ = bf16[64,256]{1,0:T(8,128)(2,1)S(1)} collective-permute-done((bf16[64,256]{1,0:T(8,128)(2,1)S(1)}, bf16[64,256]{1,0:T(8,128)(2,1)S(1)}, u32[]{:S(2)}, u32[]{:S(2)}) %collective-permute-start.13) | collective-permute-done | bytes 32800 | tf_op jit(solution)/shard_map/ppermute | solution.py:130
  16.1 0.0 collective-permute-start.14
  16.1 0.0 collective-permute-done.8.refs_9_
  16.1 0.0 collective-permute-done.6.refs_7_
  16.1 0.0 collective-permute-done.12.refs_13_
  16.1 0.0 collective-permute-done.10.refs_11_
  16.2 1.2 %collective-permute-done.14.refs_15_ = bf16[64,256]{1,0:T(8,128)(2,1)S(1)} collective-permute-done((bf16[64,256]{1,0:T(8,128)(2,1)S(1)}, bf16[64,256]{1,0:T(8,128)(2,1)S(1)}, u32[]{:S(2)}, u32[]{:S(2)}) %collective-permute-start.14) | collective-permute-done | bytes 32800 | tf_op jit(solution)/shard_map/ppermute | solution.py:130
  17.3 0.0 copy-start
  17.3 0.9 %copy-done = bf16[512,256]{1,0:T(8,128)(2,1)S(1)} copy-done((bf16[512,256]{1,0:T(8,128)(2,1)S(1)}, bf16[512,256]{1,0:T(8,128)(2,1)}, u32[]{:S(2)}) %copy-start) | copy-done | bytes 262168
  18.3 0.0 copy-start.1
  18.3 0.8 %copy-done.1 = bf16[64,256]{1,0:T(8,128)(2,1)S(1)} copy-done((bf16[64,256]{1,0:T(8,128)(2,1)S(1)}, bf16[64,256]{1,0:T(8,128)(2,1)}, u32[]{:S(2)}) %copy-start.1) | copy-done | bytes 32792
  19.0 0.0 copy-start.2
  19.0 0.7 %copy-done.2 = f32[1024]{0:T(1024)S(1)} copy-done((f32[1024]{0:T(1024)S(1)}, f32[1024]{0:T(1024)}, u32[]{:S(2)}) %copy-start.2) | copy-done | bytes 4120
  19.7 0.0 copy-start.3
  19.7 0.7 %copy-done.3 = f32[512]{0:T(512)S(1)} copy-done((f32[512]{0:T(512)S(1)}, f32[512]{0:T(512)}, u32[]{:S(2)}) %copy-start.3) | copy-done | bytes 2072
  20.4 1.6 %shard_map.59 = (f32[512,1024]{1,0:T(8,128)S(1)}, f32[16,8,128]{2,1,0:T(8,128)S(1)}) custom-call(bf16[512,256]{1,0:T(8,128)(2,1)S(1)} %copy-done, f32[512]{0:T(512)S(1)} %copy-done.3, f32[1024]{0:T(1024)S(1)} %copy-done.2, bf16[64,256]{1,0:T(8,128)(2,1)S(1)} %copy-done.1, bf16[64,256]{1,0:T(8,128)(2,1)S(1)} %collective-permute-done.refs_1_, ...), custom_call_target="tpu_custom_call" | custom-call | tf_op jit(solution)/shard_map/pallas_call | solution.py:109
  22.0 11.7 %all_to_all.16.g_ref = f32[16,8,128]{2,1,0:T(8,128)S(1)} all-to-all(f32[16,8,128]{2,1,0:T(8,128)S(1)} %get-tuple-element.7), channel_id=1, replica_groups=mesh['group'=2,'src'=16] {'src'}, dimensions={0} | all-to-all | bytes 131072 | tf_op jit(solution)/shard_map/all_to_all | solution.py:143
  33.8 1.8 %shard_map.60 = (f32[512]{0:T(512)}, f32[16,64]{1,0:T(8,128)S(1)}) custom-call(f32[512,1024]{1,0:T(8,128)S(1)} %get-tuple-element.6.s_ref, f32[16,8,128]{2,1,0:T(8,128)S(1)} %all_to_all.16.g_ref, f32[512]{0:T(512)S(1)} %copy-done.3, f32[1024]{0:T(1024)S(1)} %copy-done.2), custom_call_target="tpu_custom_call" | custom-call | tf_op jit(solution)/shard_map/pallas_call | solution.py:109
  35.5 9.0 %all_to_all.17 = f32[16,1,64]{2,1,0:T(1,128)S(1)} all-to-all(f32[16,1,64]{2,1,0:T(1,128)S(1)} %bitcast.5), channel_id=1, replica_groups=mesh['group'=2,'src'=16] {'src'}, dimensions={0} | all-to-all | bytes 8192 | tf_op jit(solution)/shard_map/all_to_all | solution.py:149
  44.5 0.5 %shard_map.61 = f32[64]{0:T(128)} custom-call(f32[16,64]{1,0:T(8,128)S(1)} %bitcast.4), custom_call_target="tpu_custom_call" | custom-call | tf_op jit(solution)/shard_map/pallas_call | solution.py:109
Async XLA Ops:
  0.6 7.2 %collective-permute-start.7 = (bf16[64,256]{1,0:T(8,128)(2,1)}, bf16[64,256]{1,0:T(8,128)(2,1)S(1)}, u32[]{:S(2)}, u32[]{:S(2)}) collective-permute-start(bf16[64,256]{1,0:T(8,128)(2,1)} %refs_0_.1), channel_id=1, source_target_pairs={{0,8},{1,9},{2,10},{3,11},{4,12},{5,13},{6,14},{7,15},{8,0},{9,1},... | collective-permute-start | bytes 98312 | tf_op jit(solution)/shard_map/ppermute | solution.py:130
  4.7 4.1 %collective-permute-start.3 = (bf16[64,256]{1,0:T(8,128)(2,1)}, bf16[64,256]{1,0:T(8,128)(2,1)S(1)}, u32[]{:S(2)}, u32[]{:S(2)}) collective-permute-start(bf16[64,256]{1,0:T(8,128)(2,1)} %refs_0_.1), channel_id=1, source_target_pairs={{0,4},{1,5},{2,6},{3,7},{4,0},{5,1},{6,2},{7,3},{8,12},{9,13},{10,... | collective-permute-start | bytes 98312 | tf_op jit(solution)/shard_map/ppermute | solution.py:130
  6.3 4.1 %collective-permute-start.1 = (bf16[64,256]{1,0:T(8,128)(2,1)}, bf16[64,256]{1,0:T(8,128)(2,1)S(1)}, u32[]{:S(2)}, u32[]{:S(2)}) collective-permute-start(bf16[64,256]{1,0:T(8,128)(2,1)} %refs_0_.1), channel_id=1, source_target_pairs={{0,2},{1,3},{2,0},{3,1},{4,6},{5,7},{6,4},{7,5},{8,10},{9,11},{10,... | collective-permute-start | bytes 98312 | tf_op jit(solution)/shard_map/ppermute | solution.py:130
  7.8 3.1 %collective-permute-start = (bf16[64,256]{1,0:T(8,128)(2,1)}, bf16[64,256]{1,0:T(8,128)(2,1)S(1)}, u32[]{:S(2)}, u32[]{:S(2)}) collective-permute-start(bf16[64,256]{1,0:T(8,128)(2,1)} %refs_0_.1), channel_id=1, source_target_pairs={{0,1},{1,0},{2,3},{3,2},{4,5},{5,4},{6,7},{7,6},{8,9},{9,8},{10,11... | collective-permute-start | bytes 98312 | tf_op jit(solution)/shard_map/ppermute | solution.py:130
  7.8 4.4 %collective-permute-start.11 = (bf16[64,256]{1,0:T(8,128)(2,1)S(1)}, bf16[64,256]{1,0:T(8,128)(2,1)S(1)}, u32[]{:S(2)}, u32[]{:S(2)}) collective-permute-start(bf16[64,256]{1,0:T(8,128)(2,1)S(1)} %collective-permute-done.7.refs_8_), channel_id=1, source_target_pairs={{0,4},{1,5},{2,6},{3,7},{4,0},{5,1},{6,2},{7,3},{8,12},{9,13},{10,... | collective-permute-start | bytes 98312 | tf_op jit(solution)/shard_map/ppermute | solution.py:130
  8.9 4.0 %collective-permute-start.5 = (bf16[64,256]{1,0:T(8,128)(2,1)S(1)}, bf16[64,256]{1,0:T(8,128)(2,1)S(1)}, u32[]{:S(2)}, u32[]{:S(2)}) collective-permute-start(bf16[64,256]{1,0:T(8,128)(2,1)S(1)} %collective-permute-done.3.refs_4_), channel_id=1, source_target_pairs={{0,2},{1,3},{2,0},{3,1},{4,6},{5,7},{6,4},{7,5},{8,10},{9,11},{10,... | collective-permute-start | bytes 98312 | tf_op jit(solution)/shard_map/ppermute | solution.py:130
  10.3 2.6 %collective-permute-start.4 = (bf16[64,256]{1,0:T(8,128)(2,1)S(1)}, bf16[64,256]{1,0:T(8,128)(2,1)S(1)}, u32[]{:S(2)}, u32[]{:S(2)}) collective-permute-start(bf16[64,256]{1,0:T(8,128)(2,1)S(1)} %collective-permute-done.3.refs_4_), channel_id=1, source_target_pairs={{0,1},{1,0},{2,3},{3,2},{4,5},{5,4},{6,7},{7,6},{8,9},{9,8},{10,11... | collective-permute-start | bytes 98312 | tf_op jit(solution)/shard_map/ppermute | solution.py:130
  10.4 3.0 %collective-permute-start.2 = (bf16[64,256]{1,0:T(8,128)(2,1)S(1)}, bf16[64,256]{1,0:T(8,128)(2,1)S(1)}, u32[]{:S(2)}, u32[]{:S(2)}) collective-permute-start(bf16[64,256]{1,0:T(8,128)(2,1)S(1)} %collective-permute-done.1.refs_2_), channel_id=1, source_target_pairs={{0,1},{1,0},{2,3},{3,2},{4,5},{5,4},{6,7},{7,6},{8,9},{9,8},{10,11... | collective-permute-start | bytes 98312 | tf_op jit(solution)/shard_map/ppermute | solution.py:130
  10.9 3.9 %collective-permute-start.9 = (bf16[64,256]{1,0:T(8,128)(2,1)S(1)}, bf16[64,256]{1,0:T(8,128)(2,1)S(1)}, u32[]{:S(2)}, u32[]{:S(2)}) collective-permute-start(bf16[64,256]{1,0:T(8,128)(2,1)S(1)} %collective-permute-done.7.refs_8_), channel_id=1, source_target_pairs={{0,2},{1,3},{2,0},{3,1},{4,6},{5,7},{6,4},{7,5},{8,10},{9,11},{10,... | collective-permute-start | bytes 98312 | tf_op jit(solution)/shard_map/ppermute | solution.py:130
  12.2 3.9 %collective-permute-start.13 = (bf16[64,256]{1,0:T(8,128)(2,1)S(1)}, bf16[64,256]{1,0:T(8,128)(2,1)S(1)}, u32[]{:S(2)}, u32[]{:S(2)}) collective-permute-start(bf16[64,256]{1,0:T(8,128)(2,1)S(1)} %collective-permute-done.11.refs_12_), channel_id=1, source_target_pairs={{0,2},{1,3},{2,0},{3,1},{4,6},{5,7},{6,4},{7,5},{8,10},{9,11},{10,... | collective-permute-start | bytes 98312 | tf_op jit(solution)/shard_map/ppermute | solution.py:130
  12.9 3.2 %collective-permute-start.8 = (bf16[64,256]{1,0:T(8,128)(2,1)S(1)}, bf16[64,256]{1,0:T(8,128)(2,1)S(1)}, u32[]{:S(2)}, u32[]{:S(2)}) collective-permute-start(bf16[64,256]{1,0:T(8,128)(2,1)S(1)} %collective-permute-done.7.refs_8_), channel_id=1, source_target_pairs={{0,1},{1,0},{2,3},{3,2},{4,5},{5,4},{6,7},{7,6},{8,9},{9,8},{10,11... | collective-permute-start | bytes 98312 | tf_op jit(solution)/shard_map/ppermute | solution.py:130
  12.9 3.2 %collective-permute-start.12 = (bf16[64,256]{1,0:T(8,128)(2,1)S(1)}, bf16[64,256]{1,0:T(8,128)(2,1)S(1)}, u32[]{:S(2)}, u32[]{:S(2)}) collective-permute-start(bf16[64,256]{1,0:T(8,128)(2,1)S(1)} %collective-permute-done.11.refs_12_), channel_id=1, source_target_pairs={{0,1},{1,0},{2,3},{3,2},{4,5},{5,4},{6,7},{7,6},{8,9},{9,8},{10,11... | collective-permute-start | bytes 98312 | tf_op jit(solution)/shard_map/ppermute | solution.py:130
  13.4 2.7 %collective-permute-start.6 = (bf16[64,256]{1,0:T(8,128)(2,1)S(1)}, bf16[64,256]{1,0:T(8,128)(2,1)S(1)}, u32[]{:S(2)}, u32[]{:S(2)}) collective-permute-start(bf16[64,256]{1,0:T(8,128)(2,1)S(1)} %collective-permute-done.5.refs_6_), channel_id=1, source_target_pairs={{0,1},{1,0},{2,3},{3,2},{4,5},{5,4},{6,7},{7,6},{8,9},{9,8},{10,11... | collective-permute-start | bytes 98312 | tf_op jit(solution)/shard_map/ppermute | solution.py:130
  14.8 1.4 %collective-permute-start.10 = (bf16[64,256]{1,0:T(8,128)(2,1)S(1)}, bf16[64,256]{1,0:T(8,128)(2,1)S(1)}, u32[]{:S(2)}, u32[]{:S(2)}) collective-permute-start(bf16[64,256]{1,0:T(8,128)(2,1)S(1)} %collective-permute-done.9.refs_10_), channel_id=1, source_target_pairs={{0,1},{1,0},{2,3},{3,2},{4,5},{5,4},{6,7},{7,6},{8,9},{9,8},{10,11... | collective-permute-start | bytes 98312 | tf_op jit(solution)/shard_map/ppermute | solution.py:130
  16.1 1.2 %collective-permute-start.14 = (bf16[64,256]{1,0:T(8,128)(2,1)S(1)}, bf16[64,256]{1,0:T(8,128)(2,1)S(1)}, u32[]{:S(2)}, u32[]{:S(2)}) collective-permute-start(bf16[64,256]{1,0:T(8,128)(2,1)S(1)} %collective-permute-done.13.refs_14_), channel_id=1, source_target_pairs={{0,1},{1,0},{2,3},{3,2},{4,5},{5,4},{6,7},{7,6},{8,9},{9,8},{10,11... | collective-permute-start | bytes 98312 | tf_op jit(solution)/shard_map/ppermute | solution.py:130
  17.3 1.0 %copy-start = (bf16[512,256]{1,0:T(8,128)(2,1)S(1)}, bf16[512,256]{1,0:T(8,128)(2,1)}, u32[]{:S(2)}) copy-start(bf16[512,256]{1,0:T(8,128)(2,1)} %e_ref.1) | copy-start | bytes 786436
  18.3 0.8 %copy-start.1 = (bf16[64,256]{1,0:T(8,128)(2,1)S(1)}, bf16[64,256]{1,0:T(8,128)(2,1)}, u32[]{:S(2)}) copy-start(bf16[64,256]{1,0:T(8,128)(2,1)} %refs_0_.1) | copy-start | bytes 98308
  19.0 0.7 %copy-start.2 = (f32[1024]{0:T(1024)S(1)}, f32[1024]{0:T(1024)}, u32[]{:S(2)}) copy-start(f32[1024]{0:T(1024)} %dlw_ref.3) | copy-start | bytes 12292
  19.7 0.7 %copy-start.3 = (f32[512]{0:T(512)S(1)}, f32[512]{0:T(512)}, u32[]{:S(2)}) copy-start(f32[512]{0:T(512)} %logw_ref.3) | copy-start | bytes 6148

commit v2 on v1

v2 whole, which is shorter than its diff:
```python
import functools
import math

import jax
import jax.numpy as jnp
from jax import lax
from jax.experimental import pallas as pl
from jax.experimental.pallas import tpu as pltpu
from jax.sharding import PartitionSpec as P

STRENGTH = 0.5
LOG2E = 1.4426950408889634
LN2 = 0.6931471805599453
VMEM_LIMIT = 40 * 1024 * 1024
ROWS = 128


def diagonal():
    return lax.broadcasted_iota(jnp.int32, (128, 128), 0) == lax.broadcasted_iota(
        jnp.int32, (128, 128), 1
    )


def to_column(row):
    return jnp.sum(
        jnp.where(diagonal(), jnp.broadcast_to(row, (128, 128)), 0.0), axis=1, keepdims=True
    )


def to_row(column):
    return jnp.sum(
        jnp.where(diagonal(), jnp.broadcast_to(column, (128, 128)), 0.0), axis=0, keepdims=True
    )


def load_kernel(e_hbm, t_hbm, logw_hbm, dlw_hbm, spread_ref, e_ref, logw_ref, dlw_ref, sems):
    copies = [
        pltpu.make_async_copy(t_hbm, spread_ref.at[0], sems.at[0]),
        pltpu.make_async_copy(e_hbm, e_ref, sems.at[1]),
        pltpu.make_async_copy(logw_hbm, logw_ref, sems.at[2]),
        pltpu.make_async_copy(dlw_hbm, dlw_ref, sems.at[3]),
    ]
    for copy in copies:
        copy.start()
    copies[0].wait()
    own = spread_ref[0]
    for d in range(1, spread_ref.shape[0]):
        spread_ref[d] = own
    for copy in copies[1:]:
        copy.wait()


def scores_of(e_ref, t_ref, s_ref):
    width = e_ref.shape[1]
    scale = LOG2E / (STRENGTH * math.sqrt(width))
    t = t_ref[...].reshape(-1, width)
    for b in range(s_ref.shape[0] // ROWS):
        part = slice(b * ROWS, (b + 1) * ROWS)
        s_ref[part, :] = (
            lax.dot_general(
                e_ref[part, :], t, (((1,), (1,)), ((), ())), preferred_element_type=jnp.float32
            )
            * scale
        )


def near_kernel(e_ref, t_ref, s_ref, max_ref, tot_ref):
    scores_of(e_ref, t_ref, s_ref)
    for b in range(s_ref.shape[0] // ROWS):
        part = slice(b * ROWS, (b + 1) * ROWS)
        s = s_ref[part, :]
        row_max = jnp.max(s, axis=1, keepdims=True)
        max_ref[part, :] = row_max
        tot_ref[part, :] = jnp.sum(jnp.exp2(s - row_max), axis=1, keepdims=True)


def column_sums(halves, pots):
    gives = []
    for s_ref in halves:
        top = None
        for b, pot in enumerate(pots):
            block = jnp.max(s_ref[b * ROWS : (b + 1) * ROWS, :] + pot, axis=0, keepdims=True)
            top = block if top is None else jnp.maximum(top, block)
        total = None
        for b, pot in enumerate(pots):
            terms = jnp.exp2(s_ref[b * ROWS : (b + 1) * ROWS, :] + pot - top)
            block = jnp.sum(terms, axis=0, keepdims=True)
            total = block if total is None else total + block
        gives.append(top + jnp.log2(total))
    return gives


def weights_column(logw_ref, b):
    pieces = [
        to_column(logw_ref[b * ROWS + k * 128 : b * ROWS + (k + 1) * 128].reshape(1, 128))
        for k in range(ROWS // 128)
    ]
    return jnp.concatenate(pieces, axis=0) * LOG2E


def far_kernel(n, e_ref, t_ref, near_ref, max_ref, tot_ref, logw_ref, far_ref, out_ref, half_ref):
    core = lax.rem(lax.axis_index("src"), 2)
    scores_of(e_ref, t_ref, far_ref)
    pots = []
    for b in range(far_ref.shape[0] // ROWS):
        part = slice(b * ROWS, (b + 1) * ROWS)
        s = far_ref[part, :]
        row_max = jnp.maximum(max_ref[part, :], jnp.max(s, axis=1, keepdims=True))
        tot = tot_ref[part, :] * jnp.exp2(max_ref[part, :] - row_max) + jnp.sum(
            jnp.exp2(s - row_max), axis=1, keepdims=True
        )
        pots.append(weights_column(logw_ref, b) - (row_max + jnp.log2(tot)))
    near, far = column_sums((near_ref, far_ref), pots)
    half_ref[core] = near
    half_ref[1 - core] = far
    chunks = near.shape[1] // 128
    both = [half_ref[0], half_ref[1]]
    tall = jnp.concatenate(
        [v[:, j * 128 : (j + 1) * 128] for v in both for j in range(chunks)], axis=0
    )
    for d in range(n):
        out_ref[d] = tall


def second_kernel(
    n, near_ref, far_ref, g_ref, logw_ref, dlw_ref, src_ref, out_ref, half_ref
):
    core = lax.rem(lax.axis_index("src"), 2)
    half = near_ref.shape[1]
    per = 2 * half // n
    chunks = half // 128
    g = g_ref[...]
    top = jnp.max(g, axis=0)
    lse = top + jnp.log2(jnp.sum(jnp.exp2(g - top[None]), axis=0))
    dlw = dlw_ref[...].reshape(1, 2 * half) * LOG2E
    for c in range(2):
        mine = [dlw[:, (2 * k + c) * per : (2 * k + c + 1) * per] for k in range(n // 2)]
        half_ref[c] = jnp.concatenate(mine, axis=1) - jnp.concatenate(
            [lse[c * chunks + j : c * chunks + j + 1, :] for j in range(chunks)], axis=1
        )
    near_pot, far_pot = half_ref[core], half_ref[1 - core]
    pots = []
    for b in range(near_ref.shape[0] // ROWS):
        part = slice(b * ROWS, (b + 1) * ROWS)
        near = near_ref[part, :] + near_pot
        far = far_ref[part, :] + far_pot
        row_max = jnp.maximum(
            jnp.max(near, axis=1, keepdims=True), jnp.max(far, axis=1, keepdims=True)
        )
        tot = jnp.sum(jnp.exp2(near - row_max), axis=1, keepdims=True) + jnp.sum(
            jnp.exp2(far - row_max), axis=1, keepdims=True
        )
        pot = weights_column(logw_ref, b) - (row_max + jnp.log2(tot))
        for k in range(ROWS // 128):
            row = to_row(pot[k * 128 : (k + 1) * 128, :]) * LN2
            src_ref[b * ROWS + k * 128 : b * ROWS + (k + 1) * 128] = row.reshape(128)
        pots.append(pot)
    near, far = column_sums((near_ref, far_ref), pots)
    half_ref[core] = near
    half_ref[1 - core] = far
    for c in range(2):
        v = half_ref[c]
        for k in range(n // 2):
            d = 2 * k + c
            out_ref[d : d + 1, :] = (
                v[:, k * per : (k + 1) * per] - dlw[:, d * per : (d + 1) * per]
            )


def last_kernel(g_ref, out_ref):
    g = g_ref[...]
    top = jnp.max(g, axis=0, keepdims=True)
    pot = -(top + jnp.log2(jnp.sum(jnp.exp2(g - top), axis=0, keepdims=True))) * LN2
    out_ref[...] = pot.reshape(out_ref.shape)


def call(kernel, out_shape, operands, scratch=(), space=pltpu.VMEM, cost=None):
    return pl.pallas_call(
        kernel,
        out_shape=out_shape,
        in_specs=[pl.BlockSpec(memory_space=space)] * len(operands),
        out_specs=jax.tree.map(lambda _: pl.BlockSpec(memory_space=pltpu.VMEM), out_shape),
        scratch_shapes=list(scratch),
        compiler_params=pltpu.CompilerParams(vmem_limit_bytes=VMEM_LIMIT),
        cost_estimate=cost,
    )(*operands)


def local(emitter_vectors, targets, src_logw, dst_logw):
    n = lax.axis_size("src")
    rows, width = emitter_vectors.shape
    per = targets.shape[0]
    cols = dst_logw.shape[0]
    half = cols // 2
    f32 = jnp.float32
    shape = jax.ShapeDtypeStruct
    spread, emitter, logw, dlw = call(
        load_kernel,
        (
            shape((n // 2, per, width), targets.dtype),
            shape(emitter_vectors.shape, emitter_vectors.dtype),
            shape(src_logw.shape, f32),
            shape(dst_logw.shape, f32),
        ),
        [
            pltpu.with_memory_space_constraint(a, pltpu.HBM)
            for a in (emitter_vectors, targets, src_logw, dst_logw)
        ],
        [pltpu.SemaphoreType.DMA((4,))],
        pltpu.HBM,
    )
    same_core = [list(range(c, n, 2)) for c in range(2)]
    near_targets = lax.all_to_all(spread, "src", 0, 0, axis_index_groups=same_core)
    far_targets = lax.ppermute(near_targets, "src", [(i, i ^ 1) for i in range(n)])
    cost = pl.CostEstimate(
        flops=2 * rows * half * width, bytes_accessed=rows * half * 4, transcendentals=rows * half
    )
    near, near_max, near_tot = call(
        near_kernel,
        (shape((rows, half), f32), shape((rows, 1), f32), shape((rows, 1), f32)),
        [emitter, near_targets],
        cost=cost,
    )
    far, sent = call(
        functools.partial(far_kernel, n),
        (shape((rows, half), f32), shape((n, cols // 128, 128), f32)),
        [emitter, far_targets, near, near_max, near_tot, logw],
        [pltpu.VMEM((2, 1, half), f32)],
    )
    heard = lax.all_to_all(sent, "src", 0, 0)
    src_pot, parts = call(
        functools.partial(second_kernel, n),
        (shape((rows,), f32), shape((n, per), f32)),
        [near, far, heard, logw, dlw],
        [pltpu.VMEM((2, 1, half), f32)],
    )
    own = lax.all_to_all(parts, "src", 0, 0)
    (own_pot,) = call(last_kernel, (shape((per,), f32),), [own])
    return (src_pot, own_pot)


def solution(mesh):
    return jax.shard_map(
        local,
        mesh=mesh,
        in_specs=(
            P(("group", "src"), None),
            P(("group", "src"), None),
            P(("group", "src")),
            P("group"),
        ),
        out_specs=(P(("group", "src")), P(("group", "src"))),
        check_vma=False,
    )
```

time: 45.4 us -> 43 us (0.947)
  blocking collectives: 20.7 us -> 35.3 us
  starting transfers between devices: 12.6 us -> 0.01 us
  waiting for transfers between devices: 4.02 us -> 0.87 us
  local copies, waits for them, and re-layouts: 3.07 us -> 0 us
  Pallas kernels: 3.93 us -> 5.86 us
    all_to_all x1 -> x2, blocking collectives: 11.7 us -> 26.4 us  [the longest x1 16 us: local(): lax.all_to_all(spread, 'src', 0, 0, axis_index_groups=same_core)]
    ppermute x15 -> x1, starting transfers between devices: 12.6 us -> 0.01 us  [local(): lax.ppermute(near_targets, 'src', [(i, i ^ 1) for i in range(n)])]
    ppermute x15 -> x1, waiting for transfers between devices: 4.02 us -> 0.87 us  [local(): lax.ppermute(near_targets, 'src', [(i, i ^ 1) for i in range(n)])]
    unnamed x8 -> x0, local copies, waits for them, and re-layouts: 3.07 us -> none
    pallas_call x3 -> x5, Pallas kernels: 3.93 us -> 5.86 us  [call(): pl.pallas_call(kernel, out_shape=out_shape, in_specs=[pl.BlockSpec(memory...]
  transfers between devices with their start and end apart: 15 -> 1, of which waited for: 5 -> 1; matrix products, arithmetic and copies ran while one was open for 0% -> 0% of each run, Pallas kernels for 0% -> 2%
where the time goes in v2:
time: 43 us; the launch traced here: 42.7 us
  blocking collectives  35.3 us (82%)
  Pallas kernels  5.86 us (14%)
  waiting for transfers between devices  0.87 us (2%)
  between operations  0.65 us (2%)
    all_to_all x1, blocking collectives, local(): lax.all_to_all(spread, 'src', 0, 0, axis_index_groups=same_core)  16 us
    all_to_all x1, blocking collectives, local(): heard = lax.all_to_all(sent, 'src', 0, 0)  10.4 us
    all_to_all x1, blocking collectives, local(): own = lax.all_to_all(parts, 'src', 0, 0)  8.97 us
    pallas_call x5, Pallas kernels, call(): pl.pallas_call(kernel, out_shape=out_shape, in_specs=[pl.BlockSpec(memory...  5.86 us
    ppermute x1, waiting for transfers between devices, local(): lax.ppermute(near_targets, 'src', [(i, i ^ 1) for i in range(n)])  0.87 us
  transfers between devices with their start and end apart: 1, of which 1 were waited for; matrix products, arithmetic and copies ran while one was open for 0% of the time, Pallas kernels for 2%

profile of v2, /device:TPU:0, one launch (start us, length us, event | category | flops | bytes accessed | tf_op | source)
XLA Modules:
  0.0 42.7 jit_solution(2133912540090187589)
XLA Ops:
  0.6 1.0 %shard_map.59 = (bf16[8,64,256]{2,1,0:T(8,128)(2,1)S(1)}, bf16[512,256]{1,0:T(8,128)(2,1)S(1)}, f32[512]{0:T(512)S(1)}, f32[1024]{0:T(1024)S(1)}) custom-call(bf16[512,256]{1,0:T(8,128)(2,1)} %e_hbm.1, bf16[64,256]{1,0:T(8,128)(2,1)} %t_hbm.1, f32[512]{0:T(512)} %logw_hbm.1, f32[1024]{0:T(1024)} %dlw_hbm.1), custom_call_target="tpu_custom_call" | custom-call | tf_op jit(solution)/shard_map/pallas_call | solution.py:178
  1.6 16.0 %all_to_all.21.t_ref = bf16[8,64,256]{2,1,0:T(8,128)(2,1)S(1)} all-to-all(bf16[8,64,256]{2,1,0:T(8,128)(2,1)S(1)} %get-tuple-element.14), channel_id=1, replica_groups={{0,2,4,6,8,10,12,14},{1,3,5,7,9,11,13,15},{16,18,20,22,24,26,28,30},{17..., dimensions={0} | all-to-all | bytes 524288 | tf_op jit(solution)/shard_map/all_to_all | solution.py:213
  17.6 0.0 collective-permute-start
  17.6 0.7 %shard_map.60 = (f32[512,512]{1,0:T(8,128)S(1)}, f32[512,1]{1,0:T(8,128)S(1)}, f32[512,1]{1,0:T(8,128)S(1)}) custom-call(bf16[512,256]{1,0:T(8,128)(2,1)S(1)} %get-tuple-element.13.e_ref, bf16[8,64,256]{2,1,0:T(8,128)(2,1)S(1)} %all_to_all.21.t_ref), custom_call_target="tpu_custom_call" | custom-call | flops 134217728 | bytes 1048576 | tf_op jit(solution)/shard_map/pallas_call | solution.py:178
  18.3 0.9 %collective-permute-done.t_ref = bf16[8,64,256]{2,1,0:T(8,128)(2,1)S(1)} collective-permute-done((bf16[8,64,256]{2,1,0:T(8,128)(2,1)S(1)}, bf16[8,64,256]{2,1,0:T(8,128)(2,1)S(1)}, u32[]{:S(2)}, u32[]{:S(2)}) %collective-permute-start) | collective-permute-done | bytes 262176 | tf_op jit(solution)/shard_map/ppermute | solution.py:214
  19.2 2.0 %shard_map.61 = (f32[512,512]{1,0:T(8,128)S(1)}, f32[16,8,128]{2,1,0:T(8,128)S(1)}) custom-call(bf16[512,256]{1,0:T(8,128)(2,1)S(1)} %get-tuple-element.13.e_ref, bf16[8,64,256]{2,1,0:T(8,128)(2,1)S(1)} %collective-permute-done.t_ref, f32[512,512]{1,0:T(8,128)S(1)} %get-tuple-element.15.near_ref, f32[512,1]{1,0:T(8,128)S(1)} %get-tuple-element.16.max_ref, ...), custom_call_target="tpu_custom_call" | custom-call | tf_op jit(solution)/shard_map/pallas_call | solution.py:178
  21.1 10.4 %all_to_all.22.g_ref = f32[16,8,128]{2,1,0:T(8,128)S(1)} all-to-all(f32[16,8,128]{2,1,0:T(8,128)S(1)} %get-tuple-element.20), channel_id=1, replica_groups=mesh['group'=2,'src'=16] {'src'}, dimensions={0} | all-to-all | bytes 131072 | tf_op jit(solution)/shard_map/all_to_all | solution.py:230
  31.5 1.7 %shard_map.62 = (f32[512]{0:T(512)}, f32[16,64]{1,0:T(8,128)S(1)}) custom-call(f32[512,512]{1,0:T(8,128)S(1)} %get-tuple-element.15.near_ref, f32[512,512]{1,0:T(8,128)S(1)} %get-tuple-element.19.far_ref, f32[16,8,128]{2,1,0:T(8,128)S(1)} %all_to_all.22.g_ref, f32[512]{0:T(512)S(1)} %get-tuple-element.18.logw_ref, f32[1024]{0:T(1024)S(1)} %get-tuple-element.21.dlw_ref), custom_call_target="tpu_custom_call" | custom-call | tf_op jit(solution)/shard_map/pallas_call | solution.py:178
  33.2 9.0 %all_to_all.23 = f32[16,1,64]{2,1,0:T(1,128)S(1)} all-to-all(f32[16,1,64]{2,1,0:T(1,128)S(1)} %bitcast.5), channel_id=1, replica_groups=mesh['group'=2,'src'=16] {'src'}, dimensions={0} | all-to-all | bytes 8192 | tf_op jit(solution)/shard_map/all_to_all | solution.py:237
  42.2 0.5 %shard_map.63 = f32[64]{0:T(128)} custom-call(f32[16,64]{1,0:T(8,128)S(1)} %bitcast.4), custom_call_target="tpu_custom_call" | custom-call | tf_op jit(solution)/shard_map/pallas_call | solution.py:178
Async XLA Ops:
  17.6 1.5 %collective-permute-start = (bf16[8,64,256]{2,1,0:T(8,128)(2,1)S(1)}, bf16[8,64,256]{2,1,0:T(8,128)(2,1)S(1)}, u32[]{:S(2)}, u32[]{:S(2)}) collective-permute-start(bf16[8,64,256]{2,1,0:T(8,128)(2,1)S(1)} %all_to_all.21.t_ref), channel_id=1, source_target_pairs={{0,1},{1,0},{2,3},{3,2},{4,5},{5,4},{6,7},{7,6},{8,9},{9,8},{10,11... | collective-permute-start | bytes 786440 | tf_op jit(solution)/shard_map/ppermute | solution.py:214

commit v3 on v2

v3 whole, which is shorter than its diff:
```python
import functools
import math

import jax
import jax.numpy as jnp
from jax import lax
from jax.experimental import pallas as pl
from jax.experimental.pallas import tpu as pltpu
from jax.sharding import PartitionSpec as P

STRENGTH = 0.5
LOG2E = 1.4426950408889634
LN2 = 0.6931471805599453
VMEM_LIMIT = 40 * 1024 * 1024


def diagonal():
    return lax.broadcasted_iota(jnp.int32, (128, 128), 0) == lax.broadcasted_iota(
        jnp.int32, (128, 128), 1
    )


def to_column(row):
    return jnp.sum(
        jnp.where(diagonal(), jnp.broadcast_to(row, (128, 128)), 0.0), axis=1, keepdims=True
    )


def to_row(column):
    return jnp.sum(
        jnp.where(diagonal(), jnp.broadcast_to(column, (128, 128)), 0.0), axis=0, keepdims=True
    )


def device_at(n, core, place):
    return (place % 2) * (n // 2) + (place // 2) * 2 + core


def load_kernel(
    n, e_hbm, t_hbm, logw_hbm, dlw_hbm, e_ref, t_ref, logw_ref, dlw_ref, row_ref, all_ref, sems
):
    copies = [
        pltpu.make_async_copy(logw_hbm, row_ref, sems.at[0]),
        pltpu.make_async_copy(dlw_hbm, all_ref, sems.at[1]),
        pltpu.make_async_copy(t_hbm, t_ref, sems.at[2]),
        pltpu.make_async_copy(e_hbm, e_ref, sems.at[3]),
    ]
    for copy in copies:
        copy.start()
    copies[0].wait()
    for k in range(row_ref.shape[0] // 128):
        part = slice(k * 128, (k + 1) * 128)
        logw_ref[part, :] = to_column(row_ref[part].reshape(1, 128)) * LOG2E
    copies[1].wait()
    dlw = all_ref[...].reshape(1, all_ref.shape[0]) * LOG2E
    per = all_ref.shape[0] // n
    for core in range(2):
        owners = [device_at(n, core, place) for place in range(n // 2)]
        dlw_ref[core] = jnp.concatenate([dlw[:, d * per : (d + 1) * per] for d in owners], axis=1)
    copies[2].wait()
    copies[3].wait()


def spread_kernel(n, t_ref, got_ref, out_ref):
    per = t_ref.shape[0]
    upper = lax.axis_index("src") // (n // 2)
    own = t_ref[...]
    got = got_ref[...]
    for d in range(out_ref.shape[0]):
        out_ref[d, pl.ds(pl.multiple_of(upper * per, per), per), :] = own
        out_ref[d, pl.ds(pl.multiple_of((1 - upper) * per, per), per), :] = got


def scores_of(e_ref, t_ref):
    width = e_ref.shape[1]
    return lax.dot_general(
        e_ref[...],
        t_ref[...].reshape(-1, width),
        (((1,), (1,)), ((), ())),
        preferred_element_type=jnp.float32,
    ) * (LOG2E / (STRENGTH * math.sqrt(width)))


def near_kernel(e_ref, t_ref, s_ref, max_ref, tot_ref):
    s = scores_of(e_ref, t_ref)
    s_ref[...] = s
    row_max = jnp.max(s, axis=1, keepdims=True)
    max_ref[...] = row_max
    tot_ref[...] = jnp.sum(jnp.exp2(s - row_max), axis=1, keepdims=True)


def column_sums(s, pot):
    t = s + pot
    top = jnp.max(t, axis=0, keepdims=True)
    return top + jnp.log2(jnp.sum(jnp.exp2(t - top), axis=0, keepdims=True))


def far_kernel(n, e_ref, t_ref, near_ref, max_ref, tot_ref, logw_ref, far_ref, out_ref, half_ref):
    core = lax.rem(lax.axis_index("src"), 2)
    s = scores_of(e_ref, t_ref)
    far_ref[...] = s
    near_max = max_ref[...]
    row_max = jnp.maximum(near_max, jnp.max(s, axis=1, keepdims=True))
    tot = tot_ref[...] * jnp.exp2(near_max - row_max) + jnp.sum(
        jnp.exp2(s - row_max), axis=1, keepdims=True
    )
    pot = logw_ref[...] - (row_max + jnp.log2(tot))
    half_ref[core] = column_sums(near_ref[...], pot)
    half_ref[1 - core] = column_sums(s, pot)
    chunks = half_ref.shape[2] // 128
    both = [half_ref[0], half_ref[1]]
    tall = jnp.concatenate(
        [v[:, j * 128 : (j + 1) * 128] for v in both for j in range(chunks)], axis=0
    )
    for d in range(n):
        out_ref[d] = tall


def second_kernel(n, near_ref, far_ref, g_ref, logw_ref, dlw_ref, src_ref, out_ref, half_ref):
    core = lax.rem(lax.axis_index("src"), 2)
    half = near_ref.shape[1]
    per = 2 * half // n
    chunks = half // 128
    g = g_ref[...]
    top = jnp.max(g, axis=0)
    lse = top + jnp.log2(jnp.sum(jnp.exp2(g - top[None]), axis=0))
    for c in range(2):
        half_ref[c] = dlw_ref[c] - jnp.concatenate(
            [lse[c * chunks + j : c * chunks + j + 1, :] for j in range(chunks)], axis=1
        )
    near = near_ref[...] + half_ref[core]
    far = far_ref[...] + half_ref[1 - core]
    row_max = jnp.maximum(
        jnp.max(near, axis=1, keepdims=True), jnp.max(far, axis=1, keepdims=True)
    )
    tot = jnp.sum(jnp.exp2(near - row_max), axis=1, keepdims=True) + jnp.sum(
        jnp.exp2(far - row_max), axis=1, keepdims=True
    )
    pot = logw_ref[...] - (row_max + jnp.log2(tot))
    src_ref[...] = pot
    half_ref[core] = column_sums(near_ref[...], pot) - dlw_ref[core]
    half_ref[1 - core] = column_sums(far_ref[...], pot) - dlw_ref[1 - core]
    for c in range(2):
        v = half_ref[c]
        for place in range(n // 2):
            d = device_at(n, c, place)
            out_ref[d : d + 1, :] = v[:, place * per : (place + 1) * per]


def last_kernel(g_ref, pot_ref, src_ref, own_ref):
    for k in range(src_ref.shape[0] // 128):
        part = slice(k * 128, (k + 1) * 128)
        src_ref[part] = (to_row(pot_ref[part, :]) * LN2).reshape(128)
    g = g_ref[...]
    top = jnp.max(g, axis=0, keepdims=True)
    pot = -(top + jnp.log2(jnp.sum(jnp.exp2(g - top), axis=0, keepdims=True))) * LN2
    own_ref[...] = pot.reshape(own_ref.shape)


def call(kernel, out_shape, operands, scratch=(), space=pltpu.VMEM, cost=None):
    return pl.pallas_call(
        kernel,
        out_shape=out_shape,
        in_specs=[pl.BlockSpec(memory_space=space)] * len(operands),
        out_specs=jax.tree.map(lambda _: pl.BlockSpec(memory_space=pltpu.VMEM), out_shape),
        scratch_shapes=list(scratch),
        compiler_params=pltpu.CompilerParams(vmem_limit_bytes=VMEM_LIMIT),
        cost_estimate=cost,
    )(*operands)


def local(emitter_vectors, targets, src_logw, dst_logw):
    n = lax.axis_size("src")
    rows, width = emitter_vectors.shape
    per = targets.shape[0]
    cols = dst_logw.shape[0]
    half = cols // 2
    f32 = jnp.float32
    shape = jax.ShapeDtypeStruct
    partner = lax.ppermute(targets, "src", [(i, (i + n // 2) % n) for i in range(n)])
    emitter, own_targets, logw, dlw = call(
        functools.partial(load_kernel, n),
        (
            shape(emitter_vectors.shape, emitter_vectors.dtype),
            shape(targets.shape, targets.dtype),
            shape((rows, 1), f32),
            shape((2, 1, half), f32),
        ),
        [
            pltpu.with_memory_space_constraint(a, pltpu.HBM)
            for a in (emitter_vectors, targets, src_logw, dst_logw)
        ],
        [
            pltpu.VMEM(src_logw.shape, f32),
            pltpu.VMEM(dst_logw.shape, f32),
            pltpu.SemaphoreType.DMA((4,)),
        ],
        pltpu.HBM,
        pl.CostEstimate(flops=0, bytes_accessed=4 * rows * width, transcendentals=0),
    )
    (spread,) = call(
        functools.partial(spread_kernel, n),
        (shape((n // 4, 2 * per, width), targets.dtype),),
        [own_targets, partner],
    )
    quarter = [
        [s * (n // 2) + 2 * q + c for q in range(n // 4)] for s in range(2) for c in range(2)
    ]
    near_targets = lax.all_to_all(spread, "src", 0, 0, axis_index_groups=quarter)
    far_targets = lax.ppermute(near_targets, "src", [(i, i ^ 1) for i in range(n)])
    near, near_max, near_tot = call(
        near_kernel,
        (shape((rows, half), f32), shape((rows, 1), f32), shape((rows, 1), f32)),
        [emitter, near_targets],
        cost=pl.CostEstimate(
            flops=2 * rows * half * width,
            bytes_accessed=rows * half * 4,
            transcendentals=rows * half,
        ),
    )
    far, sent = call(
        functools.partial(far_kernel, n),
        (shape((rows, half), f32), shape((n, cols // 128, 128), f32)),
        [emitter, far_targets, near, near_max, near_tot, logw],
        [pltpu.VMEM((2, 1, half), f32)],
    )
    heard = lax.all_to_all(sent, "src", 0, 0)
    pot, parts = call(
        functools.partial(second_kernel, n),
        (shape((rows, 1), f32), shape((n, per), f32)),
        [near, far, heard, logw, dlw],
        [pltpu.VMEM((2, 1, half), f32)],
    )
    own = lax.all_to_all(parts, "src", 0, 0)
    return call(last_kernel, (shape((rows,), f32), shape((per,), f32)), [own, pot])


def solution(mesh):
    return jax.shard_map(
        local,
        mesh=mesh,
        in_specs=(
            P(("group", "src"), None),
            P(("group", "src"), None),
            P(("group", "src")),
            P("group"),
        ),
        out_specs=(P(("group", "src")), P(("group", "src"))),
        check_vma=False,
    )
```

time: 43 us -> 42.3 us (0.984)
  blocking collectives: 35.3 us -> 29.5 us
  starting transfers between devices: 0.01 us -> 4.1 us
  waiting for transfers between devices: 0.87 us -> 2.45 us
  Pallas kernels: 5.86 us -> 5.33 us
    all_to_all x1, blocking collectives: 16 us -> 9.28 us  [local(): lax.all_to_all(spread, 'src', 0, 0, axis_index_groups=quarter)]
    ppermute x0 -> x1, starting transfers between devices: none -> 4.1 us  [local(): lax.ppermute(targets, 'src', [(i, (i + n // 2) % n) for i in range(n)])]
    ppermute x0 -> x1, waiting for transfers between devices: none -> 1.41 us  [local(): lax.ppermute(targets, 'src', [(i, (i + n // 2) % n) for i in range(n)])]
    all_to_all x1, blocking collectives: 10.4 us -> 11.3 us  [local(): heard = lax.all_to_all(sent, 'src', 0, 0)]
    pallas_call x5 -> x6, Pallas kernels: 5.86 us -> 5.33 us  [call(): pl.pallas_call(kernel, out_shape=out_shape, in_specs=[pl.BlockSpec(memory...]
  transfers between devices with their start and end apart: 1 -> 2, of which waited for: 1 -> 2; matrix products, arithmetic and copies ran while one was open for 0% -> 0% of each run, Pallas kernels for 2% -> 4%
where the time goes in v3:
time: 42.3 us; the launch traced here: 42.1 us
  blocking collectives  29.5 us (70%)
  Pallas kernels  5.33 us (13%)
  starting transfers between devices  4.1 us (10%)
  waiting for transfers between devices  2.45 us (6%)
  between operations  0.65 us (2%)
    all_to_all x1, blocking collectives, local(): heard = lax.all_to_all(sent, 'src', 0, 0)  11.3 us
    all_to_all x1, blocking collectives, local(): lax.all_to_all(spread, 'src', 0, 0, axis_index_groups=quarter)  9.28 us
    all_to_all x1, blocking collectives, local(): own = lax.all_to_all(parts, 'src', 0, 0)  8.98 us
    pallas_call x6, Pallas kernels, call(): pl.pallas_call(kernel, out_shape=out_shape, in_specs=[pl.BlockSpec(memory...  5.33 us
    ppermute x1, starting transfers between devices, local(): lax.ppermute(targets, 'src', [(i, (i + n // 2) % n) for i in range(n)])  4.1 us
    ppermute x1, waiting for transfers between devices, local(): lax.ppermute(targets, 'src', [(i, (i + n // 2) % n) for i in range(n)])  1.41 us
    ppermute x1, waiting for transfers between devices, local(): lax.ppermute(near_targets, 'src', [(i, i ^ 1) for i in range(n)])  1.04 us
  transfers between devices with their start and end apart: 2, of which 2 were waited for; matrix products, arithmetic and copies ran while one was open for 0% of the time, Pallas kernels for 4%

profile of v3, /device:TPU:0, one launch (start us, length us, event | category | flops | bytes accessed | tf_op | source)
XLA Modules:
  0.0 42.1 jit_solution(4089992401117486448)
XLA Ops:
  0.6 4.1 %collective-permute-start = (bf16[64,256]{1,0:T(8,128)(2,1)}, bf16[64,256]{1,0:T(8,128)(2,1)S(1)}, u32[]{:S(2)}, u32[]{:S(2)}) collective-permute-start(bf16[64,256]{1,0:T(8,128)(2,1)} %t_hbm.1), channel_id=1, source_target_pairs={{0,8},{1,9},{2,10},{3,11},{4,12},{5,13},{6,14},{7,15},{8,0},{9,1},... | collective-permute-start | bytes 98312 | tf_op jit(solution)/shard_map/ppermute | solution.py:180
  4.7 1.0 %shard_map.59 = (bf16[512,256]{1,0:T(8,128)(2,1)S(1)}, bf16[64,256]{1,0:T(8,128)(2,1)S(1)}, f32[512,1]{1,0:T(8,128)S(1)}, f32[2,1,512]{2,1,0:T(1,128)S(1)}) custom-call(bf16[512,256]{1,0:T(8,128)(2,1)} %e_hbm.1, bf16[64,256]{1,0:T(8,128)(2,1)} %t_hbm.1, f32[512]{0:T(512)} %logw_hbm.1, f32[1024]{0:T(1024)} %dlw_hbm.1), custom_call_target="tpu_custom_call" | custom-call | bytes 524288 | tf_op jit(solution)/shard_map/pallas_call | solution.py:161
  5.8 1.4 %collective-permute-done.got_ref = bf16[64,256]{1,0:T(8,128)(2,1)S(1)} collective-permute-done((bf16[64,256]{1,0:T(8,128)(2,1)}, bf16[64,256]{1,0:T(8,128)(2,1)S(1)}, u32[]{:S(2)}, u32[]{:S(2)}) %collective-permute-start) | collective-permute-done | bytes 32800 | tf_op jit(solution)/shard_map/ppermute | solution.py:180
  7.2 9.3 %all_to_all.21.t_ref = bf16[4,128,256]{2,1,0:T(8,128)(2,1)S(1)} all-to-all(bf16[4,128,256]{2,1,0:T(8,128)(2,1)S(1)} %shard_map.60), channel_id=1, replica_groups={{0,2,4,6},{1,3,5,7},{8,10,12,14},{9,11,13,15},{16,18,20,22},{17,19,21,2..., dimensions={0} | all-to-all | bytes 524288 | tf_op jit(solution)/shard_map/all_to_all | solution.py:209
  16.5 0.0 collective-permute-start.1
  16.5 0.5 %shard_map.61 = (f32[512,512]{1,0:T(8,128)S(1)}, f32[512,1]{1,0:T(8,128)S(1)}, f32[512,1]{1,0:T(8,128)S(1)}) custom-call(bf16[512,256]{1,0:T(8,128)(2,1)S(1)} %get-tuple-element.13.e_ref, bf16[4,128,256]{2,1,0:T(8,128)(2,1)S(1)} %all_to_all.21.t_ref), custom_call_target="tpu_custom_call" | custom-call | flops 134217728 | bytes 1048576 | tf_op jit(solution)/shard_map/pallas_call | solution.py:161
  17.0 1.0 %collective-permute-done.1.t_ref = bf16[4,128,256]{2,1,0:T(8,128)(2,1)S(1)} collective-permute-done((bf16[4,128,256]{2,1,0:T(8,128)(2,1)S(1)}, bf16[4,128,256]{2,1,0:T(8,128)(2,1)S(1)}, u32[]{:S(2)}, u32[]{:S(2)}) %collective-permute-start.1) | collective-permute-done | bytes 262176 | tf_op jit(solution)/shard_map/ppermute | solution.py:210
  18.0 1.9 %shard_map.62 = (f32[512,512]{1,0:T(8,128)S(1)}, f32[16,8,128]{2,1,0:T(8,128)S(1)}) custom-call(bf16[512,256]{1,0:T(8,128)(2,1)S(1)} %get-tuple-element.13.e_ref, bf16[4,128,256]{2,1,0:T(8,128)(2,1)S(1)} %collective-permute-done.1.t_ref, f32[512,512]{1,0:T(8,128)S(1)} %get-tuple-element.15.near_ref, f32[512,1]{1,0:T(8,128)S(1)} %get-tuple-element.16.max_ref, ...), custom_call_target="tpu_custom_call" | custom-call | tf_op jit(solution)/shard_map/pallas_call | solution.py:161
  20.0 11.3 %all_to_all.22.g_ref = f32[16,8,128]{2,1,0:T(8,128)S(1)} all-to-all(f32[16,8,128]{2,1,0:T(8,128)S(1)} %get-tuple-element.20), channel_id=1, replica_groups=mesh['group'=2,'src'=16] {'src'}, dimensions={0} | all-to-all | bytes 131072 | tf_op jit(solution)/shard_map/all_to_all | solution.py:227
  31.2 1.1 %shard_map.63 = (f32[512,1]{1,0:T(8,128)S(1)}, f32[16,64]{1,0:T(8,128)S(1)}) custom-call(f32[512,512]{1,0:T(8,128)S(1)} %get-tuple-element.15.near_ref, f32[512,512]{1,0:T(8,128)S(1)} %get-tuple-element.19.far_ref, f32[16,8,128]{2,1,0:T(8,128)S(1)} %all_to_all.22.g_ref, f32[512,1]{1,0:T(8,128)S(1)} %get-tuple-element.18.logw_ref, ...), custom_call_target="tpu_custom_call" | custom-call | tf_op jit(solution)/shard_map/pallas_call | solution.py:161
  32.4 9.0 %all_to_all.23 = f32[16,1,64]{2,1,0:T(1,128)S(1)} all-to-all(f32[16,1,64]{2,1,0:T(1,128)S(1)} %bitcast.5), channel_id=1, replica_groups=mesh['group'=2,'src'=16] {'src'}, dimensions={0} | all-to-all | bytes 8192 | tf_op jit(solution)/shard_map/all_to_all | solution.py:234
  41.3 0.7 %shard_map.64 = (f32[512]{0:T(512)}, f32[64]{0:T(128)}) custom-call(f32[16,64]{1,0:T(8,128)S(1)} %bitcast.4, f32[512,1]{1,0:T(8,128)S(1)} %get-tuple-element.23.pot_ref), custom_call_target="tpu_custom_call" | custom-call | tf_op jit(solution)/shard_map/pallas_call | solution.py:161
  (1 shorter events, 0.0 us)
Async XLA Ops:
  0.6 6.6 %collective-permute-start = (bf16[64,256]{1,0:T(8,128)(2,1)}, bf16[64,256]{1,0:T(8,128)(2,1)S(1)}, u32[]{:S(2)}, u32[]{:S(2)}) collective-permute-start(bf16[64,256]{1,0:T(8,128)(2,1)} %t_hbm.1), channel_id=1, source_target_pairs={{0,8},{1,9},{2,10},{3,11},{4,12},{5,13},{6,14},{7,15},{8,0},{9,1},... | collective-permute-start | bytes 98312 | tf_op jit(solution)/shard_map/ppermute | solution.py:180
  16.5 1.5 %collective-permute-start.1 = (bf16[4,128,256]{2,1,0:T(8,128)(2,1)S(1)}, bf16[4,128,256]{2,1,0:T(8,128)(2,1)S(1)}, u32[]{:S(2)}, u32[]{:S(2)}) collective-permute-start(bf16[4,128,256]{2,1,0:T(8,128)(2,1)S(1)} %all_to_all.21.t_ref), channel_id=1, source_target_pairs={{0,1},{1,0},{2,3},{3,2},{4,5},{5,4},{6,7},{7,6},{8,9},{9,8},{10,11... | collective-permute-start | bytes 786440 | tf_op jit(solution)/shard_map/ppermute | solution.py:210

commit v4 on v3

--- a/solution.py
+++ b/solution.py
@@ -12,24 +12,22 @@
 LOG2E = 1.4426950408889634
 LN2 = 0.6931471805599453
 VMEM_LIMIT = 40 * 1024 * 1024
+LANES = 128
 
 
 def diagonal():
-    return lax.broadcasted_iota(jnp.int32, (128, 128), 0) == lax.broadcasted_iota(
-        jnp.int32, (128, 128), 1
+    return lax.broadcasted_iota(jnp.int32, (LANES, LANES), 0) == lax.broadcasted_iota(
+        jnp.int32, (LANES, LANES), 1
     )
 
 
 def to_column(row):
-    return jnp.sum(
-        jnp.where(diagonal(), jnp.broadcast_to(row, (128, 128)), 0.0), axis=1, keepdims=True
-    )
+    spread = jnp.where(diagonal(), jnp.broadcast_to(row, (LANES, LANES)), 0.0)
+    return jnp.broadcast_to(jnp.sum(spread, axis=1, keepdims=True), (LANES, LANES))
 
 
 def to_row(column):
-    return jnp.sum(
-        jnp.where(diagonal(), jnp.broadcast_to(column, (128, 128)), 0.0), axis=0, keepdims=True
-    )
+    return jnp.sum(jnp.where(diagonal(), column, 0.0), axis=0, keepdims=True)
 
 
 def device_at(n, core, place):
@@ -48,15 +46,17 @@
     for copy in copies:
         copy.start()
     copies[0].wait()
-    for k in range(row_ref.shape[0] // 128):
-        part = slice(k * 128, (k + 1) * 128)
-        logw_ref[part, :] = to_column(row_ref[part].reshape(1, 128)) * LOG2E
+    for k in range(row_ref.shape[0] // LANES):
+        part = slice(k * LANES, (k + 1) * LANES)
+        logw_ref[part, :] = to_column(row_ref[part].reshape(1, LANES)) * LOG2E
     copies[1].wait()
     dlw = all_ref[...].reshape(1, all_ref.shape[0]) * LOG2E
     per = all_ref.shape[0] // n
     for core in range(2):
         owners = [device_at(n, core, place) for place in range(n // 2)]
-        dlw_ref[core] = jnp.concatenate([dlw[:, d * per : (d + 1) * per] for d in owners], axis=1)
+        mine = jnp.concatenate([dlw[:, d * per : (d + 1) * per] for d in owners], axis=1)
+        for j in range(dlw_ref.shape[1]):
+            dlw_ref[core, j : j + 1, :] = mine[:, j * LANES : (j + 1) * LANES]
     copies[2].wait()
     copies[3].wait()
 
@@ -81,76 +81,85 @@
     ) * (LOG2E / (STRENGTH * math.sqrt(width)))
 
 
+def chunks_of(ref):
+    return [ref[:, j * LANES : (j + 1) * LANES] for j in range(ref.shape[1] // LANES)]
+
+
+def over_lanes(reduce, parts):
+    whole = reduce(parts)
+    kind = jnp.max if reduce is largest else jnp.sum
+    return jnp.broadcast_to(kind(whole, axis=1, keepdims=True), whole.shape)
+
+
+def largest(parts):
+    return functools.reduce(jnp.maximum, parts)
+
+
+def total(parts):
+    return functools.reduce(jnp.add, parts)
+
+
 def near_kernel(e_ref, t_ref, s_ref, max_ref, tot_ref):
-    s = scores_of(e_ref, t_ref)
-    s_ref[...] = s
-    row_max = jnp.max(s, axis=1, keepdims=True)
+    s_ref[...] = scores_of(e_ref, t_ref)
+    parts = chunks_of(s_ref)
+    row_max = over_lanes(largest, parts)
     max_ref[...] = row_max
-    tot_ref[...] = jnp.sum(jnp.exp2(s - row_max), axis=1, keepdims=True)
-
-
-def column_sums(s, pot):
-    t = s + pot
-    top = jnp.max(t, axis=0, keepdims=True)
-    return top + jnp.log2(jnp.sum(jnp.exp2(t - top), axis=0, keepdims=True))
+    tot_ref[...] = over_lanes(total, [jnp.exp2(p - row_max) for p in parts])
+
+
+def column_sums(s_ref, pot, out_ref, where, less=None):
+    for j, part in enumerate(chunks_of(s_ref)):
+        terms = part + pot
+        top = jnp.max(terms, axis=0, keepdims=True)
+        lse = top + jnp.log2(jnp.sum(jnp.exp2(terms - top), axis=0, keepdims=True))
+        if less is not None:
+            lse = lse - less[where, j : j + 1, :]
+        out_ref[where, j : j + 1, :] = lse
 
 
 def far_kernel(n, e_ref, t_ref, near_ref, max_ref, tot_ref, logw_ref, far_ref, out_ref, half_ref):
     core = lax.rem(lax.axis_index("src"), 2)
-    s = scores_of(e_ref, t_ref)
-    far_ref[...] = s
+    far_ref[...] = scores_of(e_ref, t_ref)
+    parts = chunks_of(far_ref)
     near_max = max_ref[...]
-    row_max = jnp.maximum(near_max, jnp.max(s, axis=1, keepdims=True))
-    tot = tot_ref[...] * jnp.exp2(near_max - row_max) + jnp.sum(
-        jnp.exp2(s - row_max), axis=1, keepdims=True
+    row_max = jnp.maximum(near_max, over_lanes(largest, parts))
+    tot = tot_ref[...] * jnp.exp2(near_max - row_max) + over_lanes(
+        total, [jnp.exp2(p - row_max) for p in parts]
     )
     pot = logw_ref[...] - (row_max + jnp.log2(tot))
-    half_ref[core] = column_sums(near_ref[...], pot)
-    half_ref[1 - core] = column_sums(s, pot)
-    chunks = half_ref.shape[2] // 128
-    both = [half_ref[0], half_ref[1]]
-    tall = jnp.concatenate(
-        [v[:, j * 128 : (j + 1) * 128] for v in both for j in range(chunks)], axis=0
-    )
+    column_sums(near_ref, pot, half_ref, core)
+    column_sums(far_ref, pot, half_ref, 1 - core)
+    tall = half_ref[...].reshape(out_ref.shape[1:])
     for d in range(n):
         out_ref[d] = tall
 
 
 def second_kernel(n, near_ref, far_ref, g_ref, logw_ref, dlw_ref, src_ref, out_ref, half_ref):
     core = lax.rem(lax.axis_index("src"), 2)
-    half = near_ref.shape[1]
-    per = 2 * half // n
-    chunks = half // 128
+    per = 2 * near_ref.shape[1] // n
     g = g_ref[...]
     top = jnp.max(g, axis=0)
     lse = top + jnp.log2(jnp.sum(jnp.exp2(g - top[None]), axis=0))
-    for c in range(2):
-        half_ref[c] = dlw_ref[c] - jnp.concatenate(
-            [lse[c * chunks + j : c * chunks + j + 1, :] for j in range(chunks)], axis=1
-        )
-    near = near_ref[...] + half_ref[core]
-    far = far_ref[...] + half_ref[1 - core]
-    row_max = jnp.maximum(
-        jnp.max(near, axis=1, keepdims=True), jnp.max(far, axis=1, keepdims=True)
-    )
-    tot = jnp.sum(jnp.exp2(near - row_max), axis=1, keepdims=True) + jnp.sum(
-        jnp.exp2(far - row_max), axis=1, keepdims=True
-    )
+    half_ref[...] = dlw_ref[...] - lse.reshape(half_ref.shape)
+    parts = [p + half_ref[core, j : j + 1, :] for j, p in enumerate(chunks_of(near_ref))]
+    parts += [p + half_ref[1 - core, j : j + 1, :] for j, p in enumerate(chunks_of(far_ref))]
+    row_max = over_lanes(largest, parts)
+    tot = over_lanes(total, [jnp.exp2(p - row_max) for p in parts])
     pot = logw_ref[...] - (row_max + jnp.log2(tot))
     src_ref[...] = pot
-    half_ref[core] = column_sums(near_ref[...], pot) - dlw_ref[core]
-    half_ref[1 - core] = column_sums(far_ref[...], pot) - dlw_ref[1 - core]
+    column_sums(near_ref, pot, half_ref, core, dlw_ref)
+    column_sums(far_ref, pot, half_ref, 1 - core, dlw_ref)
     for c in range(2):
-        v = half_ref[c]
         for place in range(n // 2):
             d = device_at(n, c, place)
-            out_ref[d : d + 1, :] = v[:, place * per : (place + 1) * per]
+            row, lane = divmod(place * per, LANES)
+            out_ref[d : d + 1, :] = half_ref[c, row : row + 1, lane : lane + per]
 
 
 def last_kernel(g_ref, pot_ref, src_ref, own_ref):
-    for k in range(src_ref.shape[0] // 128):
-        part = slice(k * 128, (k + 1) * 128)
-        src_ref[part] = (to_row(pot_ref[part, :]) * LN2).reshape(128)
+    for k in range(src_ref.shape[0] // LANES):
+        part = slice(k * LANES, (k + 1) * LANES)
+        src_ref[part] = (to_row(pot_ref[part, :]) * LN2).reshape(LANES)
     g = g_ref[...]
     top = jnp.max(g, axis=0, keepdims=True)
     pot = -(top + jnp.log2(jnp.sum(jnp.exp2(g - top), axis=0, keepdims=True))) * LN2
@@ -183,8 +192,8 @@
         (
             shape(emitter_vectors.shape, emitter_vectors.dtype),
             shape(targets.shape, targets.dtype),
-            shape((rows, 1), f32),
-            shape((2, 1, half), f32),
+            shape((rows, LANES), f32),
+            shape((2, half // LANES, LANES), f32),
         ),
         [
             pltpu.with_memory_space_constraint(a, pltpu.HBM)
@@ -210,7 +219,7 @@
     far_targets = lax.ppermute(near_targets, "src", [(i, i ^ 1) for i in range(n)])
     near, near_max, near_tot = call(
         near_kernel,
-        (shape((rows, half), f32), shape((rows, 1), f32), shape((rows, 1), f32)),
+        (shape((rows, half), f32), shape((rows, LANES), f32), shape((rows, LANES), f32)),
         [emitter, near_targets],
         cost=pl.CostEstimate(
             flops=2 * rows * half * width,
@@ -220,16 +229,16 @@
     )
     far, sent = call(
         functools.partial(far_kernel, n),
-        (shape((rows, half), f32), shape((n, cols // 128, 128), f32)),
+        (shape((rows, half), f32), shape((n, cols // LANES, LANES), f32)),
         [emitter, far_targets, near, near_max, near_tot, logw],
-        [pltpu.VMEM((2, 1, half), f32)],
+        [pltpu.VMEM((2, half // LANES, LANES), f32)],
     )
     heard = lax.all_to_all(sent, "src", 0, 0)
     pot, parts = call(
         functools.partial(second_kernel, n),
-        (shape((rows, 1), f32), shape((n, per), f32)),
+        (shape((rows, LANES), f32), shape((n, per), f32)),
         [near, far, heard, logw, dlw],
-        [pltpu.VMEM((2, 1, half), f32)],
+        [pltpu.VMEM((2, half // LANES, LANES), f32)],
     )
     own = lax.all_to_all(parts, "src", 0, 0)
     return call(last_kernel, (shape((rows,), f32), shape((per,), f32)), [own, pot])

time: 42.3 us -> 41.1 us (0.972)
  Pallas kernels: 5.33 us -> 4.17 us
    pallas_call x6, Pallas kernels: 5.33 us -> 4.17 us  [call(): pl.pallas_call(kernel, out_shape=out_shape, in_specs=[pl.BlockSpec(memory...]
where the time goes in v4:
time: 41.1 us; the launch traced here: 40.9 us
  blocking collectives  29.5 us (72%)
  Pallas kernels  4.17 us (10%)
  starting transfers between devices  4.1 us (10%)
  waiting for transfers between devices  2.44 us (6%)
  between operations  0.65 us (2%)
    all_to_all x1, blocking collectives, local(): heard = lax.all_to_all(sent, 'src', 0, 0)  11.3 us
    all_to_all x1, blocking collectives, local(): lax.all_to_all(spread, 'src', 0, 0, axis_index_groups=quarter)  9.28 us
    all_to_all x1, blocking collectives, local(): own = lax.all_to_all(parts, 'src', 0, 0)  8.98 us
    pallas_call x6, Pallas kernels, call(): pl.pallas_call(kernel, out_shape=out_shape, in_specs=[pl.BlockSpec(memory...  4.17 us
    ppermute x1, starting transfers between devices, local(): lax.ppermute(targets, 'src', [(i, (i + n // 2) % n) for i in range(n)])  4.1 us
    ppermute x1, waiting for transfers between devices, local(): lax.ppermute(targets, 'src', [(i, (i + n // 2) % n) for i in range(n)])  1.41 us
    ppermute x1, waiting for transfers between devices, local(): lax.ppermute(near_targets, 'src', [(i, i ^ 1) for i in range(n)])  1.03 us
  transfers between devices with their start and end apart: 2, of which 2 were waited for; matrix products, arithmetic and copies ran while one was open for 0% of the time, Pallas kernels for 4%

profile of v4, /device:TPU:0, one launch (start us, length us, event | category | flops | bytes accessed | tf_op | source)
XLA Modules:
  0.0 40.9 jit_solution(2851052976060121344)
XLA Ops:
  0.6 4.1 %collective-permute-start = (bf16[64,256]{1,0:T(8,128)(2,1)}, bf16[64,256]{1,0:T(8,128)(2,1)S(1)}, u32[]{:S(2)}, u32[]{:S(2)}) collective-permute-start(bf16[64,256]{1,0:T(8,128)(2,1)} %t_hbm.1), channel_id=1, source_target_pairs={{0,8},{1,9},{2,10},{3,11},{4,12},{5,13},{6,14},{7,15},{8,0},{9,1},... | collective-permute-start | bytes 98312 | tf_op jit(solution)/shard_map/ppermute | solution.py:189
  4.7 1.0 %shard_map.59 = (bf16[512,256]{1,0:T(8,128)(2,1)S(1)}, bf16[64,256]{1,0:T(8,128)(2,1)S(1)}, f32[512,128]{1,0:T(8,128)S(1)}, f32[2,4,128]{2,1,0:T(4,128)S(1)}) custom-call(bf16[512,256]{1,0:T(8,128)(2,1)} %e_hbm.1, bf16[64,256]{1,0:T(8,128)(2,1)} %t_hbm.1, f32[512]{0:T(512)} %logw_hbm.1, f32[1024]{0:T(1024)} %dlw_hbm.1), custom_call_target="tpu_custom_call" | custom-call | bytes 524288 | tf_op jit(solution)/shard_map/pallas_call | solution.py:170
  5.8 1.4 %collective-permute-done.got_ref = bf16[64,256]{1,0:T(8,128)(2,1)S(1)} collective-permute-done((bf16[64,256]{1,0:T(8,128)(2,1)}, bf16[64,256]{1,0:T(8,128)(2,1)S(1)}, u32[]{:S(2)}, u32[]{:S(2)}) %collective-permute-start) | collective-permute-done | bytes 32800 | tf_op jit(solution)/shard_map/ppermute | solution.py:189
  7.2 9.3 %all_to_all.21.t_ref = bf16[4,128,256]{2,1,0:T(8,128)(2,1)S(1)} all-to-all(bf16[4,128,256]{2,1,0:T(8,128)(2,1)S(1)} %shard_map.60), channel_id=1, replica_groups={{0,2,4,6},{1,3,5,7},{8,10,12,14},{9,11,13,15},{16,18,20,22},{17,19,21,2..., dimensions={0} | all-to-all | bytes 524288 | tf_op jit(solution)/shard_map/all_to_all | solution.py:218
  16.5 0.0 collective-permute-start.1
  16.5 0.5 %shard_map.61 = (f32[512,512]{1,0:T(8,128)S(1)}, f32[512,128]{1,0:T(8,128)S(1)}, f32[512,128]{1,0:T(8,128)S(1)}) custom-call(bf16[512,256]{1,0:T(8,128)(2,1)S(1)} %get-tuple-element.13.e_ref, bf16[4,128,256]{2,1,0:T(8,128)(2,1)S(1)} %all_to_all.21.t_ref), custom_call_target="tpu_custom_call" | custom-call | flops 134217728 | bytes 1048576 | tf_op jit(solution)/shard_map/pallas_call | solution.py:170
  17.0 1.0 %collective-permute-done.1.t_ref = bf16[4,128,256]{2,1,0:T(8,128)(2,1)S(1)} collective-permute-done((bf16[4,128,256]{2,1,0:T(8,128)(2,1)S(1)}, bf16[4,128,256]{2,1,0:T(8,128)(2,1)S(1)}, u32[]{:S(2)}, u32[]{:S(2)}) %collective-permute-start.1) | collective-permute-done | bytes 262176 | tf_op jit(solution)/shard_map/ppermute | solution.py:219
  18.0 1.0 %shard_map.62 = (f32[512,512]{1,0:T(8,128)S(1)}, f32[16,8,128]{2,1,0:T(8,128)S(1)}) custom-call(bf16[512,256]{1,0:T(8,128)(2,1)S(1)} %get-tuple-element.13.e_ref, bf16[4,128,256]{2,1,0:T(8,128)(2,1)S(1)} %collective-permute-done.1.t_ref, f32[512,512]{1,0:T(8,128)S(1)} %get-tuple-element.15.near_ref, f32[512,128]{1,0:T(8,128)S(1)} %get-tuple-element.16.max_ref, ...), custom_call_target="tpu_custom_call" | custom-call | tf_op jit(solution)/shard_map/pallas_call | solution.py:170
  19.0 11.3 %all_to_all.22.g_ref = f32[16,8,128]{2,1,0:T(8,128)S(1)} all-to-all(f32[16,8,128]{2,1,0:T(8,128)S(1)} %get-tuple-element.20), channel_id=1, replica_groups=mesh['group'=2,'src'=16] {'src'}, dimensions={0} | all-to-all | bytes 131072 | tf_op jit(solution)/shard_map/all_to_all | solution.py:236
  30.3 1.0 %shard_map.63 = (f32[512,128]{1,0:T(8,128)S(1)}, f32[16,64]{1,0:T(8,128)S(1)}) custom-call(f32[512,512]{1,0:T(8,128)S(1)} %get-tuple-element.15.near_ref, f32[512,512]{1,0:T(8,128)S(1)} %get-tuple-element.19.far_ref, f32[16,8,128]{2,1,0:T(8,128)S(1)} %all_to_all.22.g_ref, f32[512,128]{1,0:T(8,128)S(1)} %get-tuple-element.18.logw_ref, ...), custom_call_target="tpu_custom_call" | custom-call | tf_op jit(solution)/shard_map/pallas_call | solution.py:170
  31.3 9.0 %all_to_all.23 = f32[16,1,64]{2,1,0:T(1,128)S(1)} all-to-all(f32[16,1,64]{2,1,0:T(1,128)S(1)} %bitcast.5), channel_id=1, replica_groups=mesh['group'=2,'src'=16] {'src'}, dimensions={0} | all-to-all | bytes 8192 | tf_op jit(solution)/shard_map/all_to_all | solution.py:243
  40.3 0.6 %shard_map.64 = (f32[512]{0:T(512)}, f32[64]{0:T(128)}) custom-call(f32[16,64]{1,0:T(8,128)S(1)} %bitcast.4, f32[512,128]{1,0:T(8,128)S(1)} %get-tuple-element.23.pot_ref), custom_call_target="tpu_custom_call" | custom-call | tf_op jit(solution)/shard_map/pallas_call | solution.py:170
  (1 shorter events, 0.0 us)
Async XLA Ops:
  0.6 6.6 %collective-permute-start = (bf16[64,256]{1,0:T(8,128)(2,1)}, bf16[64,256]{1,0:T(8,128)(2,1)S(1)}, u32[]{:S(2)}, u32[]{:S(2)}) collective-permute-start(bf16[64,256]{1,0:T(8,128)(2,1)} %t_hbm.1), channel_id=1, source_target_pairs={{0,8},{1,9},{2,10},{3,11},{4,12},{5,13},{6,14},{7,15},{8,0},{9,1},... | collective-permute-start | bytes 98312 | tf_op jit(solution)/shard_map/ppermute | solution.py:189
  16.5 1.5 %collective-permute-start.1 = (bf16[4,128,256]{2,1,0:T(8,128)(2,1)S(1)}, bf16[4,128,256]{2,1,0:T(8,128)(2,1)S(1)}, u32[]{:S(2)}, u32[]{:S(2)}) collective-permute-start(bf16[4,128,256]{2,1,0:T(8,128)(2,1)S(1)} %all_to_all.21.t_ref), channel_id=1, source_target_pairs={{0,1},{1,0},{2,3},{3,2},{4,5},{5,4},{6,7},{7,6},{8,9},{9,8},{10,11... | collective-permute-start | bytes 786440 | tf_op jit(solution)/shard_map/ppermute | solution.py:219

commit v5 on v4

v5 whole, which is shorter than its diff:
```python
import functools
import math

import jax
import jax.numpy as jnp
from jax import lax
from jax.experimental import pallas as pl
from jax.experimental.pallas import tpu as pltpu
from jax.sharding import PartitionSpec as P

STRENGTH = 0.5
LOG2E = 1.4426950408889634
LN2 = 0.6931471805599453
VMEM_LIMIT = 40 * 1024 * 1024
LANES = 128


def diagonal():
    return lax.broadcasted_iota(jnp.int32, (LANES, LANES), 0) == lax.broadcasted_iota(
        jnp.int32, (LANES, LANES), 1
    )


def to_column(row):
    spread = jnp.where(diagonal(), jnp.broadcast_to(row, (LANES, LANES)), 0.0)
    return jnp.broadcast_to(jnp.sum(spread, axis=1, keepdims=True), (LANES, LANES))


def to_row(column):
    return jnp.sum(jnp.where(diagonal(), column, 0.0), axis=0, keepdims=True)


def device_at(n, half, place):
    return (place % 2) * (n // 2) + (place // 2) * 2 + half


def rows_of(n, places, per_piece):
    me = lax.axis_index("src")
    core, quarter = lax.rem(me, 2), lax.rem(me, n // 2) // 2
    return [
        (jnp.bitwise_xor(core, other) * (n // 4) + jnp.bitwise_xor(quarter, away)) * per_piece + k
        for away, other in places
        for k in range(per_piece)
    ]


def load_kernel(
    n, e_hbm, t_hbm, logw_hbm, dlw_hbm, e_ref, t_ref, logw_ref, dlw_ref, row_ref, all_ref, sems
):
    copies = [
        pltpu.make_async_copy(logw_hbm, row_ref, sems.at[0]),
        pltpu.make_async_copy(dlw_hbm, all_ref, sems.at[1]),
        pltpu.make_async_copy(t_hbm, t_ref, sems.at[2]),
        pltpu.make_async_copy(e_hbm, e_ref, sems.at[3]),
    ]
    for copy in copies:
        copy.start()
    copies[0].wait()
    for k in range(row_ref.shape[0] // LANES):
        part = slice(k * LANES, (k + 1) * LANES)
        logw_ref[part, :] = to_column(row_ref[part].reshape(1, LANES)) * LOG2E
    copies[1].wait()
    dlw = all_ref[...].reshape(1, all_ref.shape[0]) * LOG2E
    per = all_ref.shape[0] // n
    owners = [device_at(n, half, place) for half in range(2) for place in range(n // 2)]
    row = jnp.concatenate([dlw[:, d * per : (d + 1) * per] for d in owners], axis=1)
    for j in range(dlw_ref.shape[0]):
        dlw_ref[j : j + 1, :] = row[:, j * LANES : (j + 1) * LANES]
    copies[2].wait()
    copies[3].wait()


def pair_kernel(n, t_ref, got_ref, out_ref):
    per = t_ref.shape[0]
    upper = lax.axis_index("src") // (n // 2)
    out_ref[pl.ds(pl.multiple_of(upper * per, per), per), :] = t_ref[...]
    out_ref[pl.ds(pl.multiple_of((1 - upper) * per, per), per), :] = got_ref[...]


def scores_of(e_ref, pieces, s_ref):
    width = e_ref.shape[1]
    t = jnp.concatenate([piece[...] for piece in pieces], axis=0)
    s_ref[...] = lax.dot_general(
        e_ref[...], t, (((1,), (1,)), ((), ())), preferred_element_type=jnp.float32
    ) * (LOG2E / (STRENGTH * math.sqrt(width)))


def chunks_of(ref):
    return [ref[:, j * LANES : (j + 1) * LANES] for j in range(ref.shape[1] // LANES)]


def over_lanes(reduce, parts):
    whole = reduce(parts)
    kind = jnp.max if reduce is largest else jnp.sum
    return jnp.broadcast_to(kind(whole, axis=1, keepdims=True), whole.shape)


def largest(parts):
    return functools.reduce(jnp.maximum, parts)


def total(parts):
    return functools.reduce(jnp.add, parts)


def row_sums(parts, before=None):
    row_max = over_lanes(largest, parts)
    if before is not None:
        old_max, old_tot = before[0][...], before[1][...]
        row_max = jnp.maximum(row_max, old_max)
    tot = over_lanes(total, [jnp.exp2(p - row_max) for p in parts])
    if before is not None:
        tot = tot + old_tot * jnp.exp2(old_max - row_max)
    return row_max, tot


def part_kernel(count, more, e_ref, *refs):
    pieces, rest = refs[:count], refs[count:]
    before, (s_ref, max_ref, tot_ref) = (rest[:2], rest[2:]) if more else (None, rest)
    scores_of(e_ref, pieces, s_ref)
    max_ref[...], tot_ref[...] = row_sums(chunks_of(s_ref), before)


def column_sums(scores, places, pot, out_ref, less=None):
    parts = [part for s_ref in scores for part in chunks_of(s_ref)]
    for part, row in zip(parts, places):
        terms = part + pot
        top = jnp.max(terms, axis=0, keepdims=True)
        lse = top + jnp.log2(jnp.sum(jnp.exp2(terms - top), axis=0, keepdims=True))
        at = pl.ds(row, 1)
        out_ref[at, :] = lse if less is None else lse - less[at, :]


def final_kernel(n, places, per_piece, e_ref, t_ref, max_ref, tot_ref, logw_ref, *refs):
    done, (s_ref, out_ref, cols_ref) = refs[:-3], refs[-3:]
    scores_of(e_ref, [t_ref], s_ref)
    row_max, tot = row_sums(chunks_of(s_ref), (max_ref, tot_ref))
    pot = logw_ref[...] - (row_max + jnp.log2(tot))
    column_sums(done + (s_ref,), rows_of(n, places, per_piece), pot, cols_ref)
    tall = cols_ref[...]
    for d in range(n):
        out_ref[d] = tall


def second_kernel(n, places, per_piece, g_ref, logw_ref, dlw_ref, *refs):
    scores, (src_ref, out_ref, cols_ref) = refs[:-3], refs[-3:]
    per = dlw_ref.shape[0] * LANES // n
    g = g_ref[...]
    top = jnp.max(g, axis=0)
    cols_ref[...] = dlw_ref[...] - (top + jnp.log2(jnp.sum(jnp.exp2(g - top[None]), axis=0)))
    rows = rows_of(n, places, per_piece)
    parts = [part for s_ref in scores for part in chunks_of(s_ref)]
    row_max, tot = row_sums([p + cols_ref[pl.ds(row, 1), :] for p, row in zip(parts, rows)])
    pot = logw_ref[...] - (row_max + jnp.log2(tot))
    src_ref[...] = pot
    column_sums(scores, rows, pot, cols_ref, dlw_ref)
    for half in range(2):
        for place in range(n // 2):
            d = device_at(n, half, place)
            row, lane = divmod((half * (n // 2) + place) * per, LANES)
            out_ref[d : d + 1, :] = cols_ref[row : row + 1, lane : lane + per]


def last_kernel(g_ref, pot_ref, src_ref, own_ref):
    for k in range(src_ref.shape[0] // LANES):
        part = slice(k * LANES, (k + 1) * LANES)
        src_ref[part] = (to_row(pot_ref[part, :]) * LN2).reshape(LANES)
    g = g_ref[...]
    top = jnp.max(g, axis=0, keepdims=True)
    pot = -(top + jnp.log2(jnp.sum(jnp.exp2(g - top), axis=0, keepdims=True))) * LN2
    own_ref[...] = pot.reshape(own_ref.shape)


def call(kernel, out_shape, operands, scratch=(), space=pltpu.VMEM, cost=None):
    return pl.pallas_call(
        kernel,
        out_shape=out_shape,
        in_specs=[pl.BlockSpec(memory_space=space)] * len(operands),
        out_specs=jax.tree.map(lambda _: pl.BlockSpec(memory_space=pltpu.VMEM), out_shape),
        scratch_shapes=list(scratch),
        compiler_params=pltpu.CompilerParams(vmem_limit_bytes=VMEM_LIMIT),
        cost_estimate=cost,
    )(*operands)


def local(emitter_vectors, targets, src_logw, dst_logw):
    n = lax.axis_size("src")
    rows, width = emitter_vectors.shape
    per = targets.shape[0]
    cols = dst_logw.shape[0]
    f32 = jnp.float32
    shape = jax.ShapeDtypeStruct

    def swap(a, distance):
        return lax.ppermute(a, "src", [(i, i ^ distance) for i in range(n)])

    partner = swap(targets, n // 2)
    emitter, own_targets, logw, dlw = call(
        functools.partial(load_kernel, n),
        (
            shape(emitter_vectors.shape, emitter_vectors.dtype),
            shape(targets.shape, targets.dtype),
            shape((rows, LANES), f32),
            shape((cols // LANES, LANES), f32),
        ),
        [
            pltpu.with_memory_space_constraint(a, pltpu.HBM)
            for a in (emitter_vectors, targets, src_logw, dst_logw)
        ],
        [
            pltpu.VMEM(src_logw.shape, f32),
            pltpu.VMEM(dst_logw.shape, f32),
            pltpu.SemaphoreType.DMA((4,)),
        ],
        pltpu.HBM,
        pl.CostEstimate(flops=0, bytes_accessed=4 * rows * width, transcendentals=0),
    )
    piece = 2 * per
    (pair,) = call(
        functools.partial(pair_kernel, n),
        (shape((piece, width), targets.dtype),),
        [own_targets, partner],
    )
    aways = list(range(n // 4 - 1, 0, -1))
    early, late = aways[:-1], aways[-1]
    other_pair = swap(pair, 1)
    near = {away: swap(pair, 2 * away) for away in aways}
    far = {away: swap(near[away], 1) for away in aways}

    def part(pieces, before):
        count = len(pieces)
        return call(
            functools.partial(part_kernel, count, bool(before)),
            (shape((rows, count * piece), f32), shape((rows, LANES), f32), shape((rows, LANES), f32)),
            [emitter] + pieces + list(before),
            cost=pl.CostEstimate(
                flops=2 * rows * count * piece * width,
                bytes_accessed=rows * count * piece * 4,
                transcendentals=rows * count * piece,
            ),
        )

    scores_a, *sums = part([pair, other_pair], ())
    scores_b, *sums = part([near[away] for away in early], sums)
    scores_c, *sums = part([near[late]] + [far[away] for away in early], sums)
    places = [(0, 0), (0, 1)] + [(away, 0) for away in early]
    places += [(late, 0)] + [(away, 1) for away in early] + [(late, 1)]
    per_piece = piece // LANES
    scores_d, sent = call(
        functools.partial(final_kernel, n, places, per_piece),
        (shape((rows, piece), f32), shape((n, cols // LANES, LANES), f32)),
        [emitter, far[late], *sums, logw, scores_a, scores_b, scores_c],
        [pltpu.VMEM((cols // LANES, LANES), f32)],
    )
    heard = lax.all_to_all(sent, "src", 0, 0)
    pot, parts = call(
        functools.partial(second_kernel, n, places, per_piece),
        (shape((rows, LANES), f32), shape((n, per), f32)),
        [heard, logw, dlw, scores_a, scores_b, scores_c, scores_d],
        [pltpu.VMEM((cols // LANES, LANES), f32)],
    )
    own = lax.all_to_all(parts, "src", 0, 0)
    return call(last_kernel, (shape((rows,), f32), shape((per,), f32)), [own, pot])


def solution(mesh):
    return jax.shard_map(
        local,
        mesh=mesh,
        in_specs=(
            P(("group", "src"), None),
            P(("group", "src"), None),
            P(("group", "src")),
            P("group"),
        ),
        out_specs=(P(("group", "src")), P(("group", "src"))),
        check_vma=False,
    )
```

time: 41.1 us -> 39.6 us (0.964)
  blocking collectives: 29.5 us -> 20.8 us
  starting transfers between devices: 4.1 us -> 7.67 us
  waiting for transfers between devices: 2.44 us -> 5.35 us
  Pallas kernels: 4.17 us -> 4.84 us
    all_to_all x1 -> x0, blocking collectives: 9.28 us -> none  [local(): lax.all_to_all(spread, 'src', 0, 0, axis_index_groups=quarter)]
    ppermute x2 -> x8, starting transfers between devices: 4.1 us -> 7.67 us  [swap(): return lax.ppermute(a, 'src', [(i, i ^ distance) for i in range(n)])]
    ppermute x2 -> x8, waiting for transfers between devices: 2.44 us -> 5.35 us  [swap(): return lax.ppermute(a, 'src', [(i, i ^ distance) for i in range(n)])]
    pallas_call x6 -> x8, Pallas kernels: 4.17 us -> 4.84 us  [call(): pl.pallas_call(kernel, out_shape=out_shape, in_specs=[pl.BlockSpec(memory...]
    all_to_all x1, blocking collectives: 11.3 us -> 11.8 us  [local(): heard = lax.all_to_all(sent, 'src', 0, 0)]
  transfers between devices with their start and end apart: 2 -> 8, of which waited for: 2 -> 4; matrix products, arithmetic and copies ran while one was open for 0% -> 0% of each run, Pallas kernels for 4% -> 6%
where the time goes in v5:
time: 39.6 us; the launch traced here: 39.3 us
  blocking collectives  20.8 us (53%)
  starting transfers between devices  7.67 us (19%)
  waiting for transfers between devices  5.35 us (14%)
  Pallas kernels  4.84 us (12%)
  between operations  0.69 us (2%)
    all_to_all x1, blocking collectives, local(): heard = lax.all_to_all(sent, 'src', 0, 0)  11.8 us
    all_to_all x1, blocking collectives, local(): own = lax.all_to_all(parts, 'src', 0, 0)  8.98 us
    ppermute x8, starting transfers between devices, swap(): return lax.ppermute(a, 'src', [(i, i ^ distance) for i in range(n)])  7.67 us
    ppermute x8, waiting for transfers between devices, swap(): return lax.ppermute(a, 'src', [(i, i ^ distance) for i in range(n)])  5.35 us
    pallas_call x8, Pallas kernels, call(): pl.pallas_call(kernel, out_shape=out_shape, in_specs=[pl.BlockSpec(memory...  4.84 us
  transfers between devices with their start and end apart: 8, of which 4 were waited for; matrix products, arithmetic and copies ran while one was open for 0% of the time, Pallas kernels for 6%

profile of v5, /device:TPU:0, one launch (start us, length us, event | category | flops | bytes accessed | tf_op | source)
XLA Modules:
  0.0 39.3 jit_solution(14017862419505458923)
XLA Ops:
  0.6 4.1 %collective-permute-start = (bf16[64,256]{1,0:T(8,128)(2,1)}, bf16[64,256]{1,0:T(8,128)(2,1)S(1)}, u32[]{:S(2)}, u32[]{:S(2)}) collective-permute-start(bf16[64,256]{1,0:T(8,128)(2,1)} %t_hbm.1), channel_id=1, source_target_pairs={{0,8},{1,9},{2,10},{3,11},{4,12},{5,13},{6,14},{7,15},{8,0},{9,1},... | collective-permute-start | bytes 98312 | tf_op jit(solution)/shard_map/ppermute | solution.py:195
  4.7 1.0 %shard_map.59 = (bf16[512,256]{1,0:T(8,128)(2,1)S(1)}, bf16[64,256]{1,0:T(8,128)(2,1)S(1)}, f32[512,128]{1,0:T(8,128)S(1)}, f32[8,128]{1,0:T(8,128)S(1)}) custom-call(bf16[512,256]{1,0:T(8,128)(2,1)} %e_hbm.1, bf16[64,256]{1,0:T(8,128)(2,1)} %t_hbm.1, f32[512]{0:T(512)} %logw_hbm.1, f32[1024]{0:T(1024)} %dlw_hbm.1), custom_call_target="tpu_custom_call" | custom-call | bytes 524288 | tf_op jit(solution)/shard_map/pallas_call | solution.py:175
  5.8 1.4 %collective-permute-done.got_ref = bf16[64,256]{1,0:T(8,128)(2,1)S(1)} collective-permute-done((bf16[64,256]{1,0:T(8,128)(2,1)}, bf16[64,256]{1,0:T(8,128)(2,1)S(1)}, u32[]{:S(2)}, u32[]{:S(2)}) %collective-permute-start) | collective-permute-done | bytes 32800 | tf_op jit(solution)/shard_map/ppermute | solution.py:195
  7.2 2.5 %collective-permute-start.3 = (bf16[128,256]{1,0:T(8,128)(2,1)S(1)}, bf16[128,256]{1,0:T(8,128)(2,1)S(1)}, u32[]{:S(2)}, u32[]{:S(2)}) collective-permute-start(bf16[128,256]{1,0:T(8,128)(2,1)S(1)} %shard_map.60.refs_0_), channel_id=1, source_target_pairs={{0,6},{1,7},{2,4},{3,5},{4,2},{5,3},{6,0},{7,1},{8,14},{9,15},{10,... | collective-permute-start | bytes 196616 | tf_op jit(solution)/shard_map/ppermute | solution.py:195
  9.7 0.7 %collective-permute-start.5 = (bf16[128,256]{1,0:T(8,128)(2,1)S(1)}, bf16[128,256]{1,0:T(8,128)(2,1)S(1)}, u32[]{:S(2)}, u32[]{:S(2)}) collective-permute-start(bf16[128,256]{1,0:T(8,128)(2,1)S(1)} %shard_map.60.refs_0_), channel_id=1, source_target_pairs={{0,4},{1,5},{2,6},{3,7},{4,0},{5,1},{6,2},{7,3},{8,12},{9,13},{10,... | collective-permute-start | bytes 196616 | tf_op jit(solution)/shard_map/ppermute | solution.py:195
  10.4 0.3 collective-permute-start.1
  10.8 0.0 collective-permute-start.7
  10.8 1.7 %collective-permute-done.3.refs_0_ = bf16[128,256]{1,0:T(8,128)(2,1)S(1)} collective-permute-done((bf16[128,256]{1,0:T(8,128)(2,1)S(1)}, bf16[128,256]{1,0:T(8,128)(2,1)S(1)}, u32[]{:S(2)}, u32[]{:S(2)}) %collective-permute-start.3) | collective-permute-done | bytes 65568 | tf_op jit(solution)/shard_map/ppermute | solution.py:195
  12.4 0.0 collective-permute-start.4
  12.4 1.6 %collective-permute-done.5.refs_1_ = bf16[128,256]{1,0:T(8,128)(2,1)S(1)} collective-permute-done((bf16[128,256]{1,0:T(8,128)(2,1)S(1)}, bf16[128,256]{1,0:T(8,128)(2,1)S(1)}, u32[]{:S(2)}, u32[]{:S(2)}) %collective-permute-start.5) | collective-permute-done | bytes 65568 | tf_op jit(solution)/shard_map/ppermute | solution.py:195
  14.0 0.0 collective-permute-start.6
  14.0 0.7 %collective-permute-done.1.refs_0_ = bf16[128,256]{1,0:T(8,128)(2,1)S(1)} collective-permute-done((bf16[128,256]{1,0:T(8,128)(2,1)S(1)}, bf16[128,256]{1,0:T(8,128)(2,1)S(1)}, u32[]{:S(2)}, u32[]{:S(2)}) %collective-permute-start.1) | collective-permute-done | bytes 65568 | tf_op jit(solution)/shard_map/ppermute | solution.py:195
  14.7 0.0 collective-permute-start.2
  14.7 0.0 collective-permute-done.7.refs_1_
  14.7 0.4 %shard_map.61 = (f32[512,256]{1,0:T(8,128)S(1)}, f32[512,128]{1,0:T(8,128)S(1)}, f32[512,128]{1,0:T(8,128)S(1)}) custom-call(bf16[512,256]{1,0:T(8,128)(2,1)S(1)} %get-tuple-element.19.e_ref, bf16[128,256]{1,0:T(8,128)(2,1)S(1)} %shard_map.60.refs_0_, bf16[128,256]{1,0:T(8,128)(2,1)S(1)} %collective-permute-done.7.refs_1_), custom_call_target="tpu_custom_call" | custom-call | flops 67108864 | bytes 524288 | tf_op jit(solution)/shard_map/pallas_call | solution.py:175
  15.1 0.5 %shard_map.62 = (f32[512,256]{1,0:T(8,128)S(1)}, f32[512,128]{1,0:T(8,128)S(1)}, f32[512,128]{1,0:T(8,128)S(1)}) custom-call(bf16[512,256]{1,0:T(8,128)(2,1)S(1)} %get-tuple-element.19.e_ref, bf16[128,256]{1,0:T(8,128)(2,1)S(1)} %collective-permute-done.3.refs_0_, bf16[128,256]{1,0:T(8,128)(2,1)S(1)} %collective-permute-done.5.refs_1_, ...), custom_call_target="tpu_custom_call" | custom-call | flops 67108864 | bytes 524288 | tf_op jit(solution)/shard_map/pallas_call | solution.py:175
  15.6 0.0 collective-permute-done.4.refs_1_
  15.6 0.0 collective-permute-done.6.refs_2_
  15.6 0.5 %shard_map.63 = (f32[512,384]{1,0:T(8,128)S(1)}, f32[512,128]{1,0:T(8,128)S(1)}, f32[512,128]{1,0:T(8,128)S(1)}) custom-call(bf16[512,256]{1,0:T(8,128)(2,1)S(1)} %get-tuple-element.19.e_ref, bf16[128,256]{1,0:T(8,128)(2,1)S(1)} %collective-permute-done.1.refs_0_, bf16[128,256]{1,0:T(8,128)(2,1)S(1)} %collective-permute-done.4.refs_1_, ...), custom_call_target="tpu_custom_call" | custom-call | flops 100663296 | bytes 786432 | tf_op jit(solution)/shard_map/pallas_call | solution.py:175
  16.1 0.0 collective-permute-done.2.t_ref
  16.1 0.8 %shard_map.64 = (f32[512,128]{1,0:T(8,128)S(1)}, f32[16,8,128]{2,1,0:T(8,128)S(1)}) custom-call(bf16[512,256]{1,0:T(8,128)(2,1)S(1)} %get-tuple-element.19.e_ref, bf16[128,256]{1,0:T(8,128)(2,1)S(1)} %collective-permute-done.2.t_ref, f32[512,128]{1,0:T(8,128)S(1)} %get-tuple-element.25.max_ref, f32[512,128]{1,0:T(8,128)S(1)} %get-tuple-element.26.tot_ref, ...), custom_call_target="tpu_custom_call" | custom-call | tf_op jit(solution)/shard_map/pallas_call | solution.py:175
  16.9 11.8 %all_to_all.16.g_ref = f32[16,8,128]{2,1,0:T(8,128)S(1)} all-to-all(f32[16,8,128]{2,1,0:T(8,128)S(1)} %get-tuple-element.31), channel_id=1, replica_groups=mesh['group'=2,'src'=16] {'src'}, dimensions={0} | all-to-all | bytes 131072 | tf_op jit(solution)/shard_map/all_to_all | solution.py:255
  28.7 1.0 %shard_map.65 = (f32[512,128]{1,0:T(8,128)S(1)}, f32[16,64]{1,0:T(8,128)S(1)}) custom-call(f32[16,8,128]{2,1,0:T(8,128)S(1)} %all_to_all.16.g_ref, f32[512,128]{1,0:T(8,128)S(1)} %get-tuple-element.27.logw_ref, f32[8,128]{1,0:T(8,128)S(1)} %get-tuple-element.32.dlw_ref, f32[512,256]{1,0:T(8,128)S(1)} %get-tuple-element.28.refs_0_, ...), custom_call_target="tpu_custom_call" | custom-call | tf_op jit(solution)/shard_map/pallas_call | solution.py:175
  29.7 9.0 %all_to_all.17 = f32[16,1,64]{2,1,0:T(1,128)S(1)} all-to-all(f32[16,1,64]{2,1,0:T(1,128)S(1)} %bitcast.5), channel_id=1, replica_groups=mesh['group'=2,'src'=16] {'src'}, dimensions={0} | all-to-all | bytes 8192 | tf_op jit(solution)/shard_map/all_to_all | solution.py:262
  38.7 0.6 %shard_map.66 = (f32[512]{0:T(512)}, f32[64]{0:T(128)}) custom-call(f32[16,64]{1,0:T(8,128)S(1)} %bitcast.4, f32[512,128]{1,0:T(8,128)S(1)} %get-tuple-element.35.pot_ref), custom_call_target="tpu_custom_call" | custom-call | tf_op jit(solution)/shard_map/pallas_call | solution.py:175
  (1 shorter events, 0.0 us)
Async XLA Ops:
  0.6 6.6 %collective-permute-start = (bf16[64,256]{1,0:T(8,128)(2,1)}, bf16[64,256]{1,0:T(8,128)(2,1)S(1)}, u32[]{:S(2)}, u32[]{:S(2)}) collective-permute-start(bf16[64,256]{1,0:T(8,128)(2,1)} %t_hbm.1), channel_id=1, source_target_pairs={{0,8},{1,9},{2,10},{3,11},{4,12},{5,13},{6,14},{7,15},{8,0},{9,1},... | collective-permute-start | bytes 98312 | tf_op jit(solution)/shard_map/ppermute | solution.py:195
  7.2 5.2 %collective-permute-start.3 = (bf16[128,256]{1,0:T(8,128)(2,1)S(1)}, bf16[128,256]{1,0:T(8,128)(2,1)S(1)}, u32[]{:S(2)}, u32[]{:S(2)}) collective-permute-start(bf16[128,256]{1,0:T(8,128)(2,1)S(1)} %shard_map.60.refs_0_), channel_id=1, source_target_pairs={{0,6},{1,7},{2,4},{3,5},{4,2},{5,3},{6,0},{7,1},{8,14},{9,15},{10,... | collective-permute-start | bytes 196616 | tf_op jit(solution)/shard_map/ppermute | solution.py:195
  9.7 4.3 %collective-permute-start.5 = (bf16[128,256]{1,0:T(8,128)(2,1)S(1)}, bf16[128,256]{1,0:T(8,128)(2,1)S(1)}, u32[]{:S(2)}, u32[]{:S(2)}) collective-permute-start(bf16[128,256]{1,0:T(8,128)(2,1)S(1)} %shard_map.60.refs_0_), channel_id=1, source_target_pairs={{0,4},{1,5},{2,6},{3,7},{4,0},{5,1},{6,2},{7,3},{8,12},{9,13},{10,... | collective-permute-start | bytes 196616 | tf_op jit(solution)/shard_map/ppermute | solution.py:195
  10.4 4.3 %collective-permute-start.1 = (bf16[128,256]{1,0:T(8,128)(2,1)S(1)}, bf16[128,256]{1,0:T(8,128)(2,1)S(1)}, u32[]{:S(2)}, u32[]{:S(2)}) collective-permute-start(bf16[128,256]{1,0:T(8,128)(2,1)S(1)} %shard_map.60.refs_0_), channel_id=1, source_target_pairs={{0,2},{1,3},{2,0},{3,1},{4,6},{5,7},{6,4},{7,5},{8,10},{9,11},{10,... | collective-permute-start | bytes 196616 | tf_op jit(solution)/shard_map/ppermute | solution.py:195
  10.8 3.9 %collective-permute-start.7 = (bf16[128,256]{1,0:T(8,128)(2,1)S(1)}, bf16[128,256]{1,0:T(8,128)(2,1)S(1)}, u32[]{:S(2)}, u32[]{:S(2)}) collective-permute-start(bf16[128,256]{1,0:T(8,128)(2,1)S(1)} %shard_map.60.refs_0_), channel_id=1, source_target_pairs={{0,1},{1,0},{2,3},{3,2},{4,5},{5,4},{6,7},{7,6},{8,9},{9,8},{10,11... | collective-permute-start | bytes 196616 | tf_op jit(solution)/shard_map/ppermute | solution.py:195
  12.4 3.2 %collective-permute-start.4 = (bf16[128,256]{1,0:T(8,128)(2,1)S(1)}, bf16[128,256]{1,0:T(8,128)(2,1)S(1)}, u32[]{:S(2)}, u32[]{:S(2)}) collective-permute-start(bf16[128,256]{1,0:T(8,128)(2,1)S(1)} %collective-permute-done.3.refs_0_), channel_id=1, source_target_pairs={{0,1},{1,0},{2,3},{3,2},{4,5},{5,4},{6,7},{7,6},{8,9},{9,8},{10,11... | collective-permute-start | bytes 196616 | tf_op jit(solution)/shard_map/ppermute | solution.py:195
  14.0 1.6 %collective-permute-start.6 = (bf16[128,256]{1,0:T(8,128)(2,1)S(1)}, bf16[128,256]{1,0:T(8,128)(2,1)S(1)}, u32[]{:S(2)}, u32[]{:S(2)}) collective-permute-start(bf16[128,256]{1,0:T(8,128)(2,1)S(1)} %collective-permute-done.5.refs_1_), channel_id=1, source_target_pairs={{0,1},{1,0},{2,3},{3,2},{4,5},{5,4},{6,7},{7,6},{8,9},{9,8},{10,11... | collective-permute-start | bytes 196616 | tf_op jit(solution)/shard_map/ppermute | solution.py:195
  14.7 1.4 %collective-permute-start.2 = (bf16[128,256]{1,0:T(8,128)(2,1)S(1)}, bf16[128,256]{1,0:T(8,128)(2,1)S(1)}, u32[]{:S(2)}, u32[]{:S(2)}) collective-permute-start(bf16[128,256]{1,0:T(8,128)(2,1)S(1)} %collective-permute-done.1.refs_0_), channel_id=1, source_target_pairs={{0,1},{1,0},{2,3},{3,2},{4,5},{5,4},{6,7},{7,6},{8,9},{9,8},{10,11... | collective-permute-start | bytes 196616 | tf_op jit(solution)/shard_map/ppermute | solution.py:195

commit v6 on v5

--- a/solution.py
+++ b/solution.py
@@ -30,17 +30,24 @@
     return jnp.sum(jnp.where(diagonal(), column, 0.0), axis=0, keepdims=True)
 
 
-def device_at(n, half, place):
-    return (place % 2) * (n // 2) + (place // 2) * 2 + half
-
-
-def rows_of(n, places, per_piece):
+def device_at(n, place):
+    quarter = n // 4
+    core, upper = place // (2 * quarter), place // quarter % 2
+    chip = upper * (n // 4) + place % quarter
+    return chip * 2 + (core + bin(chip).count("1")) % 2
+
+
+def rows_of(n, per_group, groups):
     me = lax.axis_index("src")
-    core, quarter = lax.rem(me, 2), lax.rem(me, n // 2) // 2
+    upper = me // (n // 2)
+    core = me
+    for k in range(1, n.bit_length() - 1):
+        core = core + me // 2**k
+    core = lax.rem(core, 2)
     return [
-        (jnp.bitwise_xor(core, other) * (n // 4) + jnp.bitwise_xor(quarter, away)) * per_piece + k
-        for away, other in places
-        for k in range(per_piece)
+        (jnp.bitwise_xor(core, over) * 2 + jnp.bitwise_xor(upper, across)) * per_group + k
+        for over, across in groups
+        for k in range(per_group)
     ]
 
 
@@ -62,7 +69,7 @@
     copies[1].wait()
     dlw = all_ref[...].reshape(1, all_ref.shape[0]) * LOG2E
     per = all_ref.shape[0] // n
-    owners = [device_at(n, half, place) for half in range(2) for place in range(n // 2)]
+    owners = [device_at(n, place) for place in range(n)]
     row = jnp.concatenate([dlw[:, d * per : (d + 1) * per] for d in owners], axis=1)
     for j in range(dlw_ref.shape[0]):
         dlw_ref[j : j + 1, :] = row[:, j * LANES : (j + 1) * LANES]
@@ -70,18 +77,19 @@
     copies[3].wait()
 
 
-def pair_kernel(n, t_ref, got_ref, out_ref):
-    per = t_ref.shape[0]
-    upper = lax.axis_index("src") // (n // 2)
-    out_ref[pl.ds(pl.multiple_of(upper * per, per), per), :] = t_ref[...]
-    out_ref[pl.ds(pl.multiple_of((1 - upper) * per, per), per), :] = got_ref[...]
-
-
-def scores_of(e_ref, pieces, s_ref):
+def group_kernel(n, aways, *refs):
+    out_ref = refs[-1]
+    mine = lax.rem(lax.axis_index("src"), n // 2) // 2
+    for away, ref in zip(aways, refs[:-1]):
+        per = ref.shape[0]
+        at = pl.multiple_of(jnp.bitwise_xor(mine, away) * per, per)
+        out_ref[pl.ds(at, per), :] = ref[...]
+
+
+def scores_of(e_ref, t_ref, s_ref):
     width = e_ref.shape[1]
-    t = jnp.concatenate([piece[...] for piece in pieces], axis=0)
     s_ref[...] = lax.dot_general(
-        e_ref[...], t, (((1,), (1,)), ((), ())), preferred_element_type=jnp.float32
+        e_ref[...], t_ref[...], (((1,), (1,)), ((), ())), preferred_element_type=jnp.float32
     ) * (LOG2E / (STRENGTH * math.sqrt(width)))
 
 
@@ -103,21 +111,20 @@
     return functools.reduce(jnp.add, parts)
 
 
-def row_sums(parts, before=None):
+def row_sums(parts, before=()):
     row_max = over_lanes(largest, parts)
-    if before is not None:
+    if before:
         old_max, old_tot = before[0][...], before[1][...]
         row_max = jnp.maximum(row_max, old_max)
     tot = over_lanes(total, [jnp.exp2(p - row_max) for p in parts])
-    if before is not None:
+    if before:
         tot = tot + old_tot * jnp.exp2(old_max - row_max)
     return row_max, tot
 
 
-def part_kernel(count, more, e_ref, *refs):
-    pieces, rest = refs[:count], refs[count:]
-    before, (s_ref, max_ref, tot_ref) = (rest[:2], rest[2:]) if more else (None, rest)
-    scores_of(e_ref, pieces, s_ref)
+def part_kernel(e_ref, t_ref, *refs):
+    before, (s_ref, max_ref, tot_ref) = refs[:-3], refs[-3:]
+    scores_of(e_ref, t_ref, s_ref)
     max_ref[...], tot_ref[...] = row_sums(chunks_of(s_ref), before)
 
 
@@ -131,34 +138,33 @@
         out_ref[at, :] = lse if less is None else lse - less[at, :]
 
 
-def final_kernel(n, places, per_piece, e_ref, t_ref, max_ref, tot_ref, logw_ref, *refs):
+def final_kernel(n, per_group, groups, e_ref, t_ref, max_ref, tot_ref, logw_ref, *refs):
     done, (s_ref, out_ref, cols_ref) = refs[:-3], refs[-3:]
-    scores_of(e_ref, [t_ref], s_ref)
+    scores_of(e_ref, t_ref, s_ref)
     row_max, tot = row_sums(chunks_of(s_ref), (max_ref, tot_ref))
     pot = logw_ref[...] - (row_max + jnp.log2(tot))
-    column_sums(done + (s_ref,), rows_of(n, places, per_piece), pot, cols_ref)
+    column_sums(done + (s_ref,), rows_of(n, per_group, groups), pot, cols_ref)
     tall = cols_ref[...]
     for d in range(n):
         out_ref[d] = tall
 
 
-def second_kernel(n, places, per_piece, g_ref, logw_ref, dlw_ref, *refs):
+def second_kernel(n, per_group, groups, g_ref, logw_ref, dlw_ref, *refs):
     scores, (src_ref, out_ref, cols_ref) = refs[:-3], refs[-3:]
     per = dlw_ref.shape[0] * LANES // n
     g = g_ref[...]
     top = jnp.max(g, axis=0)
     cols_ref[...] = dlw_ref[...] - (top + jnp.log2(jnp.sum(jnp.exp2(g - top[None]), axis=0)))
-    rows = rows_of(n, places, per_piece)
+    rows = rows_of(n, per_group, groups)
     parts = [part for s_ref in scores for part in chunks_of(s_ref)]
     row_max, tot = row_sums([p + cols_ref[pl.ds(row, 1), :] for p, row in zip(parts, rows)])
     pot = logw_ref[...] - (row_max + jnp.log2(tot))
     src_ref[...] = pot
     column_sums(scores, rows, pot, cols_ref, dlw_ref)
-    for half in range(2):
-        for place in range(n // 2):
-            d = device_at(n, half, place)
-            row, lane = divmod((half * (n // 2) + place) * per, LANES)
-            out_ref[d : d + 1, :] = cols_ref[row : row + 1, lane : lane + per]
+    for place in range(n):
+        d = device_at(n, place)
+        row, lane = divmod(place * per, LANES)
+        out_ref[d : d + 1, :] = cols_ref[row : row + 1, lane : lane + per]
 
 
 def last_kernel(g_ref, pot_ref, src_ref, own_ref):
@@ -192,9 +198,12 @@
     shape = jax.ShapeDtypeStruct
 
     def swap(a, distance):
-        return lax.ppermute(a, "src", [(i, i ^ distance) for i in range(n)])
-
+        flip = distance if distance == 1 else distance | bin(distance).count("1") % 2
+        return lax.ppermute(a, "src", [(i, i ^ flip) for i in range(n)])
+
+    aways = list(range(n // 4 - 1, 0, -1))
     partner = swap(targets, n // 2)
+    own_wave = [swap(targets, 2 * away) for away in aways]
     emitter, own_targets, logw, dlw = call(
         functools.partial(load_kernel, n),
         (
@@ -215,46 +224,49 @@
         pltpu.HBM,
         pl.CostEstimate(flops=0, bytes_accessed=4 * rows * width, transcendentals=0),
     )
-    piece = 2 * per
-    (pair,) = call(
-        functools.partial(pair_kernel, n),
-        (shape((piece, width), targets.dtype),),
-        [own_targets, partner],
-    )
-    aways = list(range(n // 4 - 1, 0, -1))
-    early, late = aways[:-1], aways[-1]
-    other_pair = swap(pair, 1)
-    near = {away: swap(pair, 2 * away) for away in aways}
-    far = {away: swap(near[away], 1) for away in aways}
-
-    def part(pieces, before):
-        count = len(pieces)
+    size = n // 4 * per
+
+    def group(own, got):
         return call(
-            functools.partial(part_kernel, count, bool(before)),
-            (shape((rows, count * piece), f32), shape((rows, LANES), f32), shape((rows, LANES), f32)),
-            [emitter] + pieces + list(before),
+            functools.partial(group_kernel, n, [0] + aways),
+            (shape((size, width), targets.dtype),),
+            [own] + got,
+        )[0]
+
+    near_own = group(own_targets, own_wave)
+    far_own = swap(near_own, 1)
+    partner, emitter = lax.optimization_barrier((partner, emitter))
+    partner_wave = [swap(partner, 2 * away) for away in aways]
+
+    def part(t, before):
+        return call(
+            part_kernel,
+            (shape((rows, size), f32), shape((rows, LANES), f32), shape((rows, LANES), f32)),
+            [emitter, t, *before],
             cost=pl.CostEstimate(
-                flops=2 * rows * count * piece * width,
-                bytes_accessed=rows * count * piece * 4,
-                transcendentals=rows * count * piece,
+                flops=2 * rows * size * width,
+                bytes_accessed=rows * size * 4,
+                transcendentals=rows * size,
             ),
         )
 
-    scores_a, *sums = part([pair, other_pair], ())
-    scores_b, *sums = part([near[away] for away in early], sums)
-    scores_c, *sums = part([near[late]] + [far[away] for away in early], sums)
-    places = [(0, 0), (0, 1)] + [(away, 0) for away in early]
-    places += [(late, 0)] + [(away, 1) for away in early] + [(late, 1)]
-    per_piece = piece // LANES
+    scores_a, *sums = part(near_own, ())
+    *partner_wave, scores_a = lax.optimization_barrier((*partner_wave, scores_a))
+    near_other = group(partner, partner_wave)
+    far_other = swap(near_other, 1)
+    scores_b, *sums = part(far_own, sums)
+    scores_c, *sums = part(near_other, sums)
+    groups = [(0, 0), (1, 0), (0, 1), (1, 1)]
+    per_group = size // LANES
     scores_d, sent = call(
-        functools.partial(final_kernel, n, places, per_piece),
-        (shape((rows, piece), f32), shape((n, cols // LANES, LANES), f32)),
-        [emitter, far[late], *sums, logw, scores_a, scores_b, scores_c],
+        functools.partial(final_kernel, n, per_group, groups),
+        (shape((rows, size), f32), shape((n, cols // LANES, LANES), f32)),
+        [emitter, far_other, *sums, logw, scores_a, scores_b, scores_c],
         [pltpu.VMEM((cols // LANES, LANES), f32)],
     )
     heard = lax.all_to_all(sent, "src", 0, 0)
     pot, parts = call(
-        functools.partial(second_kernel, n, places, per_piece),
+        functools.partial(second_kernel, n, per_group, groups),
         (shape((rows, LANES), f32), shape((n, per), f32)),
         [heard, logw, dlw, scores_a, scores_b, scores_c, scores_d],
         [pltpu.VMEM((cols // LANES, LANES), f32)],

time: 39.6 us -> 38.5 us (0.972)
  waiting for transfers between devices: 5.35 us -> 2.24 us
  starting transfers between devices: 7.67 us -> 10.7 us
  blocking collectives: 20.8 us -> 19.8 us
    ppermute x8 -> x9, waiting for transfers between devices: 5.35 us -> 2.24 us  [swap(): return lax.ppermute(a, 'src', [(i, i ^ flip) for i in range(n)])]
    ppermute x8 -> x9, starting transfers between devices: 7.67 us -> 10.7 us  [swap(): return lax.ppermute(a, 'src', [(i, i ^ flip) for i in range(n)])]
    all_to_all x1, blocking collectives: 11.8 us -> 10.8 us  [local(): heard = lax.all_to_all(sent, 'src', 0, 0)]
    pallas_call x8 -> x9, Pallas kernels: 4.84 us -> 4.87 us  [call(): pl.pallas_call(kernel, out_shape=out_shape, in_specs=[pl.BlockSpec(memory...]
  transfers between devices with their start and end apart: 8 -> 9, of which waited for: 4 -> 4; matrix products, arithmetic and copies ran while one was open for 0% -> 0% of each run, Pallas kernels for 6% -> 6%
where the time goes in v6:
time: 38.5 us; the launch traced here: 38.2 us
  blocking collectives  19.8 us (51%)
  starting transfers between devices  10.7 us (28%)
  Pallas kernels  4.87 us (13%)
  waiting for transfers between devices  2.24 us (6%)
  between operations  0.68 us (2%)
    all_to_all x1, blocking collectives, local(): heard = lax.all_to_all(sent, 'src', 0, 0)  10.8 us
    ppermute x9, starting transfers between devices, swap(): return lax.ppermute(a, 'src', [(i, i ^ flip) for i in range(n)])  10.7 us
    all_to_all x1, blocking collectives, local(): own = lax.all_to_all(parts, 'src', 0, 0)  8.98 us
    pallas_call x9, Pallas kernels, call(): pl.pallas_call(kernel, out_shape=out_shape, in_specs=[pl.BlockSpec(memory...  4.87 us
    ppermute x9, waiting for transfers between devices, swap(): return lax.ppermute(a, 'src', [(i, i ^ flip) for i in range(n)])  2.24 us
  transfers between devices with their start and end apart: 9, of which 4 were waited for; matrix products, arithmetic and copies ran while one was open for 0% of the time, Pallas kernels for 6%

profile of v6, /device:TPU:0, one launch (start us, length us, event | category | flops | bytes accessed | tf_op | source)
XLA Modules:
  0.0 38.2 jit_solution(7276743647797221031)
XLA Ops:
  0.6 3.5 %collective-permute-start = (bf16[64,256]{1,0:T(8,128)(2,1)}, bf16[64,256]{1,0:T(8,128)(2,1)S(1)}, u32[]{:S(2)}, u32[]{:S(2)}) collective-permute-start(bf16[64,256]{1,0:T(8,128)(2,1)} %t_hbm.1), channel_id=1, source_target_pairs={{0,9},{1,8},{2,11},{3,10},{4,13},{5,12},{6,15},{7,14},{8,1},{9,0},... | collective-permute-start | bytes 98312 | tf_op jit(solution)/shard_map/ppermute | solution.py:202
  4.2 2.5 %collective-permute-start.4 = (bf16[64,256]{1,0:T(8,128)(2,1)}, bf16[64,256]{1,0:T(8,128)(2,1)S(1)}, u32[]{:S(2)}, u32[]{:S(2)}) collective-permute-start(bf16[64,256]{1,0:T(8,128)(2,1)} %t_hbm.1), channel_id=1, source_target_pairs={{0,6},{1,7},{2,4},{3,5},{4,2},{5,3},{6,0},{7,1},{8,14},{9,15},{10,... | collective-permute-start | bytes 98312 | tf_op jit(solution)/shard_map/ppermute | solution.py:202
  6.7 0.5 %collective-permute-start.5 = (bf16[64,256]{1,0:T(8,128)(2,1)}, bf16[64,256]{1,0:T(8,128)(2,1)S(1)}, u32[]{:S(2)}, u32[]{:S(2)}) collective-permute-start(bf16[64,256]{1,0:T(8,128)(2,1)} %t_hbm.1), channel_id=1, source_target_pairs={{0,5},{1,4},{2,7},{3,6},{4,1},{5,0},{6,3},{7,2},{8,13},{9,12},{10,... | collective-permute-start | bytes 98312 | tf_op jit(solution)/shard_map/ppermute | solution.py:202
  7.2 0.2 collective-permute-start.6
  7.4 1.0 %shard_map.59 = (bf16[512,256]{1,0:T(8,128)(2,1)S(1)}, bf16[64,256]{1,0:T(8,128)(2,1)S(1)}, f32[512,128]{1,0:T(8,128)S(1)}, f32[8,128]{1,0:T(8,128)S(1)}) custom-call(bf16[512,256]{1,0:T(8,128)(2,1)} %e_hbm.1, bf16[64,256]{1,0:T(8,128)(2,1)} %t_hbm.1, f32[512]{0:T(512)} %logw_hbm.1, f32[1024]{0:T(1024)} %dlw_hbm.1), custom_call_target="tpu_custom_call" | custom-call | bytes 524288 | tf_op jit(solution)/shard_map/pallas_call | solution.py:181
  8.4 0.0 collective-permute-done.refs_0_
  8.4 2.6 %collective-permute-start.1 = (bf16[64,256]{1,0:T(8,128)(2,1)S(1)}, bf16[64,256]{1,0:T(8,128)(2,1)S(1)}, u32[]{:S(2)}, u32[]{:S(2)}) collective-permute-start(bf16[64,256]{1,0:T(8,128)(2,1)S(1)} %collective-permute-done.refs_0_), channel_id=1, source_target_pairs={{0,6},{1,7},{2,4},{3,5},{4,2},{5,3},{6,0},{7,1},{8,14},{9,15},{10,... | collective-permute-start | bytes 98312 | tf_op jit(solution)/shard_map/ppermute | solution.py:202
  11.0 0.2 collective-permute-start.2
  11.2 0.0 collective-permute-done.4.refs_1_
  11.2 0.5 %collective-permute-start.3 = (bf16[64,256]{1,0:T(8,128)(2,1)S(1)}, bf16[64,256]{1,0:T(8,128)(2,1)S(1)}, u32[]{:S(2)}, u32[]{:S(2)}) collective-permute-start(bf16[64,256]{1,0:T(8,128)(2,1)S(1)} %collective-permute-done.refs_0_), channel_id=1, source_target_pairs={{0,3},{1,2},{2,1},{3,0},{4,7},{5,6},{6,5},{7,4},{8,11},{9,10},{10,... | collective-permute-start | bytes 98312 | tf_op jit(solution)/shard_map/ppermute | solution.py:202
  11.7 0.0 collective-permute-done.5.refs_2_
  11.7 0.0 collective-permute-done.6.refs_3_
  11.8 0.2 collective-permute-start.8
  12.0 0.4 %shard_map.61 = (f32[512,256]{1,0:T(8,128)S(1)}, f32[512,128]{1,0:T(8,128)S(1)}, f32[512,128]{1,0:T(8,128)S(1)}) custom-call(bf16[512,256]{1,0:T(8,128)(2,1)S(1)} %get-tuple-element.26.e_ref, bf16[256,256]{1,0:T(8,128)(2,1)S(1)} %shard_map.60.t_ref), custom_call_target="tpu_custom_call" | custom-call | flops 67108864 | bytes 524288 | tf_op jit(solution)/shard_map/pallas_call | solution.py:181
  12.4 0.9 %collective-permute-done.1.refs_1_ = bf16[64,256]{1,0:T(8,128)(2,1)S(1)} collective-permute-done((bf16[64,256]{1,0:T(8,128)(2,1)S(1)}, bf16[64,256]{1,0:T(8,128)(2,1)S(1)}, u32[]{:S(2)}, u32[]{:S(2)}) %collective-permute-start.1) | collective-permute-done | bytes 32800 | tf_op jit(solution)/shard_map/ppermute | solution.py:202
  13.3 1.0 %collective-permute-done.2.refs_2_ = bf16[64,256]{1,0:T(8,128)(2,1)S(1)} collective-permute-done((bf16[64,256]{1,0:T(8,128)(2,1)S(1)}, bf16[64,256]{1,0:T(8,128)(2,1)S(1)}, u32[]{:S(2)}, u32[]{:S(2)}) %collective-permute-start.2) | collective-permute-done | bytes 32800 | tf_op jit(solution)/shard_map/ppermute | solution.py:202
  14.4 0.2 collective-permute-done.3.refs_3_
  14.6 0.4 %collective-permute-start.7 = (bf16[256,256]{1,0:T(8,128)(2,1)S(1)}, bf16[256,256]{1,0:T(8,128)(2,1)S(1)}, u32[]{:S(2)}, u32[]{:S(2)}) collective-permute-start(bf16[256,256]{1,0:T(8,128)(2,1)S(1)} %shard_map.62.t_ref), channel_id=1, source_target_pairs={{0,1},{1,0},{2,3},{3,2},{4,5},{5,4},{6,7},{7,6},{8,9},{9,8},{10,11... | collective-permute-start | bytes 393224 | tf_op jit(solution)/shard_map/ppermute | solution.py:202
  15.0 0.0 collective-permute-done.8.t_ref
  15.0 0.5 %shard_map.63 = (f32[512,256]{1,0:T(8,128)S(1)}, f32[512,128]{1,0:T(8,128)S(1)}, f32[512,128]{1,0:T(8,128)S(1)}) custom-call(bf16[512,256]{1,0:T(8,128)(2,1)S(1)} %get-tuple-element.26.e_ref, bf16[256,256]{1,0:T(8,128)(2,1)S(1)} %collective-permute-done.8.t_ref, f32[512,128]{1,0:T(8,128)S(1)} %get-tuple-element.33.refs_0_, ...), custom_call_target="tpu_custom_call" | custom-call | flops 67108864 | bytes 524288 | tf_op jit(solution)/shard_map/pallas_call | solution.py:181
  15.5 0.5 %shard_map.64 = (f32[512,256]{1,0:T(8,128)S(1)}, f32[512,128]{1,0:T(8,128)S(1)}, f32[512,128]{1,0:T(8,128)S(1)}) custom-call(bf16[512,256]{1,0:T(8,128)(2,1)S(1)} %get-tuple-element.26.e_ref, bf16[256,256]{1,0:T(8,128)(2,1)S(1)} %shard_map.62.t_ref, f32[512,128]{1,0:T(8,128)S(1)} %get-tuple-element.35.refs_0_, f32[512,128]{1,0:T(8,128)S(1)} %get-tuple-element.36.refs_1_), custom_call_target="tpu_custom_call" | custom-call | flops 67108864 | bytes 524288 | tf_op jit(solution)/shard_map/pallas_call | solution.py:181
  15.9 0.1 collective-permute-done.7.t_ref
  16.0 0.8 %shard_map.65 = (f32[512,256]{1,0:T(8,128)S(1)}, f32[16,8,128]{2,1,0:T(8,128)S(1)}) custom-call(bf16[512,256]{1,0:T(8,128)(2,1)S(1)} %get-tuple-element.26.e_ref, bf16[256,256]{1,0:T(8,128)(2,1)S(1)} %collective-permute-done.7.t_ref, f32[512,128]{1,0:T(8,128)S(1)} %get-tuple-element.37.max_ref, f32[512,128]{1,0:T(8,128)S(1)} %get-tuple-element.38.tot_ref, ...), custom_call_target="tpu_custom_call" | custom-call | tf_op jit(solution)/shard_map/pallas_call | solution.py:181
  16.8 10.8 %all_to_all.16.g_ref = f32[16,8,128]{2,1,0:T(8,128)S(1)} all-to-all(f32[16,8,128]{2,1,0:T(8,128)S(1)} %get-tuple-element.43), channel_id=1, replica_groups=mesh['group'=2,'src'=16] {'src'}, dimensions={0} | all-to-all | bytes 131072 | tf_op jit(solution)/shard_map/all_to_all | solution.py:267
  27.6 1.0 %shard_map.66 = (f32[512,128]{1,0:T(8,128)S(1)}, f32[16,64]{1,0:T(8,128)S(1)}) custom-call(f32[16,8,128]{2,1,0:T(8,128)S(1)} %all_to_all.16.g_ref, f32[512,128]{1,0:T(8,128)S(1)} %get-tuple-element.39.logw_ref, f32[8,128]{1,0:T(8,128)S(1)} %get-tuple-element.44.dlw_ref, f32[512,256]{1,0:T(8,128)S(1)} %get-tuple-element.40.refs_0_, ...), custom_call_target="tpu_custom_call" | custom-call | tf_op jit(solution)/shard_map/pallas_call | solution.py:181
  28.6 9.0 %all_to_all.17 = f32[16,1,64]{2,1,0:T(1,128)S(1)} all-to-all(f32[16,1,64]{2,1,0:T(1,128)S(1)} %bitcast.5), channel_id=1, replica_groups=mesh['group'=2,'src'=16] {'src'}, dimensions={0} | all-to-all | bytes 8192 | tf_op jit(solution)/shard_map/all_to_all | solution.py:274
  37.6 0.6 %shard_map.67 = (f32[512]{0:T(512)}, f32[64]{0:T(128)}) custom-call(f32[16,64]{1,0:T(8,128)S(1)} %bitcast.4, f32[512,128]{1,0:T(8,128)S(1)} %get-tuple-element.47.pot_ref), custom_call_target="tpu_custom_call" | custom-call | tf_op jit(solution)/shard_map/pallas_call | solution.py:181
  (2 shorter events, 0.0 us)
Async XLA Ops:
  0.6 7.8 %collective-permute-start = (bf16[64,256]{1,0:T(8,128)(2,1)}, bf16[64,256]{1,0:T(8,128)(2,1)S(1)}, u32[]{:S(2)}, u32[]{:S(2)}) collective-permute-start(bf16[64,256]{1,0:T(8,128)(2,1)} %t_hbm.1), channel_id=1, source_target_pairs={{0,9},{1,8},{2,11},{3,10},{4,13},{5,12},{6,15},{7,14},{8,1},{9,0},... | collective-permute-start | bytes 98312 | tf_op jit(solution)/shard_map/ppermute | solution.py:202
  4.2 7.1 %collective-permute-start.4 = (bf16[64,256]{1,0:T(8,128)(2,1)}, bf16[64,256]{1,0:T(8,128)(2,1)S(1)}, u32[]{:S(2)}, u32[]{:S(2)}) collective-permute-start(bf16[64,256]{1,0:T(8,128)(2,1)} %t_hbm.1), channel_id=1, source_target_pairs={{0,6},{1,7},{2,4},{3,5},{4,2},{5,3},{6,0},{7,1},{8,14},{9,15},{10,... | collective-permute-start | bytes 98312 | tf_op jit(solution)/shard_map/ppermute | solution.py:202
  6.7 5.0 %collective-permute-start.5 = (bf16[64,256]{1,0:T(8,128)(2,1)}, bf16[64,256]{1,0:T(8,128)(2,1)S(1)}, u32[]{:S(2)}, u32[]{:S(2)}) collective-permute-start(bf16[64,256]{1,0:T(8,128)(2,1)} %t_hbm.1), channel_id=1, source_target_pairs={{0,5},{1,4},{2,7},{3,6},{4,1},{5,0},{6,3},{7,2},{8,13},{9,12},{10,... | collective-permute-start | bytes 98312 | tf_op jit(solution)/shard_map/ppermute | solution.py:202
  7.2 4.6 %collective-permute-start.6 = (bf16[64,256]{1,0:T(8,128)(2,1)}, bf16[64,256]{1,0:T(8,128)(2,1)S(1)}, u32[]{:S(2)}, u32[]{:S(2)}) collective-permute-start(bf16[64,256]{1,0:T(8,128)(2,1)} %t_hbm.1), channel_id=1, source_target_pairs={{0,3},{1,2},{2,1},{3,0},{4,7},{5,6},{6,5},{7,4},{8,11},{9,10},{10,... | collective-permute-start | bytes 98312 | tf_op jit(solution)/shard_map/ppermute | solution.py:202
  8.4 4.9 %collective-permute-start.1 = (bf16[64,256]{1,0:T(8,128)(2,1)S(1)}, bf16[64,256]{1,0:T(8,128)(2,1)S(1)}, u32[]{:S(2)}, u32[]{:S(2)}) collective-permute-start(bf16[64,256]{1,0:T(8,128)(2,1)S(1)} %collective-permute-done.refs_0_), channel_id=1, source_target_pairs={{0,6},{1,7},{2,4},{3,5},{4,2},{5,3},{6,0},{7,1},{8,14},{9,15},{10,... | collective-permute-start | bytes 98312 | tf_op jit(solution)/shard_map/ppermute | solution.py:202
  11.0 3.3 %collective-permute-start.2 = (bf16[64,256]{1,0:T(8,128)(2,1)S(1)}, bf16[64,256]{1,0:T(8,128)(2,1)S(1)}, u32[]{:S(2)}, u32[]{:S(2)}) collective-permute-start(bf16[64,256]{1,0:T(8,128)(2,1)S(1)} %collective-permute-done.refs_0_), channel_id=1, source_target_pairs={{0,5},{1,4},{2,7},{3,6},{4,1},{5,0},{6,3},{7,2},{8,13},{9,12},{10,... | collective-permute-start | bytes 98312 | tf_op jit(solution)/shard_map/ppermute | solution.py:202
  11.2 3.3 %collective-permute-start.3 = (bf16[64,256]{1,0:T(8,128)(2,1)S(1)}, bf16[64,256]{1,0:T(8,128)(2,1)S(1)}, u32[]{:S(2)}, u32[]{:S(2)}) collective-permute-start(bf16[64,256]{1,0:T(8,128)(2,1)S(1)} %collective-permute-done.refs_0_), channel_id=1, source_target_pairs={{0,3},{1,2},{2,1},{3,0},{4,7},{5,6},{6,5},{7,4},{8,11},{9,10},{10,... | collective-permute-start | bytes 98312 | tf_op jit(solution)/shard_map/ppermute | solution.py:202
  11.8 3.3 %collective-permute-start.8 = (bf16[256,256]{1,0:T(8,128)(2,1)S(1)}, bf16[256,256]{1,0:T(8,128)(2,1)S(1)}, u32[]{:S(2)}, u32[]{:S(2)}) collective-permute-start(bf16[256,256]{1,0:T(8,128)(2,1)S(1)} %shard_map.60.t_ref), channel_id=1, source_target_pairs={{0,1},{1,0},{2,3},{3,2},{4,5},{5,4},{6,7},{7,6},{8,9},{9,8},{10,11... | collective-permute-start | bytes 393224 | tf_op jit(solution)/shard_map/ppermute | solution.py:202
  14.6 1.4 %collective-permute-start.7 = (bf16[256,256]{1,0:T(8,128)(2,1)S(1)}, bf16[256,256]{1,0:T(8,128)(2,1)S(1)}, u32[]{:S(2)}, u32[]{:S(2)}) collective-permute-start(bf16[256,256]{1,0:T(8,128)(2,1)S(1)} %shard_map.62.t_ref), channel_id=1, source_target_pairs={{0,1},{1,0},{2,3},{3,2},{4,5},{5,4},{6,7},{7,6},{8,9},{9,8},{10,11... | collective-permute-start | bytes 393224 | tf_op jit(solution)/shard_map/ppermute | solution.py:202

commit v7 on v6

--- a/solution.py
+++ b/solution.py
@@ -32,20 +32,16 @@
 
 def device_at(n, place):
     quarter = n // 4
-    core, upper = place // (2 * quarter), place // quarter % 2
-    chip = upper * (n // 4) + place % quarter
-    return chip * 2 + (core + bin(chip).count("1")) % 2
+    half, upper = place // (2 * quarter), place // quarter % 2
+    chip = place % quarter
+    return upper * (n // 2) + chip * 2 + (half ^ chip % 2)
 
 
 def rows_of(n, per_group, groups):
     me = lax.axis_index("src")
-    upper = me // (n // 2)
-    core = me
-    for k in range(1, n.bit_length() - 1):
-        core = core + me // 2**k
-    core = lax.rem(core, 2)
+    half, upper = lax.rem(me + me // 2, 2), me // (n // 2)
     return [
-        (jnp.bitwise_xor(core, over) * 2 + jnp.bitwise_xor(upper, across)) * per_group + k
+        (jnp.bitwise_xor(half, over) * 2 + jnp.bitwise_xor(upper, across)) * per_group + k
         for over, across in groups
         for k in range(per_group)
     ]
@@ -128,39 +124,45 @@
     max_ref[...], tot_ref[...] = row_sums(chunks_of(s_ref), before)
 
 
-def column_sums(scores, places, pot, out_ref, less=None):
-    parts = [part for s_ref in scores for part in chunks_of(s_ref)]
-    for part, row in zip(parts, places):
-        terms = part + pot
-        top = jnp.max(terms, axis=0, keepdims=True)
-        lse = top + jnp.log2(jnp.sum(jnp.exp2(terms - top), axis=0, keepdims=True))
-        at = pl.ds(row, 1)
-        out_ref[at, :] = lse if less is None else lse - less[at, :]
-
-
 def final_kernel(n, per_group, groups, e_ref, t_ref, max_ref, tot_ref, logw_ref, *refs):
-    done, (s_ref, out_ref, cols_ref) = refs[:-3], refs[-3:]
-    scores_of(e_ref, t_ref, s_ref)
-    row_max, tot = row_sums(chunks_of(s_ref), (max_ref, tot_ref))
+    count = len(groups)
+    done, refs = refs[: count - 1], refs[count - 1 :]
+    terms, (pot_ref, top_ref, out_ref, cols_ref) = refs[:count], refs[count:]
+    scores_of(e_ref, t_ref, terms[-1])
+    row_max, tot = row_sums(chunks_of(terms[-1]), (max_ref, tot_ref))
     pot = logw_ref[...] - (row_max + jnp.log2(tot))
-    column_sums(done + (s_ref,), rows_of(n, per_group, groups), pot, cols_ref)
+    pot_ref[...] = pot
+    rows = iter(rows_of(n, per_group, groups))
+    for s_ref, c_ref in zip(done + (terms[-1],), terms):
+        for j, part in enumerate(chunks_of(s_ref)):
+            at = pl.ds(next(rows), 1)
+            term = part + pot
+            top = jnp.max(term, axis=0, keepdims=True)
+            over = jnp.exp2(term - top)
+            c_ref[:, j * LANES : (j + 1) * LANES] = over
+            top_ref[at, :] = top
+            cols_ref[at, :] = top + jnp.log2(jnp.sum(over, axis=0, keepdims=True))
     tall = cols_ref[...]
     for d in range(n):
         out_ref[d] = tall
 
 
-def second_kernel(n, per_group, groups, g_ref, logw_ref, dlw_ref, *refs):
-    scores, (src_ref, out_ref, cols_ref) = refs[:-3], refs[-3:]
+def second_kernel(n, per_group, groups, g_ref, logw_ref, dlw_ref, pot_ref, top_ref, *refs):
+    terms, (src_ref, out_ref, cols_ref) = refs[:-3], refs[-3:]
     per = dlw_ref.shape[0] * LANES // n
     g = g_ref[...]
     top = jnp.max(g, axis=0)
-    cols_ref[...] = dlw_ref[...] - (top + jnp.log2(jnp.sum(jnp.exp2(g - top[None]), axis=0)))
+    target_pot = dlw_ref[...] - (top + jnp.log2(jnp.sum(jnp.exp2(g - top[None]), axis=0)))
+    cols_ref[...] = jnp.exp2(top_ref[...] + target_pot)
     rows = rows_of(n, per_group, groups)
-    parts = [part for s_ref in scores for part in chunks_of(s_ref)]
-    row_max, tot = row_sums([p + cols_ref[pl.ds(row, 1), :] for p, row in zip(parts, rows)])
-    pot = logw_ref[...] - (row_max + jnp.log2(tot))
-    src_ref[...] = pot
-    column_sums(scores, rows, pot, cols_ref, dlw_ref)
+    parts = [part for c_ref in terms for part in chunks_of(c_ref)]
+    tot = over_lanes(total, [p * cols_ref[pl.ds(row, 1), :] for p, row in zip(parts, rows)])
+    logw = logw_ref[...]
+    src_ref[...] = logw + pot_ref[...] - jnp.log2(tot)
+    scale = jnp.exp2(logw) / tot
+    for part, row in zip(parts, rows):
+        cols_ref[pl.ds(row, 1), :] = jnp.sum(part * scale, axis=0, keepdims=True)
+    cols_ref[...] = top_ref[...] + jnp.log2(cols_ref[...]) - dlw_ref[...]
     for place in range(n):
         d = device_at(n, place)
         row, lane = divmod(place * per, LANES)
@@ -198,12 +200,12 @@
     shape = jax.ShapeDtypeStruct
 
     def swap(a, distance):
-        flip = distance if distance == 1 else distance | bin(distance).count("1") % 2
-        return lax.ppermute(a, "src", [(i, i ^ flip) for i in range(n)])
-
-    aways = list(range(n // 4 - 1, 0, -1))
+        over = distance ^ distance // 2 % 2
+        return lax.ppermute(a, "src", [(i, i ^ over) for i in range(n)])
+
+    aways = list(range(1, n // 4))
     partner = swap(targets, n // 2)
-    own_wave = [swap(targets, 2 * away) for away in aways]
+    own_wave = [swap(targets, 2 * away) for away in reversed(aways)][::-1]
     emitter, own_targets, logw, dlw = call(
         functools.partial(load_kernel, n),
         (
@@ -258,18 +260,24 @@
     scores_c, *sums = part(near_other, sums)
     groups = [(0, 0), (1, 0), (0, 1), (1, 1)]
     per_group = size // LANES
-    scores_d, sent = call(
+    columns = shape((cols // LANES, LANES), f32)
+    *terms, first_pot, tops, sent = call(
         functools.partial(final_kernel, n, per_group, groups),
-        (shape((rows, size), f32), shape((n, cols // LANES, LANES), f32)),
+        (
+            *[shape((rows, size), f32)] * len(groups),
+            shape((rows, LANES), f32),
+            columns,
+            shape((n, *columns.shape), f32),
+        ),
         [emitter, far_other, *sums, logw, scores_a, scores_b, scores_c],
-        [pltpu.VMEM((cols // LANES, LANES), f32)],
+        [pltpu.VMEM(columns.shape, f32)],
     )
     heard = lax.all_to_all(sent, "src", 0, 0)
     pot, parts = call(
         functools.partial(second_kernel, n, per_group, groups),
         (shape((rows, LANES), f32), shape((n, per), f32)),
-        [heard, logw, dlw, scores_a, scores_b, scores_c, scores_d],
-        [pltpu.VMEM((cols // LANES, LANES), f32)],
+        [heard, logw, dlw, first_pot, tops, *terms],
+        [pltpu.VMEM(columns.shape, f32)],
     )
     own = lax.all_to_all(parts, "src", 0, 0)
     return call(last_kernel, (shape((rows,), f32), shape((per,), f32)), [own, pot])

time: 38.5 us -> 37.7 us (0.979)
  starting transfers between devices: 10.7 us -> 11.5 us
  blocking collectives: 19.8 us -> 19.1 us
  waiting for transfers between devices: 2.24 us -> 1.66 us
    ppermute x9, starting transfers between devices: 10.7 us -> 11.5 us  [swap(): return lax.ppermute(a, 'src', [(i, i ^ over) for i in range(n)])]
    all_to_all x1, blocking collectives: 10.8 us -> 10.1 us  [local(): heard = lax.all_to_all(sent, 'src', 0, 0)]
    ppermute x9, waiting for transfers between devices: 2.24 us -> 1.66 us  [swap(): return lax.ppermute(a, 'src', [(i, i ^ over) for i in range(n)])]
  transfers between devices with their start and end apart: 9 -> 9, of which waited for: 4 -> 3; matrix products, arithmetic and copies ran while one was open for 0% -> 0% of each run, Pallas kernels for 6% -> 6%
where the time goes in v7:
time: 37.7 us; the launch traced here: 37.4 us
  blocking collectives  19.1 us (51%)
  starting transfers between devices  11.5 us (31%)
  Pallas kernels  4.49 us (12%)
  waiting for transfers between devices  1.66 us (4%)
  between operations  0.69 us (2%)
    ppermute x9, starting transfers between devices, swap(): return lax.ppermute(a, 'src', [(i, i ^ over) for i in range(n)])  11.5 us
    all_to_all x1, blocking collectives, local(): heard = lax.all_to_all(sent, 'src', 0, 0)  10.1 us
    all_to_all x1, blocking collectives, local(): own = lax.all_to_all(parts, 'src', 0, 0)  8.98 us
    pallas_call x9, Pallas kernels, call(): pl.pallas_call(kernel, out_shape=out_shape, in_specs=[pl.BlockSpec(memory...  4.49 us
    ppermute x9, waiting for transfers between devices, swap(): return lax.ppermute(a, 'src', [(i, i ^ over) for i in range(n)])  1.66 us
  transfers between devices with their start and end apart: 9, of which 3 were waited for; matrix products, arithmetic and copies ran while one was open for 0% of the time, Pallas kernels for 6%

profile of v7, /device:TPU:0, one launch (start us, length us, event | category | flops | bytes accessed | tf_op | source)
XLA Modules:
  0.0 37.4 jit_solution(8317719765492266255)
XLA Ops:
  0.6 4.1 %collective-permute-start = (bf16[64,256]{1,0:T(8,128)(2,1)}, bf16[64,256]{1,0:T(8,128)(2,1)S(1)}, u32[]{:S(2)}, u32[]{:S(2)}) collective-permute-start(bf16[64,256]{1,0:T(8,128)(2,1)} %t_hbm.1), channel_id=1, source_target_pairs={{0,8},{1,9},{2,10},{3,11},{4,12},{5,13},{6,14},{7,15},{8,0},{9,1},... | collective-permute-start | bytes 98312 | tf_op jit(solution)/shard_map/ppermute | solution.py:204
  4.7 0.7 %collective-permute-start.4 = (bf16[64,256]{1,0:T(8,128)(2,1)}, bf16[64,256]{1,0:T(8,128)(2,1)S(1)}, u32[]{:S(2)}, u32[]{:S(2)}) collective-permute-start(bf16[64,256]{1,0:T(8,128)(2,1)} %t_hbm.1), channel_id=1, source_target_pairs={{0,3},{1,2},{2,1},{3,0},{4,7},{5,6},{6,5},{7,4},{8,11},{9,10},{10,... | collective-permute-start | bytes 98312 | tf_op jit(solution)/shard_map/ppermute | solution.py:204
  5.4 2.1 %collective-permute-start.6 = (bf16[64,256]{1,0:T(8,128)(2,1)}, bf16[64,256]{1,0:T(8,128)(2,1)S(1)}, u32[]{:S(2)}, u32[]{:S(2)}) collective-permute-start(bf16[64,256]{1,0:T(8,128)(2,1)} %t_hbm.1), channel_id=1, source_target_pairs={{0,7},{1,6},{2,5},{3,4},{4,3},{5,2},{6,1},{7,0},{8,15},{9,14},{10,... | collective-permute-start | bytes 98312 | tf_op jit(solution)/shard_map/ppermute | solution.py:204
  7.5 0.4 %collective-permute-start.5 = (bf16[64,256]{1,0:T(8,128)(2,1)}, bf16[64,256]{1,0:T(8,128)(2,1)S(1)}, u32[]{:S(2)}, u32[]{:S(2)}) collective-permute-start(bf16[64,256]{1,0:T(8,128)(2,1)} %t_hbm.1), channel_id=1, source_target_pairs={{0,4},{1,5},{2,6},{3,7},{4,0},{5,1},{6,2},{7,3},{8,12},{9,13},{10,... | collective-permute-start | bytes 98312 | tf_op jit(solution)/shard_map/ppermute | solution.py:204
  7.9 1.0 %shard_map.59 = (bf16[512,256]{1,0:T(8,128)(2,1)S(1)}, bf16[64,256]{1,0:T(8,128)(2,1)S(1)}, f32[512,128]{1,0:T(8,128)S(1)}, f32[8,128]{1,0:T(8,128)S(1)}) custom-call(bf16[512,256]{1,0:T(8,128)(2,1)} %e_hbm.1, bf16[64,256]{1,0:T(8,128)(2,1)} %t_hbm.1, f32[512]{0:T(512)} %logw_hbm.1, f32[1024]{0:T(1024)} %dlw_hbm.1), custom_call_target="tpu_custom_call" | custom-call | bytes 524288 | tf_op jit(solution)/shard_map/pallas_call | solution.py:183
  9.0 0.0 collective-permute-done.refs_0_
  9.0 1.4 %collective-permute-start.3 = (bf16[64,256]{1,0:T(8,128)(2,1)S(1)}, bf16[64,256]{1,0:T(8,128)(2,1)S(1)}, u32[]{:S(2)}, u32[]{:S(2)}) collective-permute-start(bf16[64,256]{1,0:T(8,128)(2,1)S(1)} %collective-permute-done.refs_0_), channel_id=1, source_target_pairs={{0,7},{1,6},{2,5},{3,4},{4,3},{5,2},{6,1},{7,0},{8,15},{9,14},{10,... | collective-permute-start | bytes 98312 | tf_op jit(solution)/shard_map/ppermute | solution.py:204
  10.4 0.4 %collective-permute-start.2 = (bf16[64,256]{1,0:T(8,128)(2,1)S(1)}, bf16[64,256]{1,0:T(8,128)(2,1)S(1)}, u32[]{:S(2)}, u32[]{:S(2)}) collective-permute-start(bf16[64,256]{1,0:T(8,128)(2,1)S(1)} %collective-permute-done.refs_0_), channel_id=1, source_target_pairs={{0,4},{1,5},{2,6},{3,7},{4,0},{5,1},{6,2},{7,3},{8,12},{9,13},{10,... | collective-permute-start | bytes 98312 | tf_op jit(solution)/shard_map/ppermute | solution.py:204
  10.9 0.0 collective-permute-done.4.refs_1_
  10.9 1.1 %collective-permute-start.1 = (bf16[64,256]{1,0:T(8,128)(2,1)S(1)}, bf16[64,256]{1,0:T(8,128)(2,1)S(1)}, u32[]{:S(2)}, u32[]{:S(2)}) collective-permute-start(bf16[64,256]{1,0:T(8,128)(2,1)S(1)} %collective-permute-done.refs_0_), channel_id=1, source_target_pairs={{0,3},{1,2},{2,1},{3,0},{4,7},{5,6},{6,5},{7,4},{8,11},{9,10},{10,... | collective-permute-start | bytes 98312 | tf_op jit(solution)/shard_map/ppermute | solution.py:204
  12.0 0.0 collective-permute-done.6.refs_3_
  12.0 0.0 collective-permute-done.5.refs_2_
  12.0 0.4 %collective-permute-start.8 = (bf16[256,256]{1,0:T(8,128)(2,1)S(1)}, bf16[256,256]{1,0:T(8,128)(2,1)S(1)}, u32[]{:S(2)}, u32[]{:S(2)}) collective-permute-start(bf16[256,256]{1,0:T(8,128)(2,1)S(1)} %shard_map.60.t_ref), channel_id=1, source_target_pairs={{0,1},{1,0},{2,3},{3,2},{4,5},{5,4},{6,7},{7,6},{8,9},{9,8},{10,11... | collective-permute-start | bytes 393224 | tf_op jit(solution)/shard_map/ppermute | solution.py:204
  12.4 0.4 %shard_map.61 = (f32[512,256]{1,0:T(8,128)S(1)}, f32[512,128]{1,0:T(8,128)S(1)}, f32[512,128]{1,0:T(8,128)S(1)}) custom-call(bf16[512,256]{1,0:T(8,128)(2,1)S(1)} %get-tuple-element.31.e_ref, bf16[256,256]{1,0:T(8,128)(2,1)S(1)} %shard_map.60.t_ref), custom_call_target="tpu_custom_call" | custom-call | flops 67108864 | bytes 524288 | tf_op jit(solution)/shard_map/pallas_call | solution.py:183
  12.9 0.6 %collective-permute-done.3.refs_3_ = bf16[64,256]{1,0:T(8,128)(2,1)S(1)} collective-permute-done((bf16[64,256]{1,0:T(8,128)(2,1)S(1)}, bf16[64,256]{1,0:T(8,128)(2,1)S(1)}, u32[]{:S(2)}, u32[]{:S(2)}) %collective-permute-start.3) | collective-permute-done | bytes 32800 | tf_op jit(solution)/shard_map/ppermute | solution.py:204
  13.5 1.0 %collective-permute-done.2.refs_2_ = bf16[64,256]{1,0:T(8,128)(2,1)S(1)} collective-permute-done((bf16[64,256]{1,0:T(8,128)(2,1)S(1)}, bf16[64,256]{1,0:T(8,128)(2,1)S(1)}, u32[]{:S(2)}, u32[]{:S(2)}) %collective-permute-start.2) | collective-permute-done | bytes 32800 | tf_op jit(solution)/shard_map/ppermute | solution.py:204
  14.4 0.0 collective-permute-done.1.refs_1_
  14.5 0.8 %collective-permute-start.7 = (bf16[256,256]{1,0:T(8,128)(2,1)S(1)}, bf16[256,256]{1,0:T(8,128)(2,1)S(1)}, u32[]{:S(2)}, u32[]{:S(2)}) collective-permute-start(bf16[256,256]{1,0:T(8,128)(2,1)S(1)} %shard_map.62.t_ref), channel_id=1, source_target_pairs={{0,1},{1,0},{2,3},{3,2},{4,5},{5,4},{6,7},{7,6},{8,9},{9,8},{10,11... | collective-permute-start | bytes 393224 | tf_op jit(solution)/shard_map/ppermute | solution.py:204
  15.3 0.0 collective-permute-done.8.t_ref
  15.3 0.5 %shard_map.63 = (f32[512,256]{1,0:T(8,128)S(1)}, f32[512,128]{1,0:T(8,128)S(1)}, f32[512,128]{1,0:T(8,128)S(1)}) custom-call(bf16[512,256]{1,0:T(8,128)(2,1)S(1)} %get-tuple-element.31.e_ref, bf16[256,256]{1,0:T(8,128)(2,1)S(1)} %collective-permute-done.8.t_ref, f32[512,128]{1,0:T(8,128)S(1)} %get-tuple-element.38.refs_0_, ...), custom_call_target="tpu_custom_call" | custom-call | flops 67108864 | bytes 524288 | tf_op jit(solution)/shard_map/pallas_call | solution.py:183
  15.7 0.5 %shard_map.64 = (f32[512,256]{1,0:T(8,128)S(1)}, f32[512,128]{1,0:T(8,128)S(1)}, f32[512,128]{1,0:T(8,128)S(1)}) custom-call(bf16[512,256]{1,0:T(8,128)(2,1)S(1)} %get-tuple-element.31.e_ref, bf16[256,256]{1,0:T(8,128)(2,1)S(1)} %shard_map.62.t_ref, f32[512,128]{1,0:T(8,128)S(1)} %get-tuple-element.40.refs_0_, f32[512,128]{1,0:T(8,128)S(1)} %get-tuple-element.41.refs_1_), custom_call_target="tpu_custom_call" | custom-call | flops 67108864 | bytes 524288 | tf_op jit(solution)/shard_map/pallas_call | solution.py:183
  16.2 0.1 collective-permute-done.7.t_ref
  16.3 0.9 %shard_map.65 = (f32[512,256]{1,0:T(8,128)S(1)}, f32[512,256]{1,0:T(8,128)S(1)}, f32[512,256]{1,0:T(8,128)S(1)}, f32[512,256]{1,0:T(8,128)S(1)}, f32[512,128]{1,...) custom-call(bf16[512,256]{1,0:T(8,128)(2,1)S(1)} %get-tuple-element.31.e_ref, ...), custom_call_target="tpu_custom_call" | custom-call | tf_op jit(solution)/shard_map/pallas_call | solution.py:183
  17.2 10.1 %all_to_all.16.g_ref = f32[16,8,128]{2,1,0:T(8,128)S(1)} all-to-all(f32[16,8,128]{2,1,0:T(8,128)S(1)} %get-tuple-element.48), channel_id=1, replica_groups=mesh['group'=2,'src'=16] {'src'}, dimensions={0} | all-to-all | bytes 131072 | tf_op jit(solution)/shard_map/all_to_all | solution.py:275
  27.3 0.5 %shard_map.66 = (f32[512,128]{1,0:T(8,128)S(1)}, f32[16,64]{1,0:T(8,128)S(1)}) custom-call(f32[16,8,128]{2,1,0:T(8,128)S(1)} %all_to_all.16.g_ref, f32[512,128]{1,0:T(8,128)S(1)} %get-tuple-element.44.logw_ref, f32[8,128]{1,0:T(8,128)S(1)} %get-tuple-element.49.dlw_ref, f32[512,128]{1,0:T(8,128)S(1)} %get-tuple-element.50.pot_ref, ...), custom_call_target="tpu_custom_call" | custom-call | tf_op jit(solution)/shard_map/pallas_call | solution.py:183
  27.8 9.0 %all_to_all.17 = f32[16,1,64]{2,1,0:T(1,128)S(1)} all-to-all(f32[16,1,64]{2,1,0:T(1,128)S(1)} %bitcast.5), channel_id=1, replica_groups=mesh['group'=2,'src'=16] {'src'}, dimensions={0} | all-to-all | bytes 8192 | tf_op jit(solution)/shard_map/all_to_all | solution.py:282
  36.8 0.6 %shard_map.67 = (f32[512]{0:T(512)}, f32[64]{0:T(128)}) custom-call(f32[16,64]{1,0:T(8,128)S(1)} %bitcast.4, f32[512,128]{1,0:T(8,128)S(1)} %get-tuple-element.57.pot_ref), custom_call_target="tpu_custom_call" | custom-call | tf_op jit(solution)/shard_map/pallas_call | solution.py:183
  (2 shorter events, 0.0 us)
Async XLA Ops:
  0.6 8.4 %collective-permute-start = (bf16[64,256]{1,0:T(8,128)(2,1)}, bf16[64,256]{1,0:T(8,128)(2,1)S(1)}, u32[]{:S(2)}, u32[]{:S(2)}) collective-permute-start(bf16[64,256]{1,0:T(8,128)(2,1)} %t_hbm.1), channel_id=1, source_target_pairs={{0,8},{1,9},{2,10},{3,11},{4,12},{5,13},{6,14},{7,15},{8,0},{9,1},... | collective-permute-start | bytes 98312 | tf_op jit(solution)/shard_map/ppermute | solution.py:204
  4.7 6.2 %collective-permute-start.4 = (bf16[64,256]{1,0:T(8,128)(2,1)}, bf16[64,256]{1,0:T(8,128)(2,1)S(1)}, u32[]{:S(2)}, u32[]{:S(2)}) collective-permute-start(bf16[64,256]{1,0:T(8,128)(2,1)} %t_hbm.1), channel_id=1, source_target_pairs={{0,3},{1,2},{2,1},{3,0},{4,7},{5,6},{6,5},{7,4},{8,11},{9,10},{10,... | collective-permute-start | bytes 98312 | tf_op jit(solution)/shard_map/ppermute | solution.py:204
  5.4 6.6 %collective-permute-start.6 = (bf16[64,256]{1,0:T(8,128)(2,1)}, bf16[64,256]{1,0:T(8,128)(2,1)S(1)}, u32[]{:S(2)}, u32[]{:S(2)}) collective-permute-start(bf16[64,256]{1,0:T(8,128)(2,1)} %t_hbm.1), channel_id=1, source_target_pairs={{0,7},{1,6},{2,5},{3,4},{4,3},{5,2},{6,1},{7,0},{8,15},{9,14},{10,... | collective-permute-start | bytes 98312 | tf_op jit(solution)/shard_map/ppermute | solution.py:204
  7.5 4.5 %collective-permute-start.5 = (bf16[64,256]{1,0:T(8,128)(2,1)}, bf16[64,256]{1,0:T(8,128)(2,1)S(1)}, u32[]{:S(2)}, u32[]{:S(2)}) collective-permute-start(bf16[64,256]{1,0:T(8,128)(2,1)} %t_hbm.1), channel_id=1, source_target_pairs={{0,4},{1,5},{2,6},{3,7},{4,0},{5,1},{6,2},{7,3},{8,12},{9,13},{10,... | collective-permute-start | bytes 98312 | tf_op jit(solution)/shard_map/ppermute | solution.py:204
  9.0 4.5 %collective-permute-start.3 = (bf16[64,256]{1,0:T(8,128)(2,1)S(1)}, bf16[64,256]{1,0:T(8,128)(2,1)S(1)}, u32[]{:S(2)}, u32[]{:S(2)}) collective-permute-start(bf16[64,256]{1,0:T(8,128)(2,1)S(1)} %collective-permute-done.refs_0_), channel_id=1, source_target_pairs={{0,7},{1,6},{2,5},{3,4},{4,3},{5,2},{6,1},{7,0},{8,15},{9,14},{10,... | collective-permute-start | bytes 98312 | tf_op jit(solution)/shard_map/ppermute | solution.py:204
  10.4 4.0 %collective-permute-start.2 = (bf16[64,256]{1,0:T(8,128)(2,1)S(1)}, bf16[64,256]{1,0:T(8,128)(2,1)S(1)}, u32[]{:S(2)}, u32[]{:S(2)}) collective-permute-start(bf16[64,256]{1,0:T(8,128)(2,1)S(1)} %collective-permute-done.refs_0_), channel_id=1, source_target_pairs={{0,4},{1,5},{2,6},{3,7},{4,0},{5,1},{6,2},{7,3},{8,12},{9,13},{10,... | collective-permute-start | bytes 98312 | tf_op jit(solution)/shard_map/ppermute | solution.py:204
  10.9 3.5 %collective-permute-start.1 = (bf16[64,256]{1,0:T(8,128)(2,1)S(1)}, bf16[64,256]{1,0:T(8,128)(2,1)S(1)}, u32[]{:S(2)}, u32[]{:S(2)}) collective-permute-start(bf16[64,256]{1,0:T(8,128)(2,1)S(1)} %collective-permute-done.refs_0_), channel_id=1, source_target_pairs={{0,3},{1,2},{2,1},{3,0},{4,7},{5,6},{6,5},{7,4},{8,11},{9,10},{10,... | collective-permute-start | bytes 98312 | tf_op jit(solution)/shard_map/ppermute | solution.py:204
  12.0 3.3 %collective-permute-start.8 = (bf16[256,256]{1,0:T(8,128)(2,1)S(1)}, bf16[256,256]{1,0:T(8,128)(2,1)S(1)}, u32[]{:S(2)}, u32[]{:S(2)}) collective-permute-start(bf16[256,256]{1,0:T(8,128)(2,1)S(1)} %shard_map.60.t_ref), channel_id=1, source_target_pairs={{0,1},{1,0},{2,3},{3,2},{4,5},{5,4},{6,7},{7,6},{8,9},{9,8},{10,11... | collective-permute-start | bytes 393224 | tf_op jit(solution)/shard_map/ppermute | solution.py:204
  14.5 1.8 %collective-permute-start.7 = (bf16[256,256]{1,0:T(8,128)(2,1)S(1)}, bf16[256,256]{1,0:T(8,128)(2,1)S(1)}, u32[]{:S(2)}, u32[]{:S(2)}) collective-permute-start(bf16[256,256]{1,0:T(8,128)(2,1)S(1)} %shard_map.62.t_ref), channel_id=1, source_target_pairs={{0,1},{1,0},{2,3},{3,2},{4,5},{5,4},{6,7},{7,6},{8,9},{9,8},{10,11... | collective-permute-start | bytes 393224 | tf_op jit(solution)/shard_map/ppermute | solution.py:204

commit v8 on v7

--- a/solution.py
+++ b/solution.py
@@ -82,10 +82,10 @@
         out_ref[pl.ds(at, per), :] = ref[...]
 
 
-def scores_of(e_ref, t_ref, s_ref):
+def scores_of(e_ref, t, s_ref):
     width = e_ref.shape[1]
     s_ref[...] = lax.dot_general(
-        e_ref[...], t_ref[...], (((1,), (1,)), ((), ())), preferred_element_type=jnp.float32
+        e_ref[...], t, (((1,), (1,)), ((), ())), preferred_element_type=jnp.float32
     ) * (LOG2E / (STRENGTH * math.sqrt(width)))
 
 
@@ -118,44 +118,53 @@
     return row_max, tot
 
 
-def part_kernel(e_ref, t_ref, *refs):
-    before, (s_ref, max_ref, tot_ref) = refs[:-3], refs[-3:]
-    scores_of(e_ref, t_ref, s_ref)
+def part_kernel(count, e_ref, *refs):
+    groups, before, (s_ref, max_ref, tot_ref) = refs[:count], refs[count:-3], refs[-3:]
+    scores_of(e_ref, jnp.concatenate([t_ref[...] for t_ref in groups], axis=0), s_ref)
     max_ref[...], tot_ref[...] = row_sums(chunks_of(s_ref), before)
 
 
 def final_kernel(n, per_group, groups, e_ref, t_ref, max_ref, tot_ref, logw_ref, *refs):
-    count = len(groups)
-    done, refs = refs[: count - 1], refs[count - 1 :]
-    terms, (pot_ref, top_ref, out_ref, cols_ref) = refs[:count], refs[count:]
-    scores_of(e_ref, t_ref, terms[-1])
-    row_max, tot = row_sums(chunks_of(terms[-1]), (max_ref, tot_ref))
+    done, (kept_ref, pot_ref, top_ref, out_ref, cols_ref, last_ref) = refs[:-6], refs[-6:]
+    scores_of(e_ref, t_ref[...], last_ref)
+    row_max, tot = row_sums(chunks_of(last_ref), (max_ref, tot_ref))
     pot = logw_ref[...] - (row_max + jnp.log2(tot))
     pot_ref[...] = pot
-    rows = iter(rows_of(n, per_group, groups))
-    for s_ref, c_ref in zip(done + (terms[-1],), terms):
-        for j, part in enumerate(chunks_of(s_ref)):
-            at = pl.ds(next(rows), 1)
-            term = part + pot
-            top = jnp.max(term, axis=0, keepdims=True)
-            over = jnp.exp2(term - top)
-            c_ref[:, j * LANES : (j + 1) * LANES] = over
-            top_ref[at, :] = top
-            cols_ref[at, :] = top + jnp.log2(jnp.sum(over, axis=0, keepdims=True))
+    parts = [part for s_ref in done + (last_ref,) for part in chunks_of(s_ref)]
+    for j, (part, row) in enumerate(zip(parts, rows_of(n, per_group, groups))):
+        at = pl.ds(row, 1)
+        term = part + pot
+        top = jnp.max(term, axis=0, keepdims=True)
+        over = jnp.exp2(term - top)
+        kept_ref[:, j * LANES : (j + 1) * LANES] = over
+        top_ref[at, :] = top
+        cols_ref[at, :] = top + jnp.log2(jnp.sum(over, axis=0, keepdims=True))
     tall = cols_ref[...]
     for d in range(n):
         out_ref[d] = tall
 
 
-def second_kernel(n, per_group, groups, g_ref, logw_ref, dlw_ref, pot_ref, top_ref, *refs):
-    terms, (src_ref, out_ref, cols_ref) = refs[:-3], refs[-3:]
+def second_kernel(
+    n,
+    per_group,
+    groups,
+    g_ref,
+    logw_ref,
+    dlw_ref,
+    pot_ref,
+    top_ref,
+    kept_ref,
+    src_ref,
+    out_ref,
+    cols_ref,
+):
     per = dlw_ref.shape[0] * LANES // n
     g = g_ref[...]
     top = jnp.max(g, axis=0)
     target_pot = dlw_ref[...] - (top + jnp.log2(jnp.sum(jnp.exp2(g - top[None]), axis=0)))
     cols_ref[...] = jnp.exp2(top_ref[...] + target_pot)
     rows = rows_of(n, per_group, groups)
-    parts = [part for c_ref in terms for part in chunks_of(c_ref)]
+    parts = chunks_of(kept_ref)
     tot = over_lanes(total, [p * cols_ref[pl.ds(row, 1), :] for p, row in zip(parts, rows)])
     logw = logw_ref[...]
     src_ref[...] = logw + pot_ref[...] - jnp.log2(tot)
@@ -205,7 +214,7 @@
 
     aways = list(range(1, n // 4))
     partner = swap(targets, n // 2)
-    own_wave = [swap(targets, 2 * away) for away in reversed(aways)][::-1]
+    own_wave = [swap(targets, 2 * away) for away in aways]
     emitter, own_targets, logw, dlw = call(
         functools.partial(load_kernel, n),
         (
@@ -240,43 +249,43 @@
     partner, emitter = lax.optimization_barrier((partner, emitter))
     partner_wave = [swap(partner, 2 * away) for away in aways]
 
-    def part(t, before):
+    def part(groups, before):
+        wide = len(groups) * size
         return call(
-            part_kernel,
-            (shape((rows, size), f32), shape((rows, LANES), f32), shape((rows, LANES), f32)),
-            [emitter, t, *before],
+            functools.partial(part_kernel, len(groups)),
+            (shape((rows, wide), f32), shape((rows, LANES), f32), shape((rows, LANES), f32)),
+            [emitter, *groups, *before],
             cost=pl.CostEstimate(
-                flops=2 * rows * size * width,
-                bytes_accessed=rows * size * 4,
-                transcendentals=rows * size,
+                flops=2 * rows * wide * width,
+                bytes_accessed=rows * wide * 4,
+                transcendentals=rows * wide,
             ),
         )
 
-    scores_a, *sums = part(near_own, ())
-    *partner_wave, scores_a = lax.optimization_barrier((*partner_wave, scores_a))
+    near_scores, *sums = part([near_own], ())
+    *partner_wave, near_scores = lax.optimization_barrier((*partner_wave, near_scores))
     near_other = group(partner, partner_wave)
     far_other = swap(near_other, 1)
-    scores_b, *sums = part(far_own, sums)
-    scores_c, *sums = part(near_other, sums)
+    more_scores, *sums = part([far_own, near_other], sums)
     groups = [(0, 0), (1, 0), (0, 1), (1, 1)]
     per_group = size // LANES
     columns = shape((cols // LANES, LANES), f32)
-    *terms, first_pot, tops, sent = call(
+    kept, first_pot, tops, sent = call(
         functools.partial(final_kernel, n, per_group, groups),
         (
-            *[shape((rows, size), f32)] * len(groups),
+            shape((rows, cols), f32),
             shape((rows, LANES), f32),
             columns,
             shape((n, *columns.shape), f32),
         ),
-        [emitter, far_other, *sums, logw, scores_a, scores_b, scores_c],
-        [pltpu.VMEM(columns.shape, f32)],
+        [emitter, far_other, *sums, logw, near_scores, more_scores],
+        [pltpu.VMEM(columns.shape, f32), pltpu.VMEM((rows, size), f32)],
     )
     heard = lax.all_to_all(sent, "src", 0, 0)
     pot, parts = call(
         functools.partial(second_kernel, n, per_group, groups),
         (shape((rows, LANES), f32), shape((n, per), f32)),
-        [heard, logw, dlw, first_pot, tops, *terms],
+        [heard, logw, dlw, first_pot, tops, kept],
         [pltpu.VMEM(columns.shape, f32)],
     )
     own = lax.all_to_all(parts, "src", 0, 0)

time: 37.7 us -> 37.7 us (level)
  Pallas kernels: 4.49 us -> 4.1 us
    pallas_call x9 -> x8, Pallas kernels: 4.49 us -> 4.1 us  [call(): pl.pallas_call(kernel, out_shape=out_shape, in_specs=[pl.BlockSpec(memory...]
  transfers between devices with their start and end apart: 9 -> 9, of which waited for: 3 -> 3; matrix products, arithmetic and copies ran while one was open for 0% -> 0% of each run, Pallas kernels for 6% -> 5%
where the time goes in v8:
time: 37.7 us; the launch traced here: 37.4 us
  blocking collectives  19.1 us (51%)
  starting transfers between devices  11.5 us (31%)
  Pallas kernels  4.1 us (11%)
  waiting for transfers between devices  2.03 us (5%)
  between operations  0.68 us (2%)
    ppermute x9, starting transfers between devices, swap(): return lax.ppermute(a, 'src', [(i, i ^ over) for i in range(n)])  11.5 us
    all_to_all x1, blocking collectives, local(): heard = lax.all_to_all(sent, 'src', 0, 0)  10.1 us
    all_to_all x1, blocking collectives, local(): own = lax.all_to_all(parts, 'src', 0, 0)  8.98 us
    pallas_call x8, Pallas kernels, call(): pl.pallas_call(kernel, out_shape=out_shape, in_specs=[pl.BlockSpec(memory...  4.1 us
    ppermute x9, waiting for transfers between devices, swap(): return lax.ppermute(a, 'src', [(i, i ^ over) for i in range(n)])  2.03 us
  transfers between devices with their start and end apart: 9, of which 3 were waited for; matrix products, arithmetic and copies ran while one was open for 0% of the time, Pallas kernels for 5%

profile of v8, /device:TPU:0, one launch (start us, length us, event | category | flops | bytes accessed | tf_op | source)
XLA Modules:
  0.0 37.4 jit_solution(17102539633966676635)
XLA Ops:
  0.6 4.1 %collective-permute-start = (bf16[64,256]{1,0:T(8,128)(2,1)}, bf16[64,256]{1,0:T(8,128)(2,1)S(1)}, u32[]{:S(2)}, u32[]{:S(2)}) collective-permute-start(bf16[64,256]{1,0:T(8,128)(2,1)} %t_hbm.1), channel_id=1, source_target_pairs={{0,8},{1,9},{2,10},{3,11},{4,12},{5,13},{6,14},{7,15},{8,0},{9,1},... | collective-permute-start | bytes 98312 | tf_op jit(solution)/shard_map/ppermute | solution.py:213
  4.7 0.7 %collective-permute-start.4 = (bf16[64,256]{1,0:T(8,128)(2,1)}, bf16[64,256]{1,0:T(8,128)(2,1)S(1)}, u32[]{:S(2)}, u32[]{:S(2)}) collective-permute-start(bf16[64,256]{1,0:T(8,128)(2,1)} %t_hbm.1), channel_id=1, source_target_pairs={{0,3},{1,2},{2,1},{3,0},{4,7},{5,6},{6,5},{7,4},{8,11},{9,10},{10,... | collective-permute-start | bytes 98312 | tf_op jit(solution)/shard_map/ppermute | solution.py:213
  5.4 2.1 %collective-permute-start.6 = (bf16[64,256]{1,0:T(8,128)(2,1)}, bf16[64,256]{1,0:T(8,128)(2,1)S(1)}, u32[]{:S(2)}, u32[]{:S(2)}) collective-permute-start(bf16[64,256]{1,0:T(8,128)(2,1)} %t_hbm.1), channel_id=1, source_target_pairs={{0,7},{1,6},{2,5},{3,4},{4,3},{5,2},{6,1},{7,0},{8,15},{9,14},{10,... | collective-permute-start | bytes 98312 | tf_op jit(solution)/shard_map/ppermute | solution.py:213
  7.5 0.4 %collective-permute-start.5 = (bf16[64,256]{1,0:T(8,128)(2,1)}, bf16[64,256]{1,0:T(8,128)(2,1)S(1)}, u32[]{:S(2)}, u32[]{:S(2)}) collective-permute-start(bf16[64,256]{1,0:T(8,128)(2,1)} %t_hbm.1), channel_id=1, source_target_pairs={{0,4},{1,5},{2,6},{3,7},{4,0},{5,1},{6,2},{7,3},{8,12},{9,13},{10,... | collective-permute-start | bytes 98312 | tf_op jit(solution)/shard_map/ppermute | solution.py:213
  7.9 1.0 %shard_map.59 = (bf16[512,256]{1,0:T(8,128)(2,1)S(1)}, bf16[64,256]{1,0:T(8,128)(2,1)S(1)}, f32[512,128]{1,0:T(8,128)S(1)}, f32[8,128]{1,0:T(8,128)S(1)}) custom-call(bf16[512,256]{1,0:T(8,128)(2,1)} %e_hbm.1, bf16[64,256]{1,0:T(8,128)(2,1)} %t_hbm.1, f32[512]{0:T(512)} %logw_hbm.1, f32[1024]{0:T(1024)} %dlw_hbm.1), custom_call_target="tpu_custom_call" | custom-call | bytes 524288 | tf_op jit(solution)/shard_map/pallas_call | solution.py:192
  9.0 0.0 collective-permute-done.refs_0_
  9.0 1.4 %collective-permute-start.3 = (bf16[64,256]{1,0:T(8,128)(2,1)S(1)}, bf16[64,256]{1,0:T(8,128)(2,1)S(1)}, u32[]{:S(2)}, u32[]{:S(2)}) collective-permute-start(bf16[64,256]{1,0:T(8,128)(2,1)S(1)} %collective-permute-done.refs_0_), channel_id=1, source_target_pairs={{0,7},{1,6},{2,5},{3,4},{4,3},{5,2},{6,1},{7,0},{8,15},{9,14},{10,... | collective-permute-start | bytes 98312 | tf_op jit(solution)/shard_map/ppermute | solution.py:213
  10.4 0.4 %collective-permute-start.2 = (bf16[64,256]{1,0:T(8,128)(2,1)S(1)}, bf16[64,256]{1,0:T(8,128)(2,1)S(1)}, u32[]{:S(2)}, u32[]{:S(2)}) collective-permute-start(bf16[64,256]{1,0:T(8,128)(2,1)S(1)} %collective-permute-done.refs_0_), channel_id=1, source_target_pairs={{0,4},{1,5},{2,6},{3,7},{4,0},{5,1},{6,2},{7,3},{8,12},{9,13},{10,... | collective-permute-start | bytes 98312 | tf_op jit(solution)/shard_map/ppermute | solution.py:213
  10.9 0.0 collective-permute-done.4.refs_1_
  10.9 1.1 %collective-permute-start.1 = (bf16[64,256]{1,0:T(8,128)(2,1)S(1)}, bf16[64,256]{1,0:T(8,128)(2,1)S(1)}, u32[]{:S(2)}, u32[]{:S(2)}) collective-permute-start(bf16[64,256]{1,0:T(8,128)(2,1)S(1)} %collective-permute-done.refs_0_), channel_id=1, source_target_pairs={{0,3},{1,2},{2,1},{3,0},{4,7},{5,6},{6,5},{7,4},{8,11},{9,10},{10,... | collective-permute-start | bytes 98312 | tf_op jit(solution)/shard_map/ppermute | solution.py:213
  12.0 0.0 collective-permute-done.6.refs_3_
  12.0 0.0 collective-permute-done.5.refs_2_
  12.0 0.4 %collective-permute-start.8 = (bf16[256,256]{1,0:T(8,128)(2,1)S(1)}, bf16[256,256]{1,0:T(8,128)(2,1)S(1)}, u32[]{:S(2)}, u32[]{:S(2)}) collective-permute-start(bf16[256,256]{1,0:T(8,128)(2,1)S(1)} %shard_map.60.refs_0_), channel_id=1, source_target_pairs={{0,1},{1,0},{2,3},{3,2},{4,5},{5,4},{6,7},{7,6},{8,9},{9,8},{10,11... | collective-permute-start | bytes 393224 | tf_op jit(solution)/shard_map/ppermute | solution.py:213
  12.4 0.4 %shard_map.61 = (f32[512,256]{1,0:T(8,128)S(1)}, f32[512,128]{1,0:T(8,128)S(1)}, f32[512,128]{1,0:T(8,128)S(1)}) custom-call(bf16[512,256]{1,0:T(8,128)(2,1)S(1)} %get-tuple-element.25.e_ref, bf16[256,256]{1,0:T(8,128)(2,1)S(1)} %shard_map.60.refs_0_), custom_call_target="tpu_custom_call" | custom-call | flops 67108864 | bytes 524288 | tf_op jit(solution)/shard_map/pallas_call | solution.py:192
  12.9 0.6 %collective-permute-done.3.refs_3_ = bf16[64,256]{1,0:T(8,128)(2,1)S(1)} collective-permute-done((bf16[64,256]{1,0:T(8,128)(2,1)S(1)}, bf16[64,256]{1,0:T(8,128)(2,1)S(1)}, u32[]{:S(2)}, u32[]{:S(2)}) %collective-permute-start.3) | collective-permute-done | bytes 32800 | tf_op jit(solution)/shard_map/ppermute | solution.py:213
  13.5 1.0 %collective-permute-done.2.refs_2_ = bf16[64,256]{1,0:T(8,128)(2,1)S(1)} collective-permute-done((bf16[64,256]{1,0:T(8,128)(2,1)S(1)}, bf16[64,256]{1,0:T(8,128)(2,1)S(1)}, u32[]{:S(2)}, u32[]{:S(2)}) %collective-permute-start.2) | collective-permute-done | bytes 32800 | tf_op jit(solution)/shard_map/ppermute | solution.py:213
  14.4 0.0 collective-permute-done.1.refs_1_
  14.5 0.8 %collective-permute-start.7 = (bf16[256,256]{1,0:T(8,128)(2,1)S(1)}, bf16[256,256]{1,0:T(8,128)(2,1)S(1)}, u32[]{:S(2)}, u32[]{:S(2)}) collective-permute-start(bf16[256,256]{1,0:T(8,128)(2,1)S(1)} %shard_map.62.refs_1_), channel_id=1, source_target_pairs={{0,1},{1,0},{2,3},{3,2},{4,5},{5,4},{6,7},{7,6},{8,9},{9,8},{10,11... | collective-permute-start | bytes 393224 | tf_op jit(solution)/shard_map/ppermute | solution.py:213
  15.3 0.0 collective-permute-done.8.refs_0_
  15.3 0.5 %shard_map.63 = (f32[512,512]{1,0:T(8,128)S(1)}, f32[512,128]{1,0:T(8,128)S(1)}, f32[512,128]{1,0:T(8,128)S(1)}) custom-call(bf16[512,256]{1,0:T(8,128)(2,1)S(1)} %get-tuple-element.25.e_ref, bf16[256,256]{1,0:T(8,128)(2,1)S(1)} %collective-permute-done.8.refs_0_, bf16[256,256]{1,0:T(8,128)(2,1)S(1)} %shard_map.62.refs_1_, ...), custom_call_target="tpu_custom_call" | custom-call | flops 134217728 | bytes 1048576 | tf_op jit(solution)/shard_map/pallas_call | solution.py:192
  15.8 0.4 %collective-permute-done.7.t_ref = bf16[256,256]{1,0:T(8,128)(2,1)S(1)} collective-permute-done((bf16[256,256]{1,0:T(8,128)(2,1)S(1)}, bf16[256,256]{1,0:T(8,128)(2,1)S(1)}, u32[]{:S(2)}, u32[]{:S(2)}) %collective-permute-start.7) | collective-permute-done | bytes 131104 | tf_op jit(solution)/shard_map/ppermute | solution.py:213
  16.3 1.0 %shard_map.64 = (f32[512,1024]{1,0:T(8,128)S(1)}, f32[512,128]{1,0:T(8,128)S(1)}, f32[8,128]{1,0:T(8,128)S(1)}, f32[16,8,128]{2,1,0:T(8,128)S(1)}) custom-call(bf16[512,256]{1,0:T(8,128)(2,1)S(1)} %get-tuple-element.25.e_ref, bf16[256,256]{1,0:T(8,128)(2,1)S(1)} %collective-permute-done.7.t_ref, f32[512,128]{1,0:T(8,128)S(1)} %get-tuple-element.34.max_ref, ...), custom_call_target="tpu_custom_call" | custom-call | tf_op jit(solution)/shard_map/pallas_call | solution.py:192
  17.2 10.1 %all_to_all.16.g_ref = f32[16,8,128]{2,1,0:T(8,128)S(1)} all-to-all(f32[16,8,128]{2,1,0:T(8,128)S(1)} %get-tuple-element.39), channel_id=1, replica_groups=mesh['group'=2,'src'=16] {'src'}, dimensions={0} | all-to-all | bytes 131072 | tf_op jit(solution)/shard_map/all_to_all | solution.py:284
  27.3 0.5 %shard_map.65 = (f32[512,128]{1,0:T(8,128)S(1)}, f32[16,64]{1,0:T(8,128)S(1)}) custom-call(f32[16,8,128]{2,1,0:T(8,128)S(1)} %all_to_all.16.g_ref, f32[512,128]{1,0:T(8,128)S(1)} %get-tuple-element.36.logw_ref, f32[8,128]{1,0:T(8,128)S(1)} %get-tuple-element.40.dlw_ref, f32[512,128]{1,0:T(8,128)S(1)} %get-tuple-element.41.pot_ref, ...), custom_call_target="tpu_custom_call" | custom-call | tf_op jit(solution)/shard_map/pallas_call | solution.py:192
  27.8 9.0 %all_to_all.17 = f32[16,1,64]{2,1,0:T(1,128)S(1)} all-to-all(f32[16,1,64]{2,1,0:T(1,128)S(1)} %bitcast.5), channel_id=1, replica_groups=mesh['group'=2,'src'=16] {'src'}, dimensions={0} | all-to-all | bytes 8192 | tf_op jit(solution)/shard_map/all_to_all | solution.py:291
  36.8 0.6 %shard_map.66 = (f32[512]{0:T(512)}, f32[64]{0:T(128)}) custom-call(f32[16,64]{1,0:T(8,128)S(1)} %bitcast.4, f32[512,128]{1,0:T(8,128)S(1)} %get-tuple-element.45.pot_ref), custom_call_target="tpu_custom_call" | custom-call | tf_op jit(solution)/shard_map/pallas_call | solution.py:192
  (2 shorter events, 0.0 us)
Async XLA Ops:
  0.6 8.4 %collective-permute-start = (bf16[64,256]{1,0:T(8,128)(2,1)}, bf16[64,256]{1,0:T(8,128)(2,1)S(1)}, u32[]{:S(2)}, u32[]{:S(2)}) collective-permute-start(bf16[64,256]{1,0:T(8,128)(2,1)} %t_hbm.1), channel_id=1, source_target_pairs={{0,8},{1,9},{2,10},{3,11},{4,12},{5,13},{6,14},{7,15},{8,0},{9,1},... | collective-permute-start | bytes 98312 | tf_op jit(solution)/shard_map/ppermute | solution.py:213
  4.7 6.2 %collective-permute-start.4 = (bf16[64,256]{1,0:T(8,128)(2,1)}, bf16[64,256]{1,0:T(8,128)(2,1)S(1)}, u32[]{:S(2)}, u32[]{:S(2)}) collective-permute-start(bf16[64,256]{1,0:T(8,128)(2,1)} %t_hbm.1), channel_id=1, source_target_pairs={{0,3},{1,2},{2,1},{3,0},{4,7},{5,6},{6,5},{7,4},{8,11},{9,10},{10,... | collective-permute-start | bytes 98312 | tf_op jit(solution)/shard_map/ppermute | solution.py:213
  5.4 6.6 %collective-permute-start.6 = (bf16[64,256]{1,0:T(8,128)(2,1)}, bf16[64,256]{1,0:T(8,128)(2,1)S(1)}, u32[]{:S(2)}, u32[]{:S(2)}) collective-permute-start(bf16[64,256]{1,0:T(8,128)(2,1)} %t_hbm.1), channel_id=1, source_target_pairs={{0,7},{1,6},{2,5},{3,4},{4,3},{5,2},{6,1},{7,0},{8,15},{9,14},{10,... | collective-permute-start | bytes 98312 | tf_op jit(solution)/shard_map/ppermute | solution.py:213
  7.5 4.5 %collective-permute-start.5 = (bf16[64,256]{1,0:T(8,128)(2,1)}, bf16[64,256]{1,0:T(8,128)(2,1)S(1)}, u32[]{:S(2)}, u32[]{:S(2)}) collective-permute-start(bf16[64,256]{1,0:T(8,128)(2,1)} %t_hbm.1), channel_id=1, source_target_pairs={{0,4},{1,5},{2,6},{3,7},{4,0},{5,1},{6,2},{7,3},{8,12},{9,13},{10,... | collective-permute-start | bytes 98312 | tf_op jit(solution)/shard_map/ppermute | solution.py:213
  9.0 4.5 %collective-permute-start.3 = (bf16[64,256]{1,0:T(8,128)(2,1)S(1)}, bf16[64,256]{1,0:T(8,128)(2,1)S(1)}, u32[]{:S(2)}, u32[]{:S(2)}) collective-permute-start(bf16[64,256]{1,0:T(8,128)(2,1)S(1)} %collective-permute-done.refs_0_), channel_id=1, source_target_pairs={{0,7},{1,6},{2,5},{3,4},{4,3},{5,2},{6,1},{7,0},{8,15},{9,14},{10,... | collective-permute-start | bytes 98312 | tf_op jit(solution)/shard_map/ppermute | solution.py:213
  10.4 4.0 %collective-permute-start.2 = (bf16[64,256]{1,0:T(8,128)(2,1)S(1)}, bf16[64,256]{1,0:T(8,128)(2,1)S(1)}, u32[]{:S(2)}, u32[]{:S(2)}) collective-permute-start(bf16[64,256]{1,0:T(8,128)(2,1)S(1)} %collective-permute-done.refs_0_), channel_id=1, source_target_pairs={{0,4},{1,5},{2,6},{3,7},{4,0},{5,1},{6,2},{7,3},{8,12},{9,13},{10,... | collective-permute-start | bytes 98312 | tf_op jit(solution)/shard_map/ppermute | solution.py:213
  10.9 3.5 %collective-permute-start.1 = (bf16[64,256]{1,0:T(8,128)(2,1)S(1)}, bf16[64,256]{1,0:T(8,128)(2,1)S(1)}, u32[]{:S(2)}, u32[]{:S(2)}) collective-permute-start(bf16[64,256]{1,0:T(8,128)(2,1)S(1)} %collective-permute-done.refs_0_), channel_id=1, source_target_pairs={{0,3},{1,2},{2,1},{3,0},{4,7},{5,6},{6,5},{7,4},{8,11},{9,10},{10,... | collective-permute-start | bytes 98312 | tf_op jit(solution)/shard_map/ppermute | solution.py:213
  12.0 3.3 %collective-permute-start.8 = (bf16[256,256]{1,0:T(8,128)(2,1)S(1)}, bf16[256,256]{1,0:T(8,128)(2,1)S(1)}, u32[]{:S(2)}, u32[]{:S(2)}) collective-permute-start(bf16[256,256]{1,0:T(8,128)(2,1)S(1)} %shard_map.60.refs_0_), channel_id=1, source_target_pairs={{0,1},{1,0},{2,3},{3,2},{4,5},{5,4},{6,7},{7,6},{8,9},{9,8},{10,11... | collective-permute-start | bytes 393224 | tf_op jit(solution)/shard_map/ppermute | solution.py:213
  14.5 1.8 %collective-permute-start.7 = (bf16[256,256]{1,0:T(8,128)(2,1)S(1)}, bf16[256,256]{1,0:T(8,128)(2,1)S(1)}, u32[]{:S(2)}, u32[]{:S(2)}) collective-permute-start(bf16[256,256]{1,0:T(8,128)(2,1)S(1)} %shard_map.62.refs_1_), channel_id=1, source_target_pairs={{0,1},{1,0},{2,3},{3,2},{4,5},{5,4},{6,7},{7,6},{8,9},{9,8},{10,11... | collective-permute-start | bytes 393224 | tf_op jit(solution)/shard_map/ppermute | solution.py:213

commit v9 on v8

--- a/solution.py
+++ b/solution.py
@@ -47,13 +47,14 @@
     ]
 
 
-def load_kernel(
-    n, e_hbm, t_hbm, logw_hbm, dlw_hbm, e_ref, t_ref, logw_ref, dlw_ref, row_ref, all_ref, sems
-):
+def load_kernel(n, aways, *refs):
+    got, refs = refs[: len(aways)], refs[len(aways) :]
+    e_hbm, t_hbm, logw_hbm, dlw_hbm, e_ref, t_ref, logw_ref, dlw_ref = refs[:8]
+    row_ref, all_ref, own_ref, sems = refs[8:]
     copies = [
         pltpu.make_async_copy(logw_hbm, row_ref, sems.at[0]),
         pltpu.make_async_copy(dlw_hbm, all_ref, sems.at[1]),
-        pltpu.make_async_copy(t_hbm, t_ref, sems.at[2]),
+        pltpu.make_async_copy(t_hbm, own_ref, sems.at[2]),
         pltpu.make_async_copy(e_hbm, e_ref, sems.at[3]),
     ]
     for copy in copies:
@@ -70,6 +71,7 @@
     for j in range(dlw_ref.shape[0]):
         dlw_ref[j : j + 1, :] = row[:, j * LANES : (j + 1) * LANES]
     copies[2].wait()
+    group_kernel(n, [0] + aways, own_ref, *got, t_ref)
     copies[3].wait()
 
 
@@ -166,9 +168,9 @@
     rows = rows_of(n, per_group, groups)
     parts = chunks_of(kept_ref)
     tot = over_lanes(total, [p * cols_ref[pl.ds(row, 1), :] for p, row in zip(parts, rows)])
-    logw = logw_ref[...]
-    src_ref[...] = logw + pot_ref[...] - jnp.log2(tot)
-    scale = jnp.exp2(logw) / tot
+    rate = logw_ref[...] - jnp.log2(tot)
+    src_ref[...] = pot_ref[...] + rate
+    scale = jnp.exp2(rate)
     for part, row in zip(parts, rows):
         cols_ref[pl.ds(row, 1), :] = jnp.sum(part * scale, axis=0, keepdims=True)
     cols_ref[...] = top_ref[...] + jnp.log2(cols_ref[...]) - dlw_ref[...]
@@ -188,16 +190,17 @@
     own_ref[...] = pot.reshape(own_ref.shape)
 
 
-def call(kernel, out_shape, operands, scratch=(), space=pltpu.VMEM, cost=None):
+def call(kernel, out_shape, operands, scratch=(), far=(), cost=None):
+    vmem, hbm = (pl.BlockSpec(memory_space=space) for space in (pltpu.VMEM, pltpu.HBM))
     return pl.pallas_call(
         kernel,
         out_shape=out_shape,
-        in_specs=[pl.BlockSpec(memory_space=space)] * len(operands),
-        out_specs=jax.tree.map(lambda _: pl.BlockSpec(memory_space=pltpu.VMEM), out_shape),
+        in_specs=[vmem] * len(operands) + [hbm] * len(far),
+        out_specs=jax.tree.map(lambda _: vmem, out_shape),
         scratch_shapes=list(scratch),
         compiler_params=pltpu.CompilerParams(vmem_limit_bytes=VMEM_LIMIT),
         cost_estimate=cost,
-    )(*operands)
+    )(*operands, *[pltpu.with_memory_space_constraint(a, pltpu.HBM) for a in far])
 
 
 def local(emitter_vectors, targets, src_logw, dst_logw):
@@ -215,26 +218,6 @@
     aways = list(range(1, n // 4))
     partner = swap(targets, n // 2)
     own_wave = [swap(targets, 2 * away) for away in aways]
-    emitter, own_targets, logw, dlw = call(
-        functools.partial(load_kernel, n),
-        (
-            shape(emitter_vectors.shape, emitter_vectors.dtype),
-            shape(targets.shape, targets.dtype),
-            shape((rows, LANES), f32),
-            shape((cols // LANES, LANES), f32),
-        ),
-        [
-            pltpu.with_memory_space_constraint(a, pltpu.HBM)
-            for a in (emitter_vectors, targets, src_logw, dst_logw)
-        ],
-        [
-            pltpu.VMEM(src_logw.shape, f32),
-            pltpu.VMEM(dst_logw.shape, f32),
-            pltpu.SemaphoreType.DMA((4,)),
-        ],
-        pltpu.HBM,
-        pl.CostEstimate(flops=0, bytes_accessed=4 * rows * width, transcendentals=0),
-    )
     size = n // 4 * per
 
     def group(own, got):
@@ -244,9 +227,25 @@
             [own] + got,
         )[0]
 
-    near_own = group(own_targets, own_wave)
+    emitter, near_own, logw, dlw = call(
+        functools.partial(load_kernel, n, aways),
+        (
+            shape(emitter_vectors.shape, emitter_vectors.dtype),
+            shape((size, width), targets.dtype),
+            shape((rows, LANES), f32),
+            shape((cols // LANES, LANES), f32),
+        ),
+        own_wave,
+        [
+            pltpu.VMEM(src_logw.shape, f32),
+            pltpu.VMEM(dst_logw.shape, f32),
+            pltpu.VMEM(targets.shape, targets.dtype),
+            pltpu.SemaphoreType.DMA((4,)),
+        ],
+        [emitter_vectors, targets, src_logw, dst_logw],
+        pl.CostEstimate(flops=0, bytes_accessed=4 * rows * width, transcendentals=0),
+    )
     far_own = swap(near_own, 1)
-    partner, emitter = lax.optimization_barrier((partner, emitter))
     partner_wave = [swap(partner, 2 * away) for away in aways]
 
     def part(groups, before):

time: 37.7 us -> 37.7 us (level)
  blocking collectives: 19.1 us -> 20.4 us
  starting transfers between devices: 11.5 us -> 10.6 us
    all_to_all x1, blocking collectives: 10.1 us -> 11.4 us  [local(): heard = lax.all_to_all(sent, 'src', 0, 0)]
    ppermute x9, starting transfers between devices: 11.5 us -> 10.6 us  [swap(): return lax.ppermute(a, 'src', [(i, i ^ over) for i in range(n)])]
    pallas_call x8 -> x7, Pallas kernels: 4.1 us -> 4.11 us  [call(): pl.pallas_call(kernel, out_shape=out_shape, in_specs=[vmem] * len(operand...]
where the time goes in v9:
time: 37.7 us; the launch traced here: 37.5 us
  blocking collectives  20.4 us (54%)
  starting transfers between devices  10.6 us (28%)
  Pallas kernels  4.11 us (11%)
  waiting for transfers between devices  1.71 us (5%)
  between operations  0.67 us (2%)
    all_to_all x1, blocking collectives, local(): heard = lax.all_to_all(sent, 'src', 0, 0)  11.4 us
    ppermute x9, starting transfers between devices, swap(): return lax.ppermute(a, 'src', [(i, i ^ over) for i in range(n)])  10.6 us
    all_to_all x1, blocking collectives, local(): own = lax.all_to_all(parts, 'src', 0, 0)  8.98 us
    pallas_call x7, Pallas kernels, call(): pl.pallas_call(kernel, out_shape=out_shape, in_specs=[vmem] * len(operand...  4.11 us
    ppermute x9, waiting for transfers between devices, swap(): return lax.ppermute(a, 'src', [(i, i ^ over) for i in range(n)])  1.71 us
  transfers between devices with their start and end apart: 9, of which 3 were waited for; matrix products, arithmetic and copies ran while one was open for 0% of the time, Pallas kernels for 5%

profile of v9, /device:TPU:0, one launch (start us, length us, event | category | flops | bytes accessed | tf_op | source)
XLA Modules:
  0.0 37.5 jit_solution(6280535837397339202)
XLA Ops:
  0.6 4.1 %collective-permute-start.3 = (bf16[64,256]{1,0:T(8,128)(2,1)}, bf16[64,256]{1,0:T(8,128)(2,1)S(1)}, u32[]{:S(2)}, u32[]{:S(2)}) collective-permute-start(bf16[64,256]{1,0:T(8,128)(2,1)} %refs_4_.1), channel_id=1, source_target_pairs={{0,8},{1,9},{2,10},{3,11},{4,12},{5,13},{6,14},{7,15},{8,0},{9,1},... | collective-permute-start | bytes 98312 | tf_op jit(solution)/shard_map/ppermute | solution.py:216
  4.7 1.7 %collective-permute-start.2 = (bf16[64,256]{1,0:T(8,128)(2,1)}, bf16[64,256]{1,0:T(8,128)(2,1)S(1)}, u32[]{:S(2)}, u32[]{:S(2)}) collective-permute-start(bf16[64,256]{1,0:T(8,128)(2,1)} %refs_4_.1), channel_id=1, source_target_pairs={{0,7},{1,6},{2,5},{3,4},{4,3},{5,2},{6,1},{7,0},{8,15},{9,14},{10,... | collective-permute-start | bytes 98312 | tf_op jit(solution)/shard_map/ppermute | solution.py:216
  6.4 0.4 %collective-permute-start.1 = (bf16[64,256]{1,0:T(8,128)(2,1)}, bf16[64,256]{1,0:T(8,128)(2,1)S(1)}, u32[]{:S(2)}, u32[]{:S(2)}) collective-permute-start(bf16[64,256]{1,0:T(8,128)(2,1)} %refs_4_.1), channel_id=1, source_target_pairs={{0,4},{1,5},{2,6},{3,7},{4,0},{5,1},{6,2},{7,3},{8,12},{9,13},{10,... | collective-permute-start | bytes 98312 | tf_op jit(solution)/shard_map/ppermute | solution.py:216
  6.8 0.8 %collective-permute-start = (bf16[64,256]{1,0:T(8,128)(2,1)}, bf16[64,256]{1,0:T(8,128)(2,1)S(1)}, u32[]{:S(2)}, u32[]{:S(2)}) collective-permute-start(bf16[64,256]{1,0:T(8,128)(2,1)} %refs_4_.1), channel_id=1, source_target_pairs={{0,3},{1,2},{2,1},{3,0},{4,7},{5,6},{6,5},{7,4},{8,11},{9,10},{10,... | collective-permute-start | bytes 98312 | tf_op jit(solution)/shard_map/ppermute | solution.py:216
  7.7 0.0 collective-permute-done.3.refs_0_
  7.7 1.9 %collective-permute-start.6 = (bf16[64,256]{1,0:T(8,128)(2,1)S(1)}, bf16[64,256]{1,0:T(8,128)(2,1)S(1)}, u32[]{:S(2)}, u32[]{:S(2)}) collective-permute-start(bf16[64,256]{1,0:T(8,128)(2,1)S(1)} %collective-permute-done.3.refs_0_), channel_id=1, source_target_pairs={{0,7},{1,6},{2,5},{3,4},{4,3},{5,2},{6,1},{7,0},{8,15},{9,14},{10,... | collective-permute-start | bytes 98312 | tf_op jit(solution)/shard_map/ppermute | solution.py:216
  9.6 0.4 %collective-permute-start.5 = (bf16[64,256]{1,0:T(8,128)(2,1)S(1)}, bf16[64,256]{1,0:T(8,128)(2,1)S(1)}, u32[]{:S(2)}, u32[]{:S(2)}) collective-permute-start(bf16[64,256]{1,0:T(8,128)(2,1)S(1)} %collective-permute-done.3.refs_0_), channel_id=1, source_target_pairs={{0,4},{1,5},{2,6},{3,7},{4,0},{5,1},{6,2},{7,3},{8,12},{9,13},{10,... | collective-permute-start | bytes 98312 | tf_op jit(solution)/shard_map/ppermute | solution.py:216
  10.1 0.0 collective-permute-done.2.refs_2_
  10.1 0.5 %collective-permute-start.4 = (bf16[64,256]{1,0:T(8,128)(2,1)S(1)}, bf16[64,256]{1,0:T(8,128)(2,1)S(1)}, u32[]{:S(2)}, u32[]{:S(2)}) collective-permute-start(bf16[64,256]{1,0:T(8,128)(2,1)S(1)} %collective-permute-done.3.refs_0_), channel_id=1, source_target_pairs={{0,3},{1,2},{2,1},{3,0},{4,7},{5,6},{6,5},{7,4},{8,11},{9,10},{10,... | collective-permute-start | bytes 98312 | tf_op jit(solution)/shard_map/ppermute | solution.py:216
  10.6 0.3 collective-permute-done.1.refs_1_
  10.9 0.0 collective-permute-done.refs_0_
  10.9 1.0 %shard_map.59 = (bf16[512,256]{1,0:T(8,128)(2,1)S(1)}, bf16[256,256]{1,0:T(8,128)(2,1)S(1)}, f32[512,128]{1,0:T(8,128)S(1)}, f32[8,128]{1,0:T(8,128)S(1)}) custom-call(bf16[64,256]{1,0:T(8,128)(2,1)S(1)} %collective-permute-done.refs_0_, bf16[64,256]{1,0:T(8,128)(2,1)S(1)} %collective-permute-done.1.refs_1_, ...), custom_call_target="tpu_custom_call" | custom-call | bytes 524288 | tf_op jit(solution)/shard_map/pallas_call | solution.py:195
  11.9 0.3 collective-permute-start.8
  12.3 0.4 %shard_map.60 = (f32[512,256]{1,0:T(8,128)S(1)}, f32[512,128]{1,0:T(8,128)S(1)}, f32[512,128]{1,0:T(8,128)S(1)}) custom-call(bf16[512,256]{1,0:T(8,128)(2,1)S(1)} %get-tuple-element.22.e_ref, bf16[256,256]{1,0:T(8,128)(2,1)S(1)} %get-tuple-element.23.refs_0_), custom_call_target="tpu_custom_call" | custom-call | flops 67108864 | bytes 524288 | tf_op jit(solution)/shard_map/pallas_call | solution.py:195
  12.7 0.0 collective-permute-done.6.refs_3_
  12.7 0.9 %collective-permute-done.5.refs_2_ = bf16[64,256]{1,0:T(8,128)(2,1)S(1)} collective-permute-done((bf16[64,256]{1,0:T(8,128)(2,1)S(1)}, bf16[64,256]{1,0:T(8,128)(2,1)S(1)}, u32[]{:S(2)}, u32[]{:S(2)}) %collective-permute-start.5) | collective-permute-done | bytes 32800 | tf_op jit(solution)/shard_map/ppermute | solution.py:216
  13.6 0.0 collective-permute-done.4.refs_1_
  13.6 0.3 collective-permute-start.7
  13.9 0.0 collective-permute-done.8.refs_0_
  13.9 0.5 %shard_map.62 = (f32[512,512]{1,0:T(8,128)S(1)}, f32[512,128]{1,0:T(8,128)S(1)}, f32[512,128]{1,0:T(8,128)S(1)}) custom-call(bf16[512,256]{1,0:T(8,128)(2,1)S(1)} %get-tuple-element.22.e_ref, bf16[256,256]{1,0:T(8,128)(2,1)S(1)} %collective-permute-done.8.refs_0_, bf16[256,256]{1,0:T(8,128)(2,1)S(1)} %shard_map.61.refs_1_, ...), custom_call_target="tpu_custom_call" | custom-call | flops 134217728 | bytes 1048576 | tf_op jit(solution)/shard_map/pallas_call | solution.py:195
  14.5 0.6 %collective-permute-done.7.t_ref = bf16[256,256]{1,0:T(8,128)(2,1)S(1)} collective-permute-done((bf16[256,256]{1,0:T(8,128)(2,1)S(1)}, bf16[256,256]{1,0:T(8,128)(2,1)S(1)}, u32[]{:S(2)}, u32[]{:S(2)}) %collective-permute-start.7) | collective-permute-done | bytes 131104 | tf_op jit(solution)/shard_map/ppermute | solution.py:216
  15.0 1.0 %shard_map.63 = (f32[512,1024]{1,0:T(8,128)S(1)}, f32[512,128]{1,0:T(8,128)S(1)}, f32[8,128]{1,0:T(8,128)S(1)}, f32[16,8,128]{2,1,0:T(8,128)S(1)}) custom-call(bf16[512,256]{1,0:T(8,128)(2,1)S(1)} %get-tuple-element.22.e_ref, bf16[256,256]{1,0:T(8,128)(2,1)S(1)} %collective-permute-done.7.t_ref, f32[512,128]{1,0:T(8,128)S(1)} %get-tuple-element.30.max_ref, ...), custom_call_target="tpu_custom_call" | custom-call | tf_op jit(solution)/shard_map/pallas_call | solution.py:195
  16.0 11.4 %all_to_all.16.g_ref = f32[16,8,128]{2,1,0:T(8,128)S(1)} all-to-all(f32[16,8,128]{2,1,0:T(8,128)S(1)} %get-tuple-element.35), channel_id=1, replica_groups=mesh['group'=2,'src'=16] {'src'}, dimensions={0} | all-to-all | bytes 131072 | tf_op jit(solution)/shard_map/all_to_all | solution.py:283
  27.4 0.5 %shard_map.64 = (f32[512,128]{1,0:T(8,128)S(1)}, f32[16,64]{1,0:T(8,128)S(1)}) custom-call(f32[16,8,128]{2,1,0:T(8,128)S(1)} %all_to_all.16.g_ref, f32[512,128]{1,0:T(8,128)S(1)} %get-tuple-element.32.logw_ref, f32[8,128]{1,0:T(8,128)S(1)} %get-tuple-element.36.dlw_ref, f32[512,128]{1,0:T(8,128)S(1)} %get-tuple-element.37.pot_ref, ...), custom_call_target="tpu_custom_call" | custom-call | tf_op jit(solution)/shard_map/pallas_call | solution.py:195
  27.9 9.0 %all_to_all.17 = f32[16,1,64]{2,1,0:T(1,128)S(1)} all-to-all(f32[16,1,64]{2,1,0:T(1,128)S(1)} %bitcast.5), channel_id=1, replica_groups=mesh['group'=2,'src'=16] {'src'}, dimensions={0} | all-to-all | bytes 8192 | tf_op jit(solution)/shard_map/all_to_all | solution.py:290
  36.8 0.6 %shard_map.65 = (f32[512]{0:T(512)}, f32[64]{0:T(128)}) custom-call(f32[16,64]{1,0:T(8,128)S(1)} %bitcast.4, f32[512,128]{1,0:T(8,128)S(1)} %get-tuple-element.41.pot_ref), custom_call_target="tpu_custom_call" | custom-call | tf_op jit(solution)/shard_map/pallas_call | solution.py:195
  (1 shorter events, 0.0 us)
Async XLA Ops:
  0.6 7.0 %collective-permute-start.3 = (bf16[64,256]{1,0:T(8,128)(2,1)}, bf16[64,256]{1,0:T(8,128)(2,1)S(1)}, u32[]{:S(2)}, u32[]{:S(2)}) collective-permute-start(bf16[64,256]{1,0:T(8,128)(2,1)} %refs_4_.1), channel_id=1, source_target_pairs={{0,8},{1,9},{2,10},{3,11},{4,12},{5,13},{6,14},{7,15},{8,0},{9,1},... | collective-permute-start | bytes 98312 | tf_op jit(solution)/shard_map/ppermute | solution.py:216
  4.7 5.3 %collective-permute-start.2 = (bf16[64,256]{1,0:T(8,128)(2,1)}, bf16[64,256]{1,0:T(8,128)(2,1)S(1)}, u32[]{:S(2)}, u32[]{:S(2)}) collective-permute-start(bf16[64,256]{1,0:T(8,128)(2,1)} %refs_4_.1), channel_id=1, source_target_pairs={{0,7},{1,6},{2,5},{3,4},{4,3},{5,2},{6,1},{7,0},{8,15},{9,14},{10,... | collective-permute-start | bytes 98312 | tf_op jit(solution)/shard_map/ppermute | solution.py:216
  6.4 4.5 %collective-permute-start.1 = (bf16[64,256]{1,0:T(8,128)(2,1)}, bf16[64,256]{1,0:T(8,128)(2,1)S(1)}, u32[]{:S(2)}, u32[]{:S(2)}) collective-permute-start(bf16[64,256]{1,0:T(8,128)(2,1)} %refs_4_.1), channel_id=1, source_target_pairs={{0,4},{1,5},{2,6},{3,7},{4,0},{5,1},{6,2},{7,3},{8,12},{9,13},{10,... | collective-permute-start | bytes 98312 | tf_op jit(solution)/shard_map/ppermute | solution.py:216
  6.8 4.0 %collective-permute-start = (bf16[64,256]{1,0:T(8,128)(2,1)}, bf16[64,256]{1,0:T(8,128)(2,1)S(1)}, u32[]{:S(2)}, u32[]{:S(2)}) collective-permute-start(bf16[64,256]{1,0:T(8,128)(2,1)} %refs_4_.1), channel_id=1, source_target_pairs={{0,3},{1,2},{2,1},{3,0},{4,7},{5,6},{6,5},{7,4},{8,11},{9,10},{10,... | collective-permute-start | bytes 98312 | tf_op jit(solution)/shard_map/ppermute | solution.py:216
  7.7 5.0 %collective-permute-start.6 = (bf16[64,256]{1,0:T(8,128)(2,1)S(1)}, bf16[64,256]{1,0:T(8,128)(2,1)S(1)}, u32[]{:S(2)}, u32[]{:S(2)}) collective-permute-start(bf16[64,256]{1,0:T(8,128)(2,1)S(1)} %collective-permute-done.3.refs_0_), channel_id=1, source_target_pairs={{0,7},{1,6},{2,5},{3,4},{4,3},{5,2},{6,1},{7,0},{8,15},{9,14},{10,... | collective-permute-start | bytes 98312 | tf_op jit(solution)/shard_map/ppermute | solution.py:216
  9.6 4.0 %collective-permute-start.5 = (bf16[64,256]{1,0:T(8,128)(2,1)S(1)}, bf16[64,256]{1,0:T(8,128)(2,1)S(1)}, u32[]{:S(2)}, u32[]{:S(2)}) collective-permute-start(bf16[64,256]{1,0:T(8,128)(2,1)S(1)} %collective-permute-done.3.refs_0_), channel_id=1, source_target_pairs={{0,4},{1,5},{2,6},{3,7},{4,0},{5,1},{6,2},{7,3},{8,12},{9,13},{10,... | collective-permute-start | bytes 98312 | tf_op jit(solution)/shard_map/ppermute | solution.py:216
  10.1 3.5 %collective-permute-start.4 = (bf16[64,256]{1,0:T(8,128)(2,1)S(1)}, bf16[64,256]{1,0:T(8,128)(2,1)S(1)}, u32[]{:S(2)}, u32[]{:S(2)}) collective-permute-start(bf16[64,256]{1,0:T(8,128)(2,1)S(1)} %collective-permute-done.3.refs_0_), channel_id=1, source_target_pairs={{0,3},{1,2},{2,1},{3,0},{4,7},{5,6},{6,5},{7,4},{8,11},{9,10},{10,... | collective-permute-start | bytes 98312 | tf_op jit(solution)/shard_map/ppermute | solution.py:216
  11.9 2.0 %collective-permute-start.8 = (bf16[256,256]{1,0:T(8,128)(2,1)S(1)}, bf16[256,256]{1,0:T(8,128)(2,1)S(1)}, u32[]{:S(2)}, u32[]{:S(2)}) collective-permute-start(bf16[256,256]{1,0:T(8,128)(2,1)S(1)} %get-tuple-element.23.refs_0_), channel_id=1, source_target_pairs={{0,1},{1,0},{2,3},{3,2},{4,5},{5,4},{6,7},{7,6},{8,9},{9,8},{10,11... | collective-permute-start | bytes 393224 | tf_op jit(solution)/shard_map/ppermute | solution.py:216
  13.6 1.4 %collective-permute-start.7 = (bf16[256,256]{1,0:T(8,128)(2,1)S(1)}, bf16[256,256]{1,0:T(8,128)(2,1)S(1)}, u32[]{:S(2)}, u32[]{:S(2)}) collective-permute-start(bf16[256,256]{1,0:T(8,128)(2,1)S(1)} %shard_map.61.refs_1_), channel_id=1, source_target_pairs={{0,1},{1,0},{2,3},{3,2},{4,5},{5,4},{6,7},{7,6},{8,9},{9,8},{10,11... | collective-permute-start | bytes 393224 | tf_op jit(solution)/shard_map/ppermute | solution.py:216

commit v10 on v9

--- a/solution.py
+++ b/solution.py
@@ -47,15 +47,77 @@
     ]
 
 
-def load_kernel(n, aways, *refs):
-    got, refs = refs[: len(aways)], refs[len(aways) :]
-    e_hbm, t_hbm, logw_hbm, dlw_hbm, e_ref, t_ref, logw_ref, dlw_ref = refs[:8]
-    row_ref, all_ref, own_ref, sems = refs[8:]
+def load_kernel(t_hbm, t_ref, sem):
+    copy = pltpu.make_async_copy(t_hbm, t_ref, sem)
+    copy.start()
+    copy.wait()
+
+
+def group_kernel(n, aways, *refs):
+    out_ref = refs[-1]
+    mine = lax.rem(lax.axis_index("src"), n // 2) // 2
+    for away, ref in zip(aways, refs[:-1]):
+        per = ref.shape[0]
+        at = pl.multiple_of(jnp.bitwise_xor(mine, away) * per, per)
+        out_ref[pl.ds(at, per), :] = ref[...]
+
+
+def scores_of(e_ref, t, s_ref):
+    width = e_ref.shape[1]
+    s_ref[...] = lax.dot_general(
+        e_ref[...], t, (((1,), (1,)), ((), ())), preferred_element_type=jnp.float32
+    ) * (LOG2E / (STRENGTH * math.sqrt(width)))
+
+
+def chunks_of(ref):
+    return [ref[:, j * LANES : (j + 1) * LANES] for j in range(ref.shape[1] // LANES)]
+
+
+def over_lanes(reduce, parts):
+    whole = reduce(parts)
+    kind = jnp.max if reduce is largest else jnp.sum
+    return jnp.broadcast_to(kind(whole, axis=1, keepdims=True), whole.shape)
+
+
+def largest(parts):
+    return functools.reduce(jnp.maximum, parts)
+
+
+def total(parts):
+    return functools.reduce(jnp.add, parts)
+
+
+def row_sums(parts, before=()):
+    row_max = over_lanes(largest, parts)
+    if before:
+        old_max, old_tot = before[0][...], before[1][...]
+        row_max = jnp.maximum(row_max, old_max)
+    tot = over_lanes(total, [jnp.exp2(p - row_max) for p in parts])
+    if before:
+        tot = tot + old_tot * jnp.exp2(old_max - row_max)
+    return row_max, tot
+
+
+def first_kernel(
+    n,
+    t_ref,
+    e_hbm,
+    logw_hbm,
+    dlw_hbm,
+    e_ref,
+    logw_ref,
+    dlw_ref,
+    s_ref,
+    max_ref,
+    tot_ref,
+    row_ref,
+    all_ref,
+    sems,
+):
     copies = [
         pltpu.make_async_copy(logw_hbm, row_ref, sems.at[0]),
         pltpu.make_async_copy(dlw_hbm, all_ref, sems.at[1]),
-        pltpu.make_async_copy(t_hbm, own_ref, sems.at[2]),
-        pltpu.make_async_copy(e_hbm, e_ref, sems.at[3]),
+        pltpu.make_async_copy(e_hbm, e_ref, sems.at[2]),
     ]
     for copy in copies:
         copy.start()
@@ -71,53 +133,8 @@
     for j in range(dlw_ref.shape[0]):
         dlw_ref[j : j + 1, :] = row[:, j * LANES : (j + 1) * LANES]
     copies[2].wait()
-    group_kernel(n, [0] + aways, own_ref, *got, t_ref)
-    copies[3].wait()
-
-
-def group_kernel(n, aways, *refs):
-    out_ref = refs[-1]
-    mine = lax.rem(lax.axis_index("src"), n // 2) // 2
-    for away, ref in zip(aways, refs[:-1]):
-        per = ref.shape[0]
-        at = pl.multiple_of(jnp.bitwise_xor(mine, away) * per, per)
-        out_ref[pl.ds(at, per), :] = ref[...]
-
-
-def scores_of(e_ref, t, s_ref):
-    width = e_ref.shape[1]
-    s_ref[...] = lax.dot_general(
-        e_ref[...], t, (((1,), (1,)), ((), ())), preferred_element_type=jnp.float32
-    ) * (LOG2E / (STRENGTH * math.sqrt(width)))
-
-
-def chunks_of(ref):
-    return [ref[:, j * LANES : (j + 1) * LANES] for j in range(ref.shape[1] // LANES)]
-
-
-def over_lanes(reduce, parts):
-    whole = reduce(parts)
-    kind = jnp.max if reduce is largest else jnp.sum
-    return jnp.broadcast_to(kind(whole, axis=1, keepdims=True), whole.shape)
-
-
-def largest(parts):
-    return functools.reduce(jnp.maximum, parts)
-
-
-def total(parts):
-    return functools.reduce(jnp.add, parts)
-
-
-def row_sums(parts, before=()):
-    row_max = over_lanes(largest, parts)
-    if before:
-        old_max, old_tot = before[0][...], before[1][...]
-        row_max = jnp.maximum(row_max, old_max)
-    tot = over_lanes(total, [jnp.exp2(p - row_max) for p in parts])
-    if before:
-        tot = tot + old_tot * jnp.exp2(old_max - row_max)
-    return row_max, tot
+    scores_of(e_ref, t_ref[...], s_ref)
+    max_ref[...], tot_ref[...] = row_sums(chunks_of(s_ref))
 
 
 def part_kernel(count, e_ref, *refs):
@@ -190,6 +207,10 @@
     own_ref[...] = pot.reshape(own_ref.shape)
 
 
+def in_hbm(a):
+    return pltpu.with_memory_space_constraint(a, pltpu.HBM)
+
+
 def call(kernel, out_shape, operands, scratch=(), far=(), cost=None):
     vmem, hbm = (pl.BlockSpec(memory_space=space) for space in (pltpu.VMEM, pltpu.HBM))
     return pl.pallas_call(
@@ -200,7 +221,7 @@
         scratch_shapes=list(scratch),
         compiler_params=pltpu.CompilerParams(vmem_limit_bytes=VMEM_LIMIT),
         cost_estimate=cost,
-    )(*operands, *[pltpu.with_memory_space_constraint(a, pltpu.HBM) for a in far])
+    )(*operands, *[in_hbm(a) for a in far])
 
 
 def local(emitter_vectors, targets, src_logw, dst_logw):
@@ -218,6 +239,14 @@
     aways = list(range(1, n // 4))
     partner = swap(targets, n // 2)
     own_wave = [swap(targets, 2 * away) for away in aways]
+    (own_targets,) = call(
+        load_kernel,
+        (shape(targets.shape, targets.dtype),),
+        [],
+        [pltpu.SemaphoreType.DMA],
+        [targets],
+        pl.CostEstimate(flops=0, bytes_accessed=4 * rows * width, transcendentals=0),
+    )
     size = n // 4 * per
 
     def group(own, got):
@@ -227,25 +256,9 @@
             [own] + got,
         )[0]
 
-    emitter, near_own, logw, dlw = call(
-        functools.partial(load_kernel, n, aways),
-        (
-            shape(emitter_vectors.shape, emitter_vectors.dtype),
-            shape((size, width), targets.dtype),
-            shape((rows, LANES), f32),
-            shape((cols // LANES, LANES), f32),
-        ),
-        own_wave,
-        [
-            pltpu.VMEM(src_logw.shape, f32),
-            pltpu.VMEM(dst_logw.shape, f32),
-            pltpu.VMEM(targets.shape, targets.dtype),
-            pltpu.SemaphoreType.DMA((4,)),
-        ],
-        [emitter_vectors, targets, src_logw, dst_logw],
-        pl.CostEstimate(flops=0, bytes_accessed=4 * rows * width, transcendentals=0),
-    )
+    near_own = group(own_targets, own_wave)
     far_own = swap(near_own, 1)
+    partner, own_targets = lax.optimization_barrier((partner, own_targets))
     partner_wave = [swap(partner, 2 * away) for away in aways]
 
     def part(groups, before):
@@ -261,14 +274,36 @@
             ),
         )
 
-    near_scores, *sums = part([near_own], ())
+    columns = shape((cols // LANES, LANES), f32)
+    emitter, logw, dlw, near_scores, *sums = call(
+        functools.partial(first_kernel, n),
+        (
+            shape(emitter_vectors.shape, emitter_vectors.dtype),
+            shape((rows, LANES), f32),
+            columns,
+            shape((rows, size), f32),
+            shape((rows, LANES), f32),
+            shape((rows, LANES), f32),
+        ),
+        [near_own],
+        [
+            pltpu.VMEM(src_logw.shape, f32),
+            pltpu.VMEM(dst_logw.shape, f32),
+            pltpu.SemaphoreType.DMA((3,)),
+        ],
+        [emitter_vectors, src_logw, dst_logw],
+        pl.CostEstimate(
+            flops=2 * rows * size * width,
+            bytes_accessed=rows * size * 4,
+            transcendentals=rows * size,
+        ),
+    )
     *partner_wave, near_scores = lax.optimization_barrier((*partner_wave, near_scores))
     near_other = group(partner, partner_wave)
     far_other = swap(near_other, 1)
     more_scores, *sums = part([far_own, near_other], sums)
     groups = [(0, 0), (1, 0), (0, 1), (1, 1)]
     per_group = size // LANES
-    columns = shape((cols // LANES, LANES), f32)
     kept, first_pot, tops, sent = call(
         functools.partial(final_kernel, n, per_group, groups),
         (

time: 37.7 us -> 37.7 us (level)
  starting transfers between devices: 10.6 us -> 11.8 us
  blocking collectives: 20.4 us -> 19.3 us
  waiting for transfers between devices: 1.71 us -> 0.75 us
  Pallas kernels: 4.11 us -> 4.89 us
    ppermute x9, starting transfers between devices: 10.6 us -> 11.8 us  [swap(): return lax.ppermute(a, 'src', [(i, i ^ over) for i in range(n)])]
    all_to_all x1, blocking collectives: 11.4 us -> 10.3 us  [local(): heard = lax.all_to_all(sent, 'src', 0, 0)]
    ppermute x9, waiting for transfers between devices: 1.71 us -> 0.75 us  [swap(): return lax.ppermute(a, 'src', [(i, i ^ over) for i in range(n)])]
    pallas_call x7 -> x8, Pallas kernels: 4.11 us -> 4.89 us  [call(): pl.pallas_call(kernel, out_shape=out_shape, in_specs=[vmem] * len(operand...]
  transfers between devices with their start and end apart: 9 -> 9, of which waited for: 3 -> 2; matrix products, arithmetic and copies ran while one was open for 0% -> 0% of each run, Pallas kernels for 5% -> 8%
where the time goes in v10:
time: 37.7 us; the launch traced here: 37.4 us
  blocking collectives  19.3 us (51%)
  starting transfers between devices  11.8 us (31%)
  Pallas kernels  4.89 us (13%)
  waiting for transfers between devices  0.75 us (2%)
  between operations  0.69 us (2%)
    ppermute x9, starting transfers between devices, swap(): return lax.ppermute(a, 'src', [(i, i ^ over) for i in range(n)])  11.8 us
    all_to_all x1, blocking collectives, local(): heard = lax.all_to_all(sent, 'src', 0, 0)  10.3 us
    all_to_all x1, blocking collectives, local(): own = lax.all_to_all(parts, 'src', 0, 0)  8.98 us
    pallas_call x8, Pallas kernels, call(): pl.pallas_call(kernel, out_shape=out_shape, in_specs=[vmem] * len(operand...  4.89 us
    ppermute x9, waiting for transfers between devices, swap(): return lax.ppermute(a, 'src', [(i, i ^ over) for i in range(n)])  0.75 us
  transfers between devices with their start and end apart: 9, of which 2 were waited for; matrix products, arithmetic and copies ran while one was open for 0% of the time, Pallas kernels for 8%

profile of v10, /device:TPU:0, one launch (start us, length us, event | category | flops | bytes accessed | tf_op | source)
XLA Modules:
  0.0 37.4 jit_solution(6224538342296560207)
XLA Ops:
  0.6 4.1 %collective-permute-start.3 = (bf16[64,256]{1,0:T(8,128)(2,1)}, bf16[64,256]{1,0:T(8,128)(2,1)S(1)}, u32[]{:S(2)}, u32[]{:S(2)}) collective-permute-start(bf16[64,256]{1,0:T(8,128)(2,1)} %t_hbm.1), channel_id=1, source_target_pairs={{0,8},{1,9},{2,10},{3,11},{4,12},{5,13},{6,14},{7,15},{8,0},{9,1},... | collective-permute-start | bytes 98312 | tf_op jit(solution)/shard_map/ppermute | solution.py:237
  4.7 1.6 %collective-permute-start.1 = (bf16[64,256]{1,0:T(8,128)(2,1)}, bf16[64,256]{1,0:T(8,128)(2,1)S(1)}, u32[]{:S(2)}, u32[]{:S(2)}) collective-permute-start(bf16[64,256]{1,0:T(8,128)(2,1)} %t_hbm.1), channel_id=1, source_target_pairs={{0,4},{1,5},{2,6},{3,7},{4,0},{5,1},{6,2},{7,3},{8,12},{9,13},{10,... | collective-permute-start | bytes 98312 | tf_op jit(solution)/shard_map/ppermute | solution.py:237
  6.3 0.4 collective-permute-start
  6.7 1.3 %collective-permute-start.2 = (bf16[64,256]{1,0:T(8,128)(2,1)}, bf16[64,256]{1,0:T(8,128)(2,1)S(1)}, u32[]{:S(2)}, u32[]{:S(2)}) collective-permute-start(bf16[64,256]{1,0:T(8,128)(2,1)} %t_hbm.1), channel_id=1, source_target_pairs={{0,7},{1,6},{2,5},{3,4},{4,3},{5,2},{6,1},{7,0},{8,15},{9,14},{10,... | collective-permute-start | bytes 98312 | tf_op jit(solution)/shard_map/ppermute | solution.py:237
  7.9 0.8 %shard_map.59.refs_0_ = bf16[64,256]{1,0:T(8,128)(2,1)S(1)} custom-call(bf16[64,256]{1,0:T(8,128)(2,1)} %t_hbm.1), custom_call_target="tpu_custom_call" | custom-call | bytes 524288 | tf_op jit(solution)/shard_map/pallas_call | solution.py:216
  8.7 0.0 collective-permute-done.3.refs_0_
  8.8 1.4 %collective-permute-start.6 = (bf16[64,256]{1,0:T(8,128)(2,1)S(1)}, bf16[64,256]{1,0:T(8,128)(2,1)S(1)}, u32[]{:S(2)}, u32[]{:S(2)}) collective-permute-start(bf16[64,256]{1,0:T(8,128)(2,1)S(1)} %collective-permute-done.3.refs_0_), channel_id=1, source_target_pairs={{0,7},{1,6},{2,5},{3,4},{4,3},{5,2},{6,1},{7,0},{8,15},{9,14},{10,... | collective-permute-start | bytes 98312 | tf_op jit(solution)/shard_map/ppermute | solution.py:237
  10.2 0.4 %collective-permute-start.5 = (bf16[64,256]{1,0:T(8,128)(2,1)S(1)}, bf16[64,256]{1,0:T(8,128)(2,1)S(1)}, u32[]{:S(2)}, u32[]{:S(2)}) collective-permute-start(bf16[64,256]{1,0:T(8,128)(2,1)S(1)} %collective-permute-done.3.refs_0_), channel_id=1, source_target_pairs={{0,4},{1,5},{2,6},{3,7},{4,0},{5,1},{6,2},{7,3},{8,12},{9,13},{10,... | collective-permute-start | bytes 98312 | tf_op jit(solution)/shard_map/ppermute | solution.py:237
  10.7 0.0 collective-permute-done.1.refs_2_
  10.7 1.1 %collective-permute-start.4 = (bf16[64,256]{1,0:T(8,128)(2,1)S(1)}, bf16[64,256]{1,0:T(8,128)(2,1)S(1)}, u32[]{:S(2)}, u32[]{:S(2)}) collective-permute-start(bf16[64,256]{1,0:T(8,128)(2,1)S(1)} %collective-permute-done.3.refs_0_), channel_id=1, source_target_pairs={{0,3},{1,2},{2,1},{3,0},{4,7},{5,6},{6,5},{7,4},{8,11},{9,10},{10,... | collective-permute-start | bytes 98312 | tf_op jit(solution)/shard_map/ppermute | solution.py:237
  11.8 0.0 collective-permute-done.refs_1_
  11.8 0.0 collective-permute-done.2.refs_3_
  11.8 0.7 %collective-permute-start.8 = (bf16[256,256]{1,0:T(8,128)(2,1)S(1)}, bf16[256,256]{1,0:T(8,128)(2,1)S(1)}, u32[]{:S(2)}, u32[]{:S(2)}) collective-permute-start(bf16[256,256]{1,0:T(8,128)(2,1)S(1)} %shard_map.60.t_ref), channel_id=1, source_target_pairs={{0,1},{1,0},{2,3},{3,2},{4,5},{5,4},{6,7},{7,6},{8,9},{9,8},{10,11... | collective-permute-start | bytes 393224 | tf_op jit(solution)/shard_map/ppermute | solution.py:237
  12.4 1.4 %shard_map.61 = (bf16[512,256]{1,0:T(8,128)(2,1)S(1)}, f32[512,128]{1,0:T(8,128)S(1)}, f32[8,128]{1,0:T(8,128)S(1)}, f32[512,256]{1,0:T(8,128)S(1)}, f32[512,128]{1,0:T(8,128)S(1)}, /*index=5*/f32[512,128]{1,0:T(8,128)S(1)}) custom-call(bf16[256,256]{1,0:T(8,128)(2,1)S(1)} %shard_map.60.t_ref, bf16[512,256]{1,0:T(8,128)(2,1)} %e_hbm.1, f32[512]{0:T(512)} %logw_hbm.1, ...), custom_call_target="tpu_custom_call" | custom-call | flops 67108864 | bytes 524288 | tf_op jit(solution)/shard_map/pallas_call | solution.py:216
  13.9 0.0 collective-permute-done.6.refs_3_
  13.9 0.3 collective-permute-done.5.refs_2_
  14.2 0.0 collective-permute-done.4.refs_1_
  14.2 0.8 %collective-permute-start.7 = (bf16[256,256]{1,0:T(8,128)(2,1)S(1)}, bf16[256,256]{1,0:T(8,128)(2,1)S(1)}, u32[]{:S(2)}, u32[]{:S(2)}) collective-permute-start(bf16[256,256]{1,0:T(8,128)(2,1)S(1)} %shard_map.62.refs_1_), channel_id=1, source_target_pairs={{0,1},{1,0},{2,3},{3,2},{4,5},{5,4},{6,7},{7,6},{8,9},{9,8},{10,11... | collective-permute-start | bytes 393224 | tf_op jit(solution)/shard_map/ppermute | solution.py:237
  15.0 0.0 collective-permute-done.8.refs_0_
  15.0 0.5 %shard_map.63 = (f32[512,512]{1,0:T(8,128)S(1)}, f32[512,128]{1,0:T(8,128)S(1)}, f32[512,128]{1,0:T(8,128)S(1)}) custom-call(bf16[512,256]{1,0:T(8,128)(2,1)S(1)} %get-tuple-element.22.e_ref, bf16[256,256]{1,0:T(8,128)(2,1)S(1)} %collective-permute-done.8.refs_0_, bf16[256,256]{1,0:T(8,128)(2,1)S(1)} %shard_map.62.refs_1_, ...), custom_call_target="tpu_custom_call" | custom-call | flops 134217728 | bytes 1048576 | tf_op jit(solution)/shard_map/pallas_call | solution.py:216
  15.6 0.4 %collective-permute-done.7.t_ref = bf16[256,256]{1,0:T(8,128)(2,1)S(1)} collective-permute-done((bf16[256,256]{1,0:T(8,128)(2,1)S(1)}, bf16[256,256]{1,0:T(8,128)(2,1)S(1)}, u32[]{:S(2)}, u32[]{:S(2)}) %collective-permute-start.7) | collective-permute-done | bytes 131104 | tf_op jit(solution)/shard_map/ppermute | solution.py:237
  16.0 0.9 %shard_map.64 = (f32[512,1024]{1,0:T(8,128)S(1)}, f32[512,128]{1,0:T(8,128)S(1)}, f32[8,128]{1,0:T(8,128)S(1)}, f32[16,8,128]{2,1,0:T(8,128)S(1)}) custom-call(bf16[512,256]{1,0:T(8,128)(2,1)S(1)} %get-tuple-element.22.e_ref, bf16[256,256]{1,0:T(8,128)(2,1)S(1)} %collective-permute-done.7.t_ref, f32[512,128]{1,0:T(8,128)S(1)} %get-tuple-element.30.max_ref, ...), custom_call_target="tpu_custom_call" | custom-call | tf_op jit(solution)/shard_map/pallas_call | solution.py:216
  17.0 10.3 %all_to_all.16.g_ref = f32[16,8,128]{2,1,0:T(8,128)S(1)} all-to-all(f32[16,8,128]{2,1,0:T(8,128)S(1)} %get-tuple-element.35), channel_id=1, replica_groups=mesh['group'=2,'src'=16] {'src'}, dimensions={0} | all-to-all | bytes 131072 | tf_op jit(solution)/shard_map/all_to_all | solution.py:318
  27.3 0.5 %shard_map.65 = (f32[512,128]{1,0:T(8,128)S(1)}, f32[16,64]{1,0:T(8,128)S(1)}) custom-call(f32[16,8,128]{2,1,0:T(8,128)S(1)} %all_to_all.16.g_ref, f32[512,128]{1,0:T(8,128)S(1)} %get-tuple-element.32.logw_ref, f32[8,128]{1,0:T(8,128)S(1)} %get-tuple-element.36.dlw_ref, f32[512,128]{1,0:T(8,128)S(1)} %get-tuple-element.37.pot_ref, ...), custom_call_target="tpu_custom_call" | custom-call | tf_op jit(solution)/shard_map/pallas_call | solution.py:216
  27.8 9.0 %all_to_all.17 = f32[16,1,64]{2,1,0:T(1,128)S(1)} all-to-all(f32[16,1,64]{2,1,0:T(1,128)S(1)} %bitcast.5), channel_id=1, replica_groups=mesh['group'=2,'src'=16] {'src'}, dimensions={0} | all-to-all | bytes 8192 | tf_op jit(solution)/shard_map/all_to_all | solution.py:325
  36.8 0.6 %shard_map.66 = (f32[512]{0:T(512)}, f32[64]{0:T(128)}) custom-call(f32[16,64]{1,0:T(8,128)S(1)} %bitcast.4, f32[512,128]{1,0:T(8,128)S(1)} %get-tuple-element.41.pot_ref), custom_call_target="tpu_custom_call" | custom-call | tf_op jit(solution)/shard_map/pallas_call | solution.py:216
  (2 shorter events, 0.0 us)
Async XLA Ops:
  0.6 8.1 %collective-permute-start.3 = (bf16[64,256]{1,0:T(8,128)(2,1)}, bf16[64,256]{1,0:T(8,128)(2,1)S(1)}, u32[]{:S(2)}, u32[]{:S(2)}) collective-permute-start(bf16[64,256]{1,0:T(8,128)(2,1)} %t_hbm.1), channel_id=1, source_target_pairs={{0,8},{1,9},{2,10},{3,11},{4,12},{5,13},{6,14},{7,15},{8,0},{9,1},... | collective-permute-start | bytes 98312 | tf_op jit(solution)/shard_map/ppermute | solution.py:237
  4.7 5.9 %collective-permute-start.1 = (bf16[64,256]{1,0:T(8,128)(2,1)}, bf16[64,256]{1,0:T(8,128)(2,1)S(1)}, u32[]{:S(2)}, u32[]{:S(2)}) collective-permute-start(bf16[64,256]{1,0:T(8,128)(2,1)} %t_hbm.1), channel_id=1, source_target_pairs={{0,4},{1,5},{2,6},{3,7},{4,0},{5,1},{6,2},{7,3},{8,12},{9,13},{10,... | collective-permute-start | bytes 98312 | tf_op jit(solution)/shard_map/ppermute | solution.py:237
  6.3 5.5 %collective-permute-start = (bf16[64,256]{1,0:T(8,128)(2,1)}, bf16[64,256]{1,0:T(8,128)(2,1)S(1)}, u32[]{:S(2)}, u32[]{:S(2)}) collective-permute-start(bf16[64,256]{1,0:T(8,128)(2,1)} %t_hbm.1), channel_id=1, source_target_pairs={{0,3},{1,2},{2,1},{3,0},{4,7},{5,6},{6,5},{7,4},{8,11},{9,10},{10,... | collective-permute-start | bytes 98312 | tf_op jit(solution)/shard_map/ppermute | solution.py:237
  6.7 5.1 %collective-permute-start.2 = (bf16[64,256]{1,0:T(8,128)(2,1)}, bf16[64,256]{1,0:T(8,128)(2,1)S(1)}, u32[]{:S(2)}, u32[]{:S(2)}) collective-permute-start(bf16[64,256]{1,0:T(8,128)(2,1)} %t_hbm.1), channel_id=1, source_target_pairs={{0,7},{1,6},{2,5},{3,4},{4,3},{5,2},{6,1},{7,0},{8,15},{9,14},{10,... | collective-permute-start | bytes 98312 | tf_op jit(solution)/shard_map/ppermute | solution.py:237
  8.8 5.1 %collective-permute-start.6 = (bf16[64,256]{1,0:T(8,128)(2,1)S(1)}, bf16[64,256]{1,0:T(8,128)(2,1)S(1)}, u32[]{:S(2)}, u32[]{:S(2)}) collective-permute-start(bf16[64,256]{1,0:T(8,128)(2,1)S(1)} %collective-permute-done.3.refs_0_), channel_id=1, source_target_pairs={{0,7},{1,6},{2,5},{3,4},{4,3},{5,2},{6,1},{7,0},{8,15},{9,14},{10,... | collective-permute-start | bytes 98312 | tf_op jit(solution)/shard_map/ppermute | solution.py:237
  10.2 4.0 %collective-permute-start.5 = (bf16[64,256]{1,0:T(8,128)(2,1)S(1)}, bf16[64,256]{1,0:T(8,128)(2,1)S(1)}, u32[]{:S(2)}, u32[]{:S(2)}) collective-permute-start(bf16[64,256]{1,0:T(8,128)(2,1)S(1)} %collective-permute-done.3.refs_0_), channel_id=1, source_target_pairs={{0,4},{1,5},{2,6},{3,7},{4,0},{5,1},{6,2},{7,3},{8,12},{9,13},{10,... | collective-permute-start | bytes 98312 | tf_op jit(solution)/shard_map/ppermute | solution.py:237
  10.7 3.5 %collective-permute-start.4 = (bf16[64,256]{1,0:T(8,128)(2,1)S(1)}, bf16[64,256]{1,0:T(8,128)(2,1)S(1)}, u32[]{:S(2)}, u32[]{:S(2)}) collective-permute-start(bf16[64,256]{1,0:T(8,128)(2,1)S(1)} %collective-permute-done.3.refs_0_), channel_id=1, source_target_pairs={{0,3},{1,2},{2,1},{3,0},{4,7},{5,6},{6,5},{7,4},{8,11},{9,10},{10,... | collective-permute-start | bytes 98312 | tf_op jit(solution)/shard_map/ppermute | solution.py:237
  11.8 3.3 %collective-permute-start.8 = (bf16[256,256]{1,0:T(8,128)(2,1)S(1)}, bf16[256,256]{1,0:T(8,128)(2,1)S(1)}, u32[]{:S(2)}, u32[]{:S(2)}) collective-permute-start(bf16[256,256]{1,0:T(8,128)(2,1)S(1)} %shard_map.60.t_ref), channel_id=1, source_target_pairs={{0,1},{1,0},{2,3},{3,2},{4,5},{5,4},{6,7},{7,6},{8,9},{9,8},{10,11... | collective-permute-start | bytes 393224 | tf_op jit(solution)/shard_map/ppermute | solution.py:237
  14.2 1.8 %collective-permute-start.7 = (bf16[256,256]{1,0:T(8,128)(2,1)S(1)}, bf16[256,256]{1,0:T(8,128)(2,1)S(1)}, u32[]{:S(2)}, u32[]{:S(2)}) collective-permute-start(bf16[256,256]{1,0:T(8,128)(2,1)S(1)} %shard_map.62.refs_1_), channel_id=1, source_target_pairs={{0,1},{1,0},{2,3},{3,2},{4,5},{5,4},{6,7},{7,6},{8,9},{9,8},{10,11... | collective-permute-start | bytes 393224 | tf_op jit(solution)/shard_map/ppermute | solution.py:237

commit v11 on v8

--- a/solution.py
+++ b/solution.py
@@ -166,9 +166,9 @@
     rows = rows_of(n, per_group, groups)
     parts = chunks_of(kept_ref)
     tot = over_lanes(total, [p * cols_ref[pl.ds(row, 1), :] for p, row in zip(parts, rows)])
-    logw = logw_ref[...]
-    src_ref[...] = logw + pot_ref[...] - jnp.log2(tot)
-    scale = jnp.exp2(logw) / tot
+    rate = logw_ref[...] - jnp.log2(tot)
+    src_ref[...] = pot_ref[...] + rate
+    scale = jnp.exp2(rate)
     for part, row in zip(parts, rows):
         cols_ref[pl.ds(row, 1), :] = jnp.sum(part * scale, axis=0, keepdims=True)
     cols_ref[...] = top_ref[...] + jnp.log2(cols_ref[...]) - dlw_ref[...]
@@ -255,11 +255,6 @@
             functools.partial(part_kernel, len(groups)),
             (shape((rows, wide), f32), shape((rows, LANES), f32), shape((rows, LANES), f32)),
             [emitter, *groups, *before],
-            cost=pl.CostEstimate(
-                flops=2 * rows * wide * width,
-                bytes_accessed=rows * wide * 4,
-                transcendentals=rows * wide,
-            ),
         )
 
     near_scores, *sums = part([near_own], ())

time: 37.7 us -> 37.7 us (level)
  no operation moved by 1% of the time
where the time goes in v11:
time: 37.7 us; the launch traced here: 37.4 us
  blocking collectives  19.1 us (51%)
  starting transfers between devices  11.5 us (31%)
  Pallas kernels  4.12 us (11%)
  waiting for transfers between devices  2.03 us (5%)
  between operations  0.68 us (2%)
    ppermute x9, starting transfers between devices, swap(): return lax.ppermute(a, 'src', [(i, i ^ over) for i in range(n)])  11.5 us
    all_to_all x1, blocking collectives, local(): heard = lax.all_to_all(sent, 'src', 0, 0)  10.1 us
    all_to_all x1, blocking collectives, local(): own = lax.all_to_all(parts, 'src', 0, 0)  8.98 us
    pallas_call x8, Pallas kernels, call(): pl.pallas_call(kernel, out_shape=out_shape, in_specs=[pl.BlockSpec(memory...  4.12 us
    ppermute x9, waiting for transfers between devices, swap(): return lax.ppermute(a, 'src', [(i, i ^ over) for i in range(n)])  2.03 us
  transfers between devices with their start and end apart: 9, of which 3 were waited for; matrix products, arithmetic and copies ran while one was open for 0% of the time, Pallas kernels for 5%

profile of v11, /device:TPU:0, one launch (start us, length us, event | category | flops | bytes accessed | tf_op | source)
XLA Modules:
  0.0 37.4 jit_solution(16500750841543752270)
XLA Ops:
  0.6 4.1 %collective-permute-start = (bf16[64,256]{1,0:T(8,128)(2,1)}, bf16[64,256]{1,0:T(8,128)(2,1)S(1)}, u32[]{:S(2)}, u32[]{:S(2)}) collective-permute-start(bf16[64,256]{1,0:T(8,128)(2,1)} %t_hbm.1), channel_id=1, source_target_pairs={{0,8},{1,9},{2,10},{3,11},{4,12},{5,13},{6,14},{7,15},{8,0},{9,1},... | collective-permute-start | bytes 98312 | tf_op jit(solution)/shard_map/ppermute | solution.py:213
  4.7 0.7 %collective-permute-start.4 = (bf16[64,256]{1,0:T(8,128)(2,1)}, bf16[64,256]{1,0:T(8,128)(2,1)S(1)}, u32[]{:S(2)}, u32[]{:S(2)}) collective-permute-start(bf16[64,256]{1,0:T(8,128)(2,1)} %t_hbm.1), channel_id=1, source_target_pairs={{0,3},{1,2},{2,1},{3,0},{4,7},{5,6},{6,5},{7,4},{8,11},{9,10},{10,... | collective-permute-start | bytes 98312 | tf_op jit(solution)/shard_map/ppermute | solution.py:213
  5.4 2.1 %collective-permute-start.6 = (bf16[64,256]{1,0:T(8,128)(2,1)}, bf16[64,256]{1,0:T(8,128)(2,1)S(1)}, u32[]{:S(2)}, u32[]{:S(2)}) collective-permute-start(bf16[64,256]{1,0:T(8,128)(2,1)} %t_hbm.1), channel_id=1, source_target_pairs={{0,7},{1,6},{2,5},{3,4},{4,3},{5,2},{6,1},{7,0},{8,15},{9,14},{10,... | collective-permute-start | bytes 98312 | tf_op jit(solution)/shard_map/ppermute | solution.py:213
  7.5 0.4 %collective-permute-start.5 = (bf16[64,256]{1,0:T(8,128)(2,1)}, bf16[64,256]{1,0:T(8,128)(2,1)S(1)}, u32[]{:S(2)}, u32[]{:S(2)}) collective-permute-start(bf16[64,256]{1,0:T(8,128)(2,1)} %t_hbm.1), channel_id=1, source_target_pairs={{0,4},{1,5},{2,6},{3,7},{4,0},{5,1},{6,2},{7,3},{8,12},{9,13},{10,... | collective-permute-start | bytes 98312 | tf_op jit(solution)/shard_map/ppermute | solution.py:213
  7.9 1.0 %shard_map.59 = (bf16[512,256]{1,0:T(8,128)(2,1)S(1)}, bf16[64,256]{1,0:T(8,128)(2,1)S(1)}, f32[512,128]{1,0:T(8,128)S(1)}, f32[8,128]{1,0:T(8,128)S(1)}) custom-call(bf16[512,256]{1,0:T(8,128)(2,1)} %e_hbm.1, bf16[64,256]{1,0:T(8,128)(2,1)} %t_hbm.1, f32[512]{0:T(512)} %logw_hbm.1, f32[1024]{0:T(1024)} %dlw_hbm.1), custom_call_target="tpu_custom_call" | custom-call | bytes 524288 | tf_op jit(solution)/shard_map/pallas_call | solution.py:192
  9.0 0.0 collective-permute-done.refs_0_
  9.0 1.4 %collective-permute-start.3 = (bf16[64,256]{1,0:T(8,128)(2,1)S(1)}, bf16[64,256]{1,0:T(8,128)(2,1)S(1)}, u32[]{:S(2)}, u32[]{:S(2)}) collective-permute-start(bf16[64,256]{1,0:T(8,128)(2,1)S(1)} %collective-permute-done.refs_0_), channel_id=1, source_target_pairs={{0,7},{1,6},{2,5},{3,4},{4,3},{5,2},{6,1},{7,0},{8,15},{9,14},{10,... | collective-permute-start | bytes 98312 | tf_op jit(solution)/shard_map/ppermute | solution.py:213
  10.4 0.4 %collective-permute-start.2 = (bf16[64,256]{1,0:T(8,128)(2,1)S(1)}, bf16[64,256]{1,0:T(8,128)(2,1)S(1)}, u32[]{:S(2)}, u32[]{:S(2)}) collective-permute-start(bf16[64,256]{1,0:T(8,128)(2,1)S(1)} %collective-permute-done.refs_0_), channel_id=1, source_target_pairs={{0,4},{1,5},{2,6},{3,7},{4,0},{5,1},{6,2},{7,3},{8,12},{9,13},{10,... | collective-permute-start | bytes 98312 | tf_op jit(solution)/shard_map/ppermute | solution.py:213
  10.9 0.0 collective-permute-done.4.refs_1_
  10.9 1.1 %collective-permute-start.1 = (bf16[64,256]{1,0:T(8,128)(2,1)S(1)}, bf16[64,256]{1,0:T(8,128)(2,1)S(1)}, u32[]{:S(2)}, u32[]{:S(2)}) collective-permute-start(bf16[64,256]{1,0:T(8,128)(2,1)S(1)} %collective-permute-done.refs_0_), channel_id=1, source_target_pairs={{0,3},{1,2},{2,1},{3,0},{4,7},{5,6},{6,5},{7,4},{8,11},{9,10},{10,... | collective-permute-start | bytes 98312 | tf_op jit(solution)/shard_map/ppermute | solution.py:213
  12.0 0.0 collective-permute-done.6.refs_3_
  12.0 0.0 collective-permute-done.5.refs_2_
  12.0 0.4 %collective-permute-start.8 = (bf16[256,256]{1,0:T(8,128)(2,1)S(1)}, bf16[256,256]{1,0:T(8,128)(2,1)S(1)}, u32[]{:S(2)}, u32[]{:S(2)}) collective-permute-start(bf16[256,256]{1,0:T(8,128)(2,1)S(1)} %shard_map.60.refs_0_), channel_id=1, source_target_pairs={{0,1},{1,0},{2,3},{3,2},{4,5},{5,4},{6,7},{7,6},{8,9},{9,8},{10,11... | collective-permute-start | bytes 393224 | tf_op jit(solution)/shard_map/ppermute | solution.py:213
  12.4 0.4 %shard_map.61 = (f32[512,256]{1,0:T(8,128)S(1)}, f32[512,128]{1,0:T(8,128)S(1)}, f32[512,128]{1,0:T(8,128)S(1)}) custom-call(bf16[512,256]{1,0:T(8,128)(2,1)S(1)} %get-tuple-element.25.e_ref, bf16[256,256]{1,0:T(8,128)(2,1)S(1)} %shard_map.60.refs_0_), custom_call_target="tpu_custom_call" | custom-call | tf_op jit(solution)/shard_map/pallas_call | solution.py:192
  12.9 0.6 %collective-permute-done.3.refs_3_ = bf16[64,256]{1,0:T(8,128)(2,1)S(1)} collective-permute-done((bf16[64,256]{1,0:T(8,128)(2,1)S(1)}, bf16[64,256]{1,0:T(8,128)(2,1)S(1)}, u32[]{:S(2)}, u32[]{:S(2)}) %collective-permute-start.3) | collective-permute-done | bytes 32800 | tf_op jit(solution)/shard_map/ppermute | solution.py:213
  13.5 1.0 %collective-permute-done.2.refs_2_ = bf16[64,256]{1,0:T(8,128)(2,1)S(1)} collective-permute-done((bf16[64,256]{1,0:T(8,128)(2,1)S(1)}, bf16[64,256]{1,0:T(8,128)(2,1)S(1)}, u32[]{:S(2)}, u32[]{:S(2)}) %collective-permute-start.2) | collective-permute-done | bytes 32800 | tf_op jit(solution)/shard_map/ppermute | solution.py:213
  14.4 0.0 collective-permute-done.1.refs_1_
  14.5 0.8 %collective-permute-start.7 = (bf16[256,256]{1,0:T(8,128)(2,1)S(1)}, bf16[256,256]{1,0:T(8,128)(2,1)S(1)}, u32[]{:S(2)}, u32[]{:S(2)}) collective-permute-start(bf16[256,256]{1,0:T(8,128)(2,1)S(1)} %shard_map.62.refs_1_), channel_id=1, source_target_pairs={{0,1},{1,0},{2,3},{3,2},{4,5},{5,4},{6,7},{7,6},{8,9},{9,8},{10,11... | collective-permute-start | bytes 393224 | tf_op jit(solution)/shard_map/ppermute | solution.py:213
  15.3 0.0 collective-permute-done.8.refs_0_
  15.3 0.5 %shard_map.63 = (f32[512,512]{1,0:T(8,128)S(1)}, f32[512,128]{1,0:T(8,128)S(1)}, f32[512,128]{1,0:T(8,128)S(1)}) custom-call(bf16[512,256]{1,0:T(8,128)(2,1)S(1)} %get-tuple-element.25.e_ref, bf16[256,256]{1,0:T(8,128)(2,1)S(1)} %collective-permute-done.8.refs_0_, bf16[256,256]{1,0:T(8,128)(2,1)S(1)} %shard_map.62.refs_1_, ...), custom_call_target="tpu_custom_call" | custom-call | tf_op jit(solution)/shard_map/pallas_call | solution.py:192
  15.8 0.4 %collective-permute-done.7.t_ref = bf16[256,256]{1,0:T(8,128)(2,1)S(1)} collective-permute-done((bf16[256,256]{1,0:T(8,128)(2,1)S(1)}, bf16[256,256]{1,0:T(8,128)(2,1)S(1)}, u32[]{:S(2)}, u32[]{:S(2)}) %collective-permute-start.7) | collective-permute-done | bytes 131104 | tf_op jit(solution)/shard_map/ppermute | solution.py:213
  16.3 1.0 %shard_map.64 = (f32[512,1024]{1,0:T(8,128)S(1)}, f32[512,128]{1,0:T(8,128)S(1)}, f32[8,128]{1,0:T(8,128)S(1)}, f32[16,8,128]{2,1,0:T(8,128)S(1)}) custom-call(bf16[512,256]{1,0:T(8,128)(2,1)S(1)} %get-tuple-element.25.e_ref, bf16[256,256]{1,0:T(8,128)(2,1)S(1)} %collective-permute-done.7.t_ref, f32[512,128]{1,0:T(8,128)S(1)} %get-tuple-element.34.max_ref, ...), custom_call_target="tpu_custom_call" | custom-call | tf_op jit(solution)/shard_map/pallas_call | solution.py:192
  17.2 10.1 %all_to_all.16.g_ref = f32[16,8,128]{2,1,0:T(8,128)S(1)} all-to-all(f32[16,8,128]{2,1,0:T(8,128)S(1)} %get-tuple-element.39), channel_id=1, replica_groups=mesh['group'=2,'src'=16] {'src'}, dimensions={0} | all-to-all | bytes 131072 | tf_op jit(solution)/shard_map/all_to_all | solution.py:279
  27.3 0.5 %shard_map.65 = (f32[512,128]{1,0:T(8,128)S(1)}, f32[16,64]{1,0:T(8,128)S(1)}) custom-call(f32[16,8,128]{2,1,0:T(8,128)S(1)} %all_to_all.16.g_ref, f32[512,128]{1,0:T(8,128)S(1)} %get-tuple-element.36.logw_ref, f32[8,128]{1,0:T(8,128)S(1)} %get-tuple-element.40.dlw_ref, f32[512,128]{1,0:T(8,128)S(1)} %get-tuple-element.41.pot_ref, ...), custom_call_target="tpu_custom_call" | custom-call | tf_op jit(solution)/shard_map/pallas_call | solution.py:192
  27.8 9.0 %all_to_all.17 = f32[16,1,64]{2,1,0:T(1,128)S(1)} all-to-all(f32[16,1,64]{2,1,0:T(1,128)S(1)} %bitcast.5), channel_id=1, replica_groups=mesh['group'=2,'src'=16] {'src'}, dimensions={0} | all-to-all | bytes 8192 | tf_op jit(solution)/shard_map/all_to_all | solution.py:286
  36.8 0.6 %shard_map.66 = (f32[512]{0:T(512)}, f32[64]{0:T(128)}) custom-call(f32[16,64]{1,0:T(8,128)S(1)} %bitcast.4, f32[512,128]{1,0:T(8,128)S(1)} %get-tuple-element.45.pot_ref), custom_call_target="tpu_custom_call" | custom-call | tf_op jit(solution)/shard_map/pallas_call | solution.py:192
  (2 shorter events, 0.0 us)
Async XLA Ops:
  0.6 8.4 %collective-permute-start = (bf16[64,256]{1,0:T(8,128)(2,1)}, bf16[64,256]{1,0:T(8,128)(2,1)S(1)}, u32[]{:S(2)}, u32[]{:S(2)}) collective-permute-start(bf16[64,256]{1,0:T(8,128)(2,1)} %t_hbm.1), channel_id=1, source_target_pairs={{0,8},{1,9},{2,10},{3,11},{4,12},{5,13},{6,14},{7,15},{8,0},{9,1},... | collective-permute-start | bytes 98312 | tf_op jit(solution)/shard_map/ppermute | solution.py:213
  4.7 6.2 %collective-permute-start.4 = (bf16[64,256]{1,0:T(8,128)(2,1)}, bf16[64,256]{1,0:T(8,128)(2,1)S(1)}, u32[]{:S(2)}, u32[]{:S(2)}) collective-permute-start(bf16[64,256]{1,0:T(8,128)(2,1)} %t_hbm.1), channel_id=1, source_target_pairs={{0,3},{1,2},{2,1},{3,0},{4,7},{5,6},{6,5},{7,4},{8,11},{9,10},{10,... | collective-permute-start | bytes 98312 | tf_op jit(solution)/shard_map/ppermute | solution.py:213
  5.4 6.6 %collective-permute-start.6 = (bf16[64,256]{1,0:T(8,128)(2,1)}, bf16[64,256]{1,0:T(8,128)(2,1)S(1)}, u32[]{:S(2)}, u32[]{:S(2)}) collective-permute-start(bf16[64,256]{1,0:T(8,128)(2,1)} %t_hbm.1), channel_id=1, source_target_pairs={{0,7},{1,6},{2,5},{3,4},{4,3},{5,2},{6,1},{7,0},{8,15},{9,14},{10,... | collective-permute-start | bytes 98312 | tf_op jit(solution)/shard_map/ppermute | solution.py:213
  7.5 4.5 %collective-permute-start.5 = (bf16[64,256]{1,0:T(8,128)(2,1)}, bf16[64,256]{1,0:T(8,128)(2,1)S(1)}, u32[]{:S(2)}, u32[]{:S(2)}) collective-permute-start(bf16[64,256]{1,0:T(8,128)(2,1)} %t_hbm.1), channel_id=1, source_target_pairs={{0,4},{1,5},{2,6},{3,7},{4,0},{5,1},{6,2},{7,3},{8,12},{9,13},{10,... | collective-permute-start | bytes 98312 | tf_op jit(solution)/shard_map/ppermute | solution.py:213
  9.0 4.5 %collective-permute-start.3 = (bf16[64,256]{1,0:T(8,128)(2,1)S(1)}, bf16[64,256]{1,0:T(8,128)(2,1)S(1)}, u32[]{:S(2)}, u32[]{:S(2)}) collective-permute-start(bf16[64,256]{1,0:T(8,128)(2,1)S(1)} %collective-permute-done.refs_0_), channel_id=1, source_target_pairs={{0,7},{1,6},{2,5},{3,4},{4,3},{5,2},{6,1},{7,0},{8,15},{9,14},{10,... | collective-permute-start | bytes 98312 | tf_op jit(solution)/shard_map/ppermute | solution.py:213
  10.4 4.0 %collective-permute-start.2 = (bf16[64,256]{1,0:T(8,128)(2,1)S(1)}, bf16[64,256]{1,0:T(8,128)(2,1)S(1)}, u32[]{:S(2)}, u32[]{:S(2)}) collective-permute-start(bf16[64,256]{1,0:T(8,128)(2,1)S(1)} %collective-permute-done.refs_0_), channel_id=1, source_target_pairs={{0,4},{1,5},{2,6},{3,7},{4,0},{5,1},{6,2},{7,3},{8,12},{9,13},{10,... | collective-permute-start | bytes 98312 | tf_op jit(solution)/shard_map/ppermute | solution.py:213
  10.9 3.5 %collective-permute-start.1 = (bf16[64,256]{1,0:T(8,128)(2,1)S(1)}, bf16[64,256]{1,0:T(8,128)(2,1)S(1)}, u32[]{:S(2)}, u32[]{:S(2)}) collective-permute-start(bf16[64,256]{1,0:T(8,128)(2,1)S(1)} %collective-permute-done.refs_0_), channel_id=1, source_target_pairs={{0,3},{1,2},{2,1},{3,0},{4,7},{5,6},{6,5},{7,4},{8,11},{9,10},{10,... | collective-permute-start | bytes 98312 | tf_op jit(solution)/shard_map/ppermute | solution.py:213
  12.0 3.3 %collective-permute-start.8 = (bf16[256,256]{1,0:T(8,128)(2,1)S(1)}, bf16[256,256]{1,0:T(8,128)(2,1)S(1)}, u32[]{:S(2)}, u32[]{:S(2)}) collective-permute-start(bf16[256,256]{1,0:T(8,128)(2,1)S(1)} %shard_map.60.refs_0_), channel_id=1, source_target_pairs={{0,1},{1,0},{2,3},{3,2},{4,5},{5,4},{6,7},{7,6},{8,9},{9,8},{10,11... | collective-permute-start | bytes 393224 | tf_op jit(solution)/shard_map/ppermute | solution.py:213
  14.5 1.8 %collective-permute-start.7 = (bf16[256,256]{1,0:T(8,128)(2,1)S(1)}, bf16[256,256]{1,0:T(8,128)(2,1)S(1)}, u32[]{:S(2)}, u32[]{:S(2)}) collective-permute-start(bf16[256,256]{1,0:T(8,128)(2,1)S(1)} %shard_map.62.refs_1_), channel_id=1, source_target_pairs={{0,1},{1,0},{2,3},{3,2},{4,5},{5,4},{6,7},{7,6},{8,9},{9,8},{10,11... | collective-permute-start | bytes 393224 | tf_op jit(solution)/shard_map/ppermute | solution.py:213

commit v12 on v8

--- a/solution.py
+++ b/solution.py
@@ -178,22 +178,30 @@
         out_ref[d : d + 1, :] = cols_ref[row : row + 1, lane : lane + per]
 
 
-def last_kernel(g_ref, pot_ref, src_ref, own_ref):
+def last_kernel(g_ref, pot_ref, src_hbm, own_hbm, src_ref, own_ref, sems):
     for k in range(src_ref.shape[0] // LANES):
         part = slice(k * LANES, (k + 1) * LANES)
         src_ref[part] = (to_row(pot_ref[part, :]) * LN2).reshape(LANES)
+    src_copy = pltpu.make_async_copy(src_ref, src_hbm, sems.at[0])
+    src_copy.start()
     g = g_ref[...]
     top = jnp.max(g, axis=0, keepdims=True)
     pot = -(top + jnp.log2(jnp.sum(jnp.exp2(g - top), axis=0, keepdims=True))) * LN2
     own_ref[...] = pot.reshape(own_ref.shape)
-
-
-def call(kernel, out_shape, operands, scratch=(), space=pltpu.VMEM, cost=None):
+    own_copy = pltpu.make_async_copy(own_ref, own_hbm, sems.at[1])
+    own_copy.start()
+    src_copy.wait()
+    own_copy.wait()
+
+
+def call(
+    kernel, out_shape, operands, scratch=(), space=pltpu.VMEM, cost=None, out_space=pltpu.VMEM
+):
     return pl.pallas_call(
         kernel,
         out_shape=out_shape,
         in_specs=[pl.BlockSpec(memory_space=space)] * len(operands),
-        out_specs=jax.tree.map(lambda _: pl.BlockSpec(memory_space=pltpu.VMEM), out_shape),
+        out_specs=jax.tree.map(lambda _: pl.BlockSpec(memory_space=out_space), out_shape),
         scratch_shapes=list(scratch),
         compiler_params=pltpu.CompilerParams(vmem_limit_bytes=VMEM_LIMIT),
         cost_estimate=cost,
@@ -289,7 +297,17 @@
         [pltpu.VMEM(columns.shape, f32)],
     )
     own = lax.all_to_all(parts, "src", 0, 0)
-    return call(last_kernel, (shape((rows,), f32), shape((per,), f32)), [own, pot])
+    return call(
+        last_kernel,
+        (shape((rows,), f32), shape((per,), f32)),
+        [own, pot],
+        [
+            pltpu.VMEM((rows,), f32),
+            pltpu.VMEM((per,), f32),
+            pltpu.SemaphoreType.DMA((2,)),
+        ],
+        out_space=pltpu.HBM,
+    )
 
 
 def solution(mesh):

time: 37.7 us -> 37.7 us (level)
  no operation moved by 1% of the time
where the time goes in v12:
time: 37.7 us; the launch traced here: 37.4 us
  blocking collectives  19.1 us (51%)
  starting transfers between devices  11.5 us (31%)
  Pallas kernels  4.12 us (11%)
  waiting for transfers between devices  2.03 us (5%)
  between operations  0.68 us (2%)
    ppermute x9, starting transfers between devices, swap(): return lax.ppermute(a, 'src', [(i, i ^ over) for i in range(n)])  11.5 us
    all_to_all x1, blocking collectives, local(): heard = lax.all_to_all(sent, 'src', 0, 0)  10.1 us
    all_to_all x1, blocking collectives, local(): own = lax.all_to_all(parts, 'src', 0, 0)  8.98 us
    pallas_call x8, Pallas kernels, call(): pl.pallas_call(kernel, out_shape=out_shape, in_specs=[pl.BlockSpec(memory...  4.12 us
    ppermute x9, waiting for transfers between devices, swap(): return lax.ppermute(a, 'src', [(i, i ^ over) for i in range(n)])  2.03 us
  transfers between devices with their start and end apart: 9, of which 3 were waited for; matrix products, arithmetic and copies ran while one was open for 0% of the time, Pallas kernels for 5%

profile of v12, /device:TPU:0, one launch (start us, length us, event | category | flops | bytes accessed | tf_op | source)
XLA Modules:
  0.0 37.4 jit_solution(10580117333936382348)
XLA Ops:
  0.6 4.1 %collective-permute-start = (bf16[64,256]{1,0:T(8,128)(2,1)}, bf16[64,256]{1,0:T(8,128)(2,1)S(1)}, u32[]{:S(2)}, u32[]{:S(2)}) collective-permute-start(bf16[64,256]{1,0:T(8,128)(2,1)} %t_hbm.1), channel_id=1, source_target_pairs={{0,8},{1,9},{2,10},{3,11},{4,12},{5,13},{6,14},{7,15},{8,0},{9,1},... | collective-permute-start | bytes 98312 | tf_op jit(solution)/shard_map/ppermute | solution.py:221
  4.7 0.7 %collective-permute-start.4 = (bf16[64,256]{1,0:T(8,128)(2,1)}, bf16[64,256]{1,0:T(8,128)(2,1)S(1)}, u32[]{:S(2)}, u32[]{:S(2)}) collective-permute-start(bf16[64,256]{1,0:T(8,128)(2,1)} %t_hbm.1), channel_id=1, source_target_pairs={{0,3},{1,2},{2,1},{3,0},{4,7},{5,6},{6,5},{7,4},{8,11},{9,10},{10,... | collective-permute-start | bytes 98312 | tf_op jit(solution)/shard_map/ppermute | solution.py:221
  5.4 2.1 %collective-permute-start.6 = (bf16[64,256]{1,0:T(8,128)(2,1)}, bf16[64,256]{1,0:T(8,128)(2,1)S(1)}, u32[]{:S(2)}, u32[]{:S(2)}) collective-permute-start(bf16[64,256]{1,0:T(8,128)(2,1)} %t_hbm.1), channel_id=1, source_target_pairs={{0,7},{1,6},{2,5},{3,4},{4,3},{5,2},{6,1},{7,0},{8,15},{9,14},{10,... | collective-permute-start | bytes 98312 | tf_op jit(solution)/shard_map/ppermute | solution.py:221
  7.5 0.4 %collective-permute-start.5 = (bf16[64,256]{1,0:T(8,128)(2,1)}, bf16[64,256]{1,0:T(8,128)(2,1)S(1)}, u32[]{:S(2)}, u32[]{:S(2)}) collective-permute-start(bf16[64,256]{1,0:T(8,128)(2,1)} %t_hbm.1), channel_id=1, source_target_pairs={{0,4},{1,5},{2,6},{3,7},{4,0},{5,1},{6,2},{7,3},{8,12},{9,13},{10,... | collective-permute-start | bytes 98312 | tf_op jit(solution)/shard_map/ppermute | solution.py:221
  7.9 1.0 %shard_map.59 = (bf16[512,256]{1,0:T(8,128)(2,1)S(1)}, bf16[64,256]{1,0:T(8,128)(2,1)S(1)}, f32[512,128]{1,0:T(8,128)S(1)}, f32[8,128]{1,0:T(8,128)S(1)}) custom-call(bf16[512,256]{1,0:T(8,128)(2,1)} %e_hbm.1, bf16[64,256]{1,0:T(8,128)(2,1)} %t_hbm.1, f32[512]{0:T(512)} %logw_hbm.1, f32[1024]{0:T(1024)} %dlw_hbm.1), custom_call_target="tpu_custom_call" | custom-call | bytes 524288 | tf_op jit(solution)/shard_map/pallas_call | solution.py:200
  9.0 0.0 collective-permute-done.refs_0_
  9.0 1.4 %collective-permute-start.3 = (bf16[64,256]{1,0:T(8,128)(2,1)S(1)}, bf16[64,256]{1,0:T(8,128)(2,1)S(1)}, u32[]{:S(2)}, u32[]{:S(2)}) collective-permute-start(bf16[64,256]{1,0:T(8,128)(2,1)S(1)} %collective-permute-done.refs_0_), channel_id=1, source_target_pairs={{0,7},{1,6},{2,5},{3,4},{4,3},{5,2},{6,1},{7,0},{8,15},{9,14},{10,... | collective-permute-start | bytes 98312 | tf_op jit(solution)/shard_map/ppermute | solution.py:221
  10.4 0.4 %collective-permute-start.2 = (bf16[64,256]{1,0:T(8,128)(2,1)S(1)}, bf16[64,256]{1,0:T(8,128)(2,1)S(1)}, u32[]{:S(2)}, u32[]{:S(2)}) collective-permute-start(bf16[64,256]{1,0:T(8,128)(2,1)S(1)} %collective-permute-done.refs_0_), channel_id=1, source_target_pairs={{0,4},{1,5},{2,6},{3,7},{4,0},{5,1},{6,2},{7,3},{8,12},{9,13},{10,... | collective-permute-start | bytes 98312 | tf_op jit(solution)/shard_map/ppermute | solution.py:221
  10.9 0.0 collective-permute-done.4.refs_1_
  10.9 1.1 %collective-permute-start.1 = (bf16[64,256]{1,0:T(8,128)(2,1)S(1)}, bf16[64,256]{1,0:T(8,128)(2,1)S(1)}, u32[]{:S(2)}, u32[]{:S(2)}) collective-permute-start(bf16[64,256]{1,0:T(8,128)(2,1)S(1)} %collective-permute-done.refs_0_), channel_id=1, source_target_pairs={{0,3},{1,2},{2,1},{3,0},{4,7},{5,6},{6,5},{7,4},{8,11},{9,10},{10,... | collective-permute-start | bytes 98312 | tf_op jit(solution)/shard_map/ppermute | solution.py:221
  12.0 0.0 collective-permute-done.6.refs_3_
  12.0 0.0 collective-permute-done.5.refs_2_
  12.0 0.4 %collective-permute-start.8 = (bf16[256,256]{1,0:T(8,128)(2,1)S(1)}, bf16[256,256]{1,0:T(8,128)(2,1)S(1)}, u32[]{:S(2)}, u32[]{:S(2)}) collective-permute-start(bf16[256,256]{1,0:T(8,128)(2,1)S(1)} %shard_map.60.refs_0_), channel_id=1, source_target_pairs={{0,1},{1,0},{2,3},{3,2},{4,5},{5,4},{6,7},{7,6},{8,9},{9,8},{10,11... | collective-permute-start | bytes 393224 | tf_op jit(solution)/shard_map/ppermute | solution.py:221
  12.4 0.4 %shard_map.61 = (f32[512,256]{1,0:T(8,128)S(1)}, f32[512,128]{1,0:T(8,128)S(1)}, f32[512,128]{1,0:T(8,128)S(1)}) custom-call(bf16[512,256]{1,0:T(8,128)(2,1)S(1)} %get-tuple-element.25.e_ref, bf16[256,256]{1,0:T(8,128)(2,1)S(1)} %shard_map.60.refs_0_), custom_call_target="tpu_custom_call" | custom-call | flops 67108864 | bytes 524288 | tf_op jit(solution)/shard_map/pallas_call | solution.py:200
  12.9 0.6 %collective-permute-done.3.refs_3_ = bf16[64,256]{1,0:T(8,128)(2,1)S(1)} collective-permute-done((bf16[64,256]{1,0:T(8,128)(2,1)S(1)}, bf16[64,256]{1,0:T(8,128)(2,1)S(1)}, u32[]{:S(2)}, u32[]{:S(2)}) %collective-permute-start.3) | collective-permute-done | bytes 32800 | tf_op jit(solution)/shard_map/ppermute | solution.py:221
  13.5 1.0 %collective-permute-done.2.refs_2_ = bf16[64,256]{1,0:T(8,128)(2,1)S(1)} collective-permute-done((bf16[64,256]{1,0:T(8,128)(2,1)S(1)}, bf16[64,256]{1,0:T(8,128)(2,1)S(1)}, u32[]{:S(2)}, u32[]{:S(2)}) %collective-permute-start.2) | collective-permute-done | bytes 32800 | tf_op jit(solution)/shard_map/ppermute | solution.py:221
  14.4 0.0 collective-permute-done.1.refs_1_
  14.5 0.8 %collective-permute-start.7 = (bf16[256,256]{1,0:T(8,128)(2,1)S(1)}, bf16[256,256]{1,0:T(8,128)(2,1)S(1)}, u32[]{:S(2)}, u32[]{:S(2)}) collective-permute-start(bf16[256,256]{1,0:T(8,128)(2,1)S(1)} %shard_map.62.refs_1_), channel_id=1, source_target_pairs={{0,1},{1,0},{2,3},{3,2},{4,5},{5,4},{6,7},{7,6},{8,9},{9,8},{10,11... | collective-permute-start | bytes 393224 | tf_op jit(solution)/shard_map/ppermute | solution.py:221
  15.3 0.0 collective-permute-done.8.refs_0_
  15.3 0.5 %shard_map.63 = (f32[512,512]{1,0:T(8,128)S(1)}, f32[512,128]{1,0:T(8,128)S(1)}, f32[512,128]{1,0:T(8,128)S(1)}) custom-call(bf16[512,256]{1,0:T(8,128)(2,1)S(1)} %get-tuple-element.25.e_ref, bf16[256,256]{1,0:T(8,128)(2,1)S(1)} %collective-permute-done.8.refs_0_, bf16[256,256]{1,0:T(8,128)(2,1)S(1)} %shard_map.62.refs_1_, ...), custom_call_target="tpu_custom_call" | custom-call | flops 134217728 | bytes 1048576 | tf_op jit(solution)/shard_map/pallas_call | solution.py:200
  15.8 0.4 %collective-permute-done.7.t_ref = bf16[256,256]{1,0:T(8,128)(2,1)S(1)} collective-permute-done((bf16[256,256]{1,0:T(8,128)(2,1)S(1)}, bf16[256,256]{1,0:T(8,128)(2,1)S(1)}, u32[]{:S(2)}, u32[]{:S(2)}) %collective-permute-start.7) | collective-permute-done | bytes 131104 | tf_op jit(solution)/shard_map/ppermute | solution.py:221
  16.3 1.0 %shard_map.64 = (f32[512,1024]{1,0:T(8,128)S(1)}, f32[512,128]{1,0:T(8,128)S(1)}, f32[8,128]{1,0:T(8,128)S(1)}, f32[16,8,128]{2,1,0:T(8,128)S(1)}) custom-call(bf16[512,256]{1,0:T(8,128)(2,1)S(1)} %get-tuple-element.25.e_ref, bf16[256,256]{1,0:T(8,128)(2,1)S(1)} %collective-permute-done.7.t_ref, f32[512,128]{1,0:T(8,128)S(1)} %get-tuple-element.34.max_ref, ...), custom_call_target="tpu_custom_call" | custom-call | tf_op jit(solution)/shard_map/pallas_call | solution.py:200
  17.2 10.1 %all_to_all.16.g_ref = f32[16,8,128]{2,1,0:T(8,128)S(1)} all-to-all(f32[16,8,128]{2,1,0:T(8,128)S(1)} %get-tuple-element.39), channel_id=1, replica_groups=mesh['group'=2,'src'=16] {'src'}, dimensions={0} | all-to-all | bytes 131072 | tf_op jit(solution)/shard_map/all_to_all | solution.py:292
  27.3 0.5 %shard_map.65 = (f32[512,128]{1,0:T(8,128)S(1)}, f32[16,64]{1,0:T(8,128)S(1)}) custom-call(f32[16,8,128]{2,1,0:T(8,128)S(1)} %all_to_all.16.g_ref, f32[512,128]{1,0:T(8,128)S(1)} %get-tuple-element.36.logw_ref, f32[8,128]{1,0:T(8,128)S(1)} %get-tuple-element.40.dlw_ref, f32[512,128]{1,0:T(8,128)S(1)} %get-tuple-element.41.pot_ref, ...), custom_call_target="tpu_custom_call" | custom-call | tf_op jit(solution)/shard_map/pallas_call | solution.py:200
  27.8 9.0 %all_to_all.17 = f32[16,1,64]{2,1,0:T(1,128)S(1)} all-to-all(f32[16,1,64]{2,1,0:T(1,128)S(1)} %bitcast.5), channel_id=1, replica_groups=mesh['group'=2,'src'=16] {'src'}, dimensions={0} | all-to-all | bytes 8192 | tf_op jit(solution)/shard_map/all_to_all | solution.py:299
  36.8 0.6 %shard_map.66 = (f32[512]{0:T(512)}, f32[64]{0:T(128)}) custom-call(f32[16,64]{1,0:T(8,128)S(1)} %bitcast.4, f32[512,128]{1,0:T(8,128)S(1)} %get-tuple-element.45.pot_ref), custom_call_target="tpu_custom_call" | custom-call | tf_op jit(solution)/shard_map/pallas_call | solution.py:200
  (2 shorter events, 0.0 us)
Async XLA Ops:
  0.6 8.4 %collective-permute-start = (bf16[64,256]{1,0:T(8,128)(2,1)}, bf16[64,256]{1,0:T(8,128)(2,1)S(1)}, u32[]{:S(2)}, u32[]{:S(2)}) collective-permute-start(bf16[64,256]{1,0:T(8,128)(2,1)} %t_hbm.1), channel_id=1, source_target_pairs={{0,8},{1,9},{2,10},{3,11},{4,12},{5,13},{6,14},{7,15},{8,0},{9,1},... | collective-permute-start | bytes 98312 | tf_op jit(solution)/shard_map/ppermute | solution.py:221
  4.7 6.2 %collective-permute-start.4 = (bf16[64,256]{1,0:T(8,128)(2,1)}, bf16[64,256]{1,0:T(8,128)(2,1)S(1)}, u32[]{:S(2)}, u32[]{:S(2)}) collective-permute-start(bf16[64,256]{1,0:T(8,128)(2,1)} %t_hbm.1), channel_id=1, source_target_pairs={{0,3},{1,2},{2,1},{3,0},{4,7},{5,6},{6,5},{7,4},{8,11},{9,10},{10,... | collective-permute-start | bytes 98312 | tf_op jit(solution)/shard_map/ppermute | solution.py:221
  5.4 6.6 %collective-permute-start.6 = (bf16[64,256]{1,0:T(8,128)(2,1)}, bf16[64,256]{1,0:T(8,128)(2,1)S(1)}, u32[]{:S(2)}, u32[]{:S(2)}) collective-permute-start(bf16[64,256]{1,0:T(8,128)(2,1)} %t_hbm.1), channel_id=1, source_target_pairs={{0,7},{1,6},{2,5},{3,4},{4,3},{5,2},{6,1},{7,0},{8,15},{9,14},{10,... | collective-permute-start | bytes 98312 | tf_op jit(solution)/shard_map/ppermute | solution.py:221
  7.5 4.5 %collective-permute-start.5 = (bf16[64,256]{1,0:T(8,128)(2,1)}, bf16[64,256]{1,0:T(8,128)(2,1)S(1)}, u32[]{:S(2)}, u32[]{:S(2)}) collective-permute-start(bf16[64,256]{1,0:T(8,128)(2,1)} %t_hbm.1), channel_id=1, source_target_pairs={{0,4},{1,5},{2,6},{3,7},{4,0},{5,1},{6,2},{7,3},{8,12},{9,13},{10,... | collective-permute-start | bytes 98312 | tf_op jit(solution)/shard_map/ppermute | solution.py:221
  9.0 4.5 %collective-permute-start.3 = (bf16[64,256]{1,0:T(8,128)(2,1)S(1)}, bf16[64,256]{1,0:T(8,128)(2,1)S(1)}, u32[]{:S(2)}, u32[]{:S(2)}) collective-permute-start(bf16[64,256]{1,0:T(8,128)(2,1)S(1)} %collective-permute-done.refs_0_), channel_id=1, source_target_pairs={{0,7},{1,6},{2,5},{3,4},{4,3},{5,2},{6,1},{7,0},{8,15},{9,14},{10,... | collective-permute-start | bytes 98312 | tf_op jit(solution)/shard_map/ppermute | solution.py:221
  10.4 4.0 %collective-permute-start.2 = (bf16[64,256]{1,0:T(8,128)(2,1)S(1)}, bf16[64,256]{1,0:T(8,128)(2,1)S(1)}, u32[]{:S(2)}, u32[]{:S(2)}) collective-permute-start(bf16[64,256]{1,0:T(8,128)(2,1)S(1)} %collective-permute-done.refs_0_), channel_id=1, source_target_pairs={{0,4},{1,5},{2,6},{3,7},{4,0},{5,1},{6,2},{7,3},{8,12},{9,13},{10,... | collective-permute-start | bytes 98312 | tf_op jit(solution)/shard_map/ppermute | solution.py:221
  10.9 3.5 %collective-permute-start.1 = (bf16[64,256]{1,0:T(8,128)(2,1)S(1)}, bf16[64,256]{1,0:T(8,128)(2,1)S(1)}, u32[]{:S(2)}, u32[]{:S(2)}) collective-permute-start(bf16[64,256]{1,0:T(8,128)(2,1)S(1)} %collective-permute-done.refs_0_), channel_id=1, source_target_pairs={{0,3},{1,2},{2,1},{3,0},{4,7},{5,6},{6,5},{7,4},{8,11},{9,10},{10,... | collective-permute-start | bytes 98312 | tf_op jit(solution)/shard_map/ppermute | solution.py:221
  12.0 3.3 %collective-permute-start.8 = (bf16[256,256]{1,0:T(8,128)(2,1)S(1)}, bf16[256,256]{1,0:T(8,128)(2,1)S(1)}, u32[]{:S(2)}, u32[]{:S(2)}) collective-permute-start(bf16[256,256]{1,0:T(8,128)(2,1)S(1)} %shard_map.60.refs_0_), channel_id=1, source_target_pairs={{0,1},{1,0},{2,3},{3,2},{4,5},{5,4},{6,7},{7,6},{8,9},{9,8},{10,11... | collective-permute-start | bytes 393224 | tf_op jit(solution)/shard_map/ppermute | solution.py:221
  14.5 1.8 %collective-permute-start.7 = (bf16[256,256]{1,0:T(8,128)(2,1)S(1)}, bf16[256,256]{1,0:T(8,128)(2,1)S(1)}, u32[]{:S(2)}, u32[]{:S(2)}) collective-permute-start(bf16[256,256]{1,0:T(8,128)(2,1)S(1)} %shard_map.62.refs_1_), channel_id=1, source_target_pairs={{0,1},{1,0},{2,3},{3,2},{4,5},{5,4},{6,7},{7,6},{8,9},{9,8},{10,11... | collective-permute-start | bytes 393224 | tf_op jit(solution)/shard_map/ppermute | solution.py:221
